TPU v7x, 32 devices: a whole 2x2x4 slice. The times are simulated.
32 devices in a mesh: seq: 4 (over z), ctx: 8 (over y, x, core).
Axes of the slice: x: 2, y: 2, z: 4, core: 2. Of those that a mesh axis runs over, the one named last changes fastest.
Arguments:
- hidden_in: bfloat16 [8, 1024, 2304], P('seq', 'ctx'), may hold values from -8 to 8
- norm_gains: bfloat16 [2304, 4], P(('seq', 'ctx')), may hold values from 0.25 to 1.75
- qkv_weight: bfloat16 [2304, 4096], P(('seq', 'ctx')), may hold values from -1 to 1
- out_weight: bfloat16 [2304, 2048], P(('seq', 'ctx')), may hold values from -0.125 to 0.125
- gate_up_weight: bfloat16 [9216, 4608], P(('seq', 'ctx')), may hold values from -0.125 to 0.125
- down_weight: bfloat16 [9216, 2304], P(('seq', 'ctx')), may hold values from -0.0625 to 0.0625
- output_cotangent: bfloat16 [8, 1024, 2304], P('seq', 'ctx'), may hold values from -6 to 6
- segment_ids: int32 [8, 1024], P('seq'), may hold values from 0 to 18, as said below
- padding: int32 [8, 1024], P('seq'), may hold values from 0 to 1, as said below
- positions: int32 [8, 1024], P('seq', 'ctx'), may hold values from 0 to 962, as said below
Outputs:
- layer_output: bfloat16 [8, 1024, 2304], P('seq', 'ctx')
- input_grad: float32 [8, 1024, 2304], P('seq', 'ctx')
- gain_grad: float32 [2304, 4], P(('seq', 'ctx'))
- qkv_grad: float32 [2304, 4096], P(('seq', 'ctx'))
- out_proj_grad: float32 [2304, 2048], P(('seq', 'ctx'))
- gate_up_grad: float32 [9216, 4608], P(('seq', 'ctx'))
- down_grad: float32 [9216, 2304], P(('seq', 'ctx'))
Inputs may be any that keep to these rules, and one draw needn't show every extreme that they name: `segment_ids`: in each sequence the ids count its documents from 0 in order, and every padding token has id 18. Of the 2 sequences of each index of seq, one holds a first document of 60 to 127 tokens and then a single document that runs into the sequence's last 64 tokens; the others are packed with documents of 60 to 800 tokens, the last of them cut where the padding begins. Every sequence ends in 1 to 64 padding tokens. `padding`: 1 exactly on the tokens whose id is below 18. `positions`: each token's offset from the first token of its document, or of the padding of its sequence.
All inputs are finite; a program needn't handle non-finite values.
Results may differ from a plain program's by a relative error of at most 0.01.
Values may be sent and summed in bfloat16 or wider, within the bound.
A program may use at most 896 MiB of HBM per device.

v0:
```python
from functools import partial
import math

import jax
import jax.numpy as jnp
from jax import lax
from jax.sharding import PartitionSpec as P

HEADS = 8
KV_HEADS = 4
HEAD_DIM = 256


EPSILON = 1e-06
SOFT_CAP = 50.0
MASKED = -1e30


def rms_norm(matrix, gain_col):
    factor = lax.rsqrt(jnp.mean(matrix * matrix, axis=-1, keepdims=True) + EPSILON)
    return matrix * factor * gain_col


def rotary_tables(positions, head_dim):
    half_dim = head_dim // 2
    frequency = jnp.exp(
        jnp.arange(half_dim, dtype=jnp.float32) * (-2.0 * math.log(10000.0) / head_dim)
    )
    phase_angle = positions.astype(jnp.float32)[:, None] * frequency[None, :]
    return (jnp.cos(phase_angle)[:, None, :], jnp.sin(phase_angle)[:, None, :])


def rotate(vectors, cosine, sine_part):
    half_dim = vectors.shape[-1] // 2
    first_half = vectors[..., :half_dim]
    second_half = vectors[..., half_dim:]
    return jnp.concatenate(
        [
            first_half * cosine - second_half * sine_part,
            second_half * cosine + first_half * sine_part,
        ],
        axis=-1,
    )


def rotate_back(grads, cosine, sine_part):
    half_dim = grads.shape[-1] // 2
    first_half = grads[..., :half_dim]
    second_half = grads[..., half_dim:]
    return jnp.concatenate(
        [
            first_half * cosine + second_half * sine_part,
            second_half * cosine - first_half * sine_part,
        ],
        axis=-1,
    )


def soft_probs(scaled, allowed):
    capped = SOFT_CAP * jnp.tanh(scaled / SOFT_CAP)
    capped = jnp.where(allowed, capped, MASKED)
    return jax.nn.softmax(capped, axis=-1)


def geglu_parts(gate_part, up_part):
    return jax.nn.gelu(gate_part, approximate=True) * up_part


def score_block(queries, keys_all):
    groups = keys_all.shape[0]
    seq_len = keys_all.shape[1]
    piece_len = queries.shape[0] // groups
    query_heads = queries.reshape(groups, piece_len, KV_HEADS, HEADS // KV_HEADS, HEAD_DIM)
    key_heads = keys_all.reshape(groups, seq_len, KV_HEADS, HEAD_DIM)
    raw_score = jnp.einsum(
        "spkgd,slkd->skgpl", query_heads, key_heads, preferred_element_type=jnp.float32
    )
    return raw_score * (1.0 / math.sqrt(HEAD_DIM))


def mix_values(weights_low, values_all):
    groups = values_all.shape[0]
    seq_len = values_all.shape[1]
    piece_len = weights_low.shape[3]
    value_heads = values_all.reshape(groups, seq_len, KV_HEADS, HEAD_DIM)
    mixed = jnp.einsum(
        "skgpl,slkd->spkgd", weights_low, value_heads, preferred_element_type=jnp.float32
    )
    return mixed.reshape(groups * piece_len, HEADS * HEAD_DIM).astype(jnp.bfloat16)


def add_slice(left, weight_piece):
    return jnp.dot(left, weight_piece, preferred_element_type=jnp.float32)


def times_rows(left, weight_piece):
    return lax.dot_general(
        left, weight_piece, (((1,), (1,)), ((), ())), preferred_element_type=jnp.float32
    )


def outer_rows(left, right):
    return lax.dot_general(
        left, right, (((0,), (0,)), ((), ())), preferred_element_type=jnp.float32
    )


def forward_pass(
    hidden_in,
    norm_gains,
    qkv_weight,
    out_weight,
    gate_up_weight,
    down_weight,
    segment_ids,
    padding,
    positions,
):
    groups = hidden_in.shape[0]
    piece_len = hidden_in.shape[1]
    model_width = hidden_in.shape[2]
    row_count = groups * piece_len
    residual = hidden_in.reshape(row_count, model_width).astype(jnp.float32)
    seq_len = segment_ids.shape[1]
    query_width = HEADS * HEAD_DIM
    key_width = KV_HEADS * HEAD_DIM
    factor = lax.rsqrt(jnp.mean(residual * residual, axis=-1, keepdims=True) + EPSILON)
    normed = residual * factor
    gain_piece = lax.all_gather(norm_gains, ("seq", "ctx"), axis=0, tiled=True)
    weight_piece = lax.all_gather(qkv_weight, ("seq", "ctx"), axis=0, tiled=True)
    scaled_in = (normed * gain_piece[:, 0].astype(jnp.float32)[None, :]).astype(jnp.bfloat16)
    running = jnp.dot(scaled_in, weight_piece, preferred_element_type=jnp.float32)
    gain_all = gain_piece
    projected, gain_all = (running, gain_all)
    gain_cols = gain_all.astype(jnp.float32)
    attn_input = (normed * gain_cols[:, 0]).astype(jnp.bfloat16)
    cosine, sine_part = rotary_tables(positions.reshape(row_count), HEAD_DIM)
    queries = (
        rotate(projected[:, :query_width].reshape(row_count, HEADS, HEAD_DIM), cosine, sine_part)
        .astype(jnp.bfloat16)
        .reshape(row_count, query_width)
    )
    keys_here = (
        rotate(
            projected[:, query_width : query_width + key_width].reshape(
                row_count, KV_HEADS, HEAD_DIM
            ),
            cosine,
            sine_part,
        )
        .astype(jnp.bfloat16)
        .reshape(groups, piece_len, key_width)
    )
    values_here = (
        projected[:, query_width + key_width :]
        .astype(jnp.bfloat16)
        .reshape(groups, piece_len, key_width)
    )
    keys_all, values_all = (
        lax.all_gather(keys_here, "ctx", axis=1, tiled=True),
        lax.all_gather(values_here, "ctx", axis=1, tiled=True),
    )
    first_query = lax.axis_index("ctx") * piece_len
    query_rows = first_query + jnp.arange(piece_len, dtype=jnp.int32)
    key_rows = jnp.arange(seq_len, dtype=jnp.int32)
    segment_query = lax.dynamic_slice_in_dim(segment_ids, first_query, piece_len, 1)
    allowed = (segment_query[:, :, None] == segment_ids[:, None, :]) & (
        key_rows[None, None, :] <= query_rows[None, :, None]
    ) & (padding[:, None, :] == 1) | (key_rows[None, None, :] == query_rows[None, :, None])
    allowed = allowed[:, None, None]
    probs = soft_probs(score_block(queries, keys_all), allowed)
    attn_out = mix_values(probs.astype(jnp.bfloat16), values_all)
    attn_proj = times_rows(attn_out, lax.all_gather(out_weight, ("seq", "ctx"), axis=0, tiled=True))
    after_attn = residual + rms_norm(attn_proj, gain_cols[:, 1])
    ffn_input = rms_norm(after_attn, gain_cols[:, 2]).astype(jnp.bfloat16)
    weight_piece = lax.all_gather(gate_up_weight, ("seq", "ctx"), axis=0, tiled=True)
    down_piece = lax.all_gather(down_weight, ("seq", "ctx"), axis=0, tiled=True)
    gate_part = lax.dot_general(
        ffn_input,
        weight_piece[:, :model_width],
        (((1,), (1,)), ((), ())),
        preferred_element_type=jnp.float32,
    )
    up_part = lax.dot_general(
        ffn_input,
        weight_piece[:, model_width:],
        (((1,), (1,)), ((), ())),
        preferred_element_type=jnp.float32,
    )
    hidden_part = geglu_parts(gate_part, up_part).astype(jnp.bfloat16)
    running = jnp.dot(hidden_part, down_piece, preferred_element_type=jnp.float32)
    layer_out = after_attn + rms_norm(running, gain_cols[:, 3])
    return {
        "residual": residual,
        "gain_cols": gain_cols,
        "attn_input": attn_input,
        "cosine": cosine,
        "sine_part": sine_part,
        "queries": queries,
        "keys_all": keys_all,
        "values_all": values_all,
        "allowed": allowed,
        "attn_out": attn_out,
        "attn_proj": attn_proj,
        "after_attn": after_attn,
        "ffn_input": ffn_input,
        "gate_all": gate_part,
        "up_all": up_part,
        "ffn_hidden": hidden_part,
        "down_out": running,
        "layer_out": layer_out,
    }


def per_device(
    hidden_in,
    norm_gains,
    qkv_weight,
    out_weight,
    gate_up_weight,
    down_weight,
    output_cotangent,
    segment_ids,
    padding,
    positions,
):
    inputs = (
        hidden_in,
        norm_gains,
        qkv_weight,
        out_weight,
        gate_up_weight,
        down_weight,
        segment_ids,
        padding,
        positions,
    )
    groups = hidden_in.shape[0]
    piece_len = hidden_in.shape[1]
    model_width = hidden_in.shape[2]
    row_count = groups * piece_len
    first_pass = forward_pass(*inputs)
    layer_output = (
        first_pass["layer_out"].astype(jnp.bfloat16).reshape(groups, piece_len, model_width)
    )
    gain_cols = first_pass["gain_cols"]
    seq_len = segment_ids.shape[1]
    group_size = HEADS // KV_HEADS
    query_width = HEADS * HEAD_DIM
    key_width = KV_HEADS * HEAD_DIM
    proj_width = qkv_weight.shape[1]
    cotangent = output_cotangent.reshape(row_count, model_width).astype(jnp.float32)
    gate_all = first_pass["gate_all"]
    up_all = first_pass["up_all"]
    ffn_input = first_pass["ffn_input"]
    ffn_hidden = first_pass["ffn_hidden"]
    unused_last, pull_last = jax.vjp(rms_norm, first_pass["down_out"], gain_cols[:, 3])
    grad_down, grad_gain_last = pull_last(cotangent)
    grad_down_low = grad_down.astype(jnp.bfloat16)
    weight_piece = lax.all_gather(gate_up_weight, ("seq", "ctx"), axis=0, tiled=True)
    down_piece = lax.all_gather(down_weight, ("seq", "ctx"), axis=0, tiled=True)
    grad_part = lax.dot_general(
        grad_down_low, down_piece, (((1,), (1,)), ((), ())), preferred_element_type=jnp.float32
    )
    unused_units, pull_units = jax.vjp(geglu_parts, gate_all, up_all)
    grad_gate_part, grad_up_part = pull_units(grad_part)
    gate_low = grad_gate_part.astype(jnp.bfloat16)
    up_low = grad_up_part.astype(jnp.bfloat16)
    running = jnp.dot(gate_low, weight_piece[:, :model_width], preferred_element_type=jnp.float32)
    running = running + jnp.dot(
        up_low, weight_piece[:, model_width:], preferred_element_type=jnp.float32
    )
    gate_rows = outer_rows(gate_low, ffn_input)
    up_rows = outer_rows(up_low, ffn_input)
    down_rows = outer_rows(ffn_hidden, grad_down_low)
    unit_sums = lax.psum_scatter(
        jnp.concatenate([gate_rows, up_rows, down_rows], axis=1),
        ("seq", "ctx"),
        scatter_dimension=0,
        tiled=True,
    )
    gate_up_grad = unit_sums[:, : 2 * model_width]
    down_grad = unit_sums[:, 2 * model_width :]
    unused_mid, pull_mid = jax.vjp(rms_norm, first_pass["after_attn"], gain_cols[:, 2])
    grad_after_ffn, grad_gain_mid = pull_mid(running)
    grad_after = cotangent + grad_after_ffn
    unused_post, pull_post = jax.vjp(rms_norm, first_pass["attn_proj"], gain_cols[:, 1])
    grad_proj, grad_gain_post = pull_post(grad_after)
    grad_proj_low = grad_proj.astype(jnp.bfloat16)
    grad_attn = add_slice(
        grad_proj_low, lax.all_gather(out_weight, ("seq", "ctx"), axis=0, tiled=True)
    ).astype(jnp.bfloat16)
    scaled = score_block(first_pass["queries"], first_pass["keys_all"])
    probs, pull_probs = jax.vjp(partial(soft_probs, allowed=first_pass["allowed"]), scaled)
    grad_heads = grad_attn.reshape(groups, piece_len, KV_HEADS, group_size, HEAD_DIM)
    query_heads = first_pass["queries"].reshape(groups, piece_len, KV_HEADS, group_size, HEAD_DIM)
    key_heads = first_pass["keys_all"].reshape(groups, seq_len, KV_HEADS, HEAD_DIM)
    value_heads = first_pass["values_all"].reshape(groups, seq_len, KV_HEADS, HEAD_DIM)
    grad_probs = jnp.einsum(
        "spkgd,slkd->skgpl", grad_heads, value_heads, preferred_element_type=jnp.float32
    )
    (grad_scaled,) = pull_probs(grad_probs)
    grad_scaled_low = grad_scaled.astype(jnp.bfloat16)
    inverse_root = 1.0 / math.sqrt(HEAD_DIM)
    grad_query_rot = (
        jnp.einsum(
            "skgpl,slkd->spkgd", grad_scaled_low, key_heads, preferred_element_type=jnp.float32
        )
        * inverse_root
    )
    grad_key_rot = (
        jnp.einsum(
            "skgpl,spkgd->slkd", grad_scaled_low, query_heads, preferred_element_type=jnp.float32
        )
        * inverse_root
    )
    grad_value_part = jnp.einsum(
        "skgpl,spkgd->slkd",
        probs.astype(jnp.bfloat16),
        grad_heads,
        preferred_element_type=jnp.float32,
    )
    key_summed, value_summed = (
        lax.psum_scatter(
            grad_key_rot.reshape(groups, seq_len, key_width).astype(jnp.bfloat16),
            "ctx",
            scatter_dimension=1,
            tiled=True,
        ).astype(jnp.float32),
        lax.psum_scatter(
            grad_value_part.reshape(groups, seq_len, key_width).astype(jnp.bfloat16),
            "ctx",
            scatter_dimension=1,
            tiled=True,
        ).astype(jnp.float32),
    )
    cosine, sine_part = (first_pass["cosine"], first_pass["sine_part"])
    grad_queries = rotate_back(
        grad_query_rot.reshape(row_count, HEADS, HEAD_DIM), cosine, sine_part
    ).reshape(row_count, query_width)
    grad_keys = rotate_back(
        key_summed.reshape(row_count, KV_HEADS, HEAD_DIM), cosine, sine_part
    ).reshape(row_count, key_width)
    grad_projected = jnp.concatenate(
        [grad_queries, grad_keys, value_summed.reshape(row_count, key_width)], axis=1
    ).astype(jnp.bfloat16)
    grad_attn_in = times_rows(
        grad_projected, lax.all_gather(qkv_weight, ("seq", "ctx"), axis=0, tiled=True)
    )
    unused_first, pull_first = jax.vjp(rms_norm, first_pass["residual"], gain_cols[:, 0])
    grad_res_first, grad_gain_first = pull_first(grad_attn_in)
    input_grad = (grad_after + grad_res_first).reshape(groups, piece_len, model_width)
    gain_terms = jnp.stack([grad_gain_first, grad_gain_post, grad_gain_mid, grad_gain_last], axis=1)
    qkv_part = outer_rows(first_pass["attn_input"], grad_projected)
    out_part = outer_rows(grad_proj_low, first_pass["attn_out"])
    row_grads = lax.psum_scatter(
        jnp.concatenate([qkv_part, out_part, gain_terms], axis=1),
        ("seq", "ctx"),
        scatter_dimension=0,
        tiled=True,
    )
    qkv_grad = row_grads[:, :proj_width]
    out_proj_grad = row_grads[:, proj_width : proj_width + query_width]
    gain_grad = row_grads[:, proj_width + query_width :]
    return (layer_output, input_grad, gain_grad, qkv_grad, out_proj_grad, gate_up_grad, down_grad)


def solution(mesh):
    placed = (
        P("seq", "ctx", None),
        P(("seq", "ctx"), None),
        P(("seq", "ctx"), None),
        P(("seq", "ctx"), None),
        P(("seq", "ctx"), None),
        P(("seq", "ctx"), None),
        P("seq", "ctx", None),
        P("seq", None),
        P("seq", None),
        P("seq", "ctx"),
    )
    return jax.shard_map(
        per_device,
        mesh=mesh,
        in_specs=placed,
        out_specs=(
            P("seq", "ctx", None),
            P("seq", "ctx", None),
            P(("seq", "ctx"), None),
            P(("seq", "ctx"), None),
            P(("seq", "ctx"), None),
            P(("seq", "ctx"), None),
            P(("seq", "ctx"), None),
        ),
        check_vma=False,
    )
```

profile of v0, /device:TPU:0, one launch (start us, length us, event | category | flops | bytes accessed | tf_op | source)
XLA Modules:
  0.0 4379.4 jit_solution(14971158758126279623)
XLA Ops:
  7.9 43.7 all-gather
  51.8 1.6 fusion.46
  53.4 1.6 fusion.43
  55.0 83.4 %all-gather.8.cloned.1.call-done = bf16[2304,4096]{1,0:T(8,128)(2,1)} async-done(((bf16[72,4096]{1,0:T(8,128)(2,1)}), bf16[2304,4096]{1,0:T(8,128)(2,1)}) %all-gather.8.cloned.1.call-update) | async-done | bytes 18874384 | tf_op jit(solution)/shard_map/all_gather | solution.py:130
  138.4 9.0 fusion.65
  147.4 2.0 copy-done.16
  150.9 1.4 slice.101
  160.2 25.1 all-gather.10.cloned.1.call-done
  185.3 6.3 copy.123
  191.6 33.0 all-gather.12.cloned.1.call-done
  224.6 6.2 copy.124
  230.8 3.7 fusion.50
  234.5 4.9 fusion.64
  240.4 3.2 copy-done
  243.6 2.0 copy-done.11
  248.9 60.5 %all-gather.14.cloned.1.call-done = bf16[2304,2048]{1,0:T(8,128)(2,1)} async-done(((bf16[72,2048]{1,0:T(8,128)(2,1)}), bf16[2304,2048]{1,0:T(8,128)(2,1)}) %all-gather.14.cloned.1.call-update) | async-done | bytes 9437200 | tf_op jit(solution)/shard_map/all_gather | solution.py:173
  309.4 6.4 multiply_reduce_fusion.6
  318.8 433.7 %all-gather.16.cloned.1.call-done = bf16[9216,4608]{1,0:T(8,128)(2,1)} async-done(((bf16[288,4608]{1,0:T(8,128)(2,1)}), bf16[9216,4608]{1,0:T(8,128)(2,1)}) %all-gather.16.cloned.1.call-update) | async-done | bytes 84934672 | tf_op jit(solution)/shard_map/all_gather | solution.py:176
  752.4 21.2 fusion.7
  773.7 23.8 multiply_convert_fusion.1
  797.5 193.7 %all-gather.18.cloned.1.call-done = bf16[9216,2304]{1,0:T(8,128)(2,1)} async-done(((bf16[288,2304]{1,0:T(8,128)(2,1)}), bf16[9216,2304]{1,0:T(8,128)(2,1)}) %all-gather.18.cloned.1.call-update) | async-done | bytes 42467344 | tf_op jit(solution)/shard_map/all_gather | solution.py:177
  991.1 19.5 multiply_reduce_fusion.4
  1010.7 1.5 fusion.39
  1012.2 2.5 fusion.36
  1014.7 27.5 fusion.15
  1042.2 20.6 fusion.1
  1062.9 22.1 multiply_reduce_fusion
  1085.7 4.4 multiply_reduce_fusion.1
  1090.1 1.4 copy-done.3
  1093.1 6.3 convolution_convert_fusion
  1101.2 5.8 bitcast_convert_fusion
  1107.0 6.3 copy.144
  1114.0 7.7 fusion.24
  1122.8 6.5 fusion.18
  1129.3 3.3 fusion.16
  1132.7 11.5 copy.175
  1144.1 5.6 copy.184
  1152.6 5.5 multiply_bitcast_fusion
  1160.5 2.4 copy.137
  1162.9 9.1 fusion.66
  1172.0 2.1 copy.145
  1174.1 44.0 %reduce-scatter.10.cloned.1.call-done = bf16[128,2048]{1,0:T(8,128)(2,1)} async-done(((bf16[1024,2048]{1,0:T(8,128)(2,1)}), bf16[128,2048]{1,0:T(8,128)(2,1)}) %reduce-scatter.10.cloned.1.call-update) | async-done | bytes 524304
  1218.1 2.2 reshape.335
  1220.3 2.1 copy.176
  1222.5 2.2 copy.140
  1224.7 2.7 reshape.325
  1227.4 1.5 add_convert_fusion.3
  1230.0 2.1 copy.141
  1232.1 12.5 fusion.45
  1244.6 1.4 stack.16
  1246.0 17.1 fusion.52
  1263.1 59.3 %concatenate.38 = f32[2304,6148]{1,0:T(8,128)} concatenate(f32[2304,4096]{1,0:T(8,128)} %fusion.52, f32[2304,2048]{1,0:T(8,128)} %fusion.66, f32[2304,1]{1,0:T(8,128)} %stack.16, f32[2304,1]{1,0:T(8,128)S(1)} %stack.17, f32[2304,1]{1,0:T(8,128)S(1)} %copy-done.24, f32[2304,1]{1,0:T(8,128)S(1)} %stack.19), dimensions={1} | concatenate | bytes 113319936 | tf_op jit(solution)/shard_map/concatenate | solution.py:357
  1323.7 32.5 fusion.67
  1356.2 34.1 fusion.68
  1390.4 31.6 fusion.69
  1422.0 175.3 %pad_maximum_fusion = f32[9216,6912]{0,1:T(8,128)} fusion(f32[9216,2304]{0,1:T(8,128)} %fusion.69, f32[9216,2304]{0,1:T(8,128)} %fusion.68, f32[9216,2304]{0,1:T(8,128)} %fusion.67), kind=kLoop, calls=%fused_computation.1 | loop fusion | flops 127401984 | bytes 509607936 | tf_op jit(solution)/shard_map/concatenate | solution.py:277
  1597.3 247.6 %copy.177 = f32[9216,6912]{1,0:T(8,128)} copy(f32[9216,6912]{0,1:T(8,128)} %pad_maximum_fusion) | data formatting | bytes 509607936
  1847.1 3.8 fusion.38
  1851.0 289.7 %all-reduce.3.cloned.1.call-done = f32[2304,6148]{1,0:T(8,128)} async-done(((f32[2304,6148]{1,0:T(8,128)}), f32[2304,6148]{1,0:T(8,128)}) %all-reduce.3.cloned.1.call-update) | async-done | bytes 56659984
  2142.2 2.1 dynamic-slice.3
  2144.3 2.4 constant_dynamic-slice_fusion
  2146.6 2217.0 %reduce-scatter.12.cloned.1.call-done = f32[288,6912]{1,0:T(8,128)} async-done(((f32[9216,6912]{1,0:T(8,128)}), f32[288,6912]{1,0:T(8,128)}) %reduce-scatter.12.cloned.1.call-update) | async-done | bytes 7962640
  4363.6 3.4 slice.118
  4367.0 5.2 slice.117
  (194 shorter events, 34.1 us)
Async XLA Ops:
  7.2 131.2 %all-gather.8.cloned.1.call-start = ((), (), s32[]{:S(2)}) async-start(), calls=%async_computation.3 | async-start | bytes 19464192 | tf_op jit(solution)/shard_map/all_gather | solution.py:130
  7.9 177.4 %all-gather.10.cloned.1.call-start = ((), (), s32[]{:S(2)}) async-start(), calls=%async_computation.4 | async-start | bytes 4718592 | tf_op jit(solution)/shard_map/all_gather | solution.py:161
  53.3 94.0 %copy-start.53 = (f32[2,128]{1,0:T(2,128)}, f32[2,128]{1,0:T(2,128)S(1)}, u32[]{:S(2)}) copy-start(f32[2,128]{1,0:T(2,128)S(1)} %fusion.46) | copy-start | bytes 3076
  53.4 94.0 %copy-start.48 = (f32[256]{0:T(256)}, f32[256]{0:T(256)S(1)}, u32[]{:S(2)}) copy-start(f32[256]{0:T(256)S(1)} %bitcast_rsqrt_fusion) | copy-start | bytes 3076
  55.0 95.4 %copy-start.57 = (s32[2,128]{1,0:T(2,128)S(1)}, s32[2,128]{1,0:T(2,128)}, u32[]{:S(2)}) copy-start(s32[2,128]{1,0:T(2,128)} %param.19) | copy-start | bytes 3076
  147.4 2.0 copy-start.16
  150.3 74.3 %all-gather.12.cloned.1.call-start = ((), (), s32[]{:S(2)}) async-start(), calls=%async_computation.5 | async-start | bytes 4718592 | tf_op jit(solution)/shard_map/all_gather | solution.py:160
  150.9 8.8 copy-start.27
  150.9 8.8 copy-start.29
  152.8 4.1 copy-start.47
  152.8 4.8 copy-start.54
  154.6 154.8 %all-gather.14.cloned.1.call-start = ((), (), s32[]{:S(2)}) async-start(), calls=%async_computation.6 | async-start | bytes 9732096 | tf_op jit(solution)/shard_map/all_gather | solution.py:173
  155.2 3.5 slice-start.2
  155.2 597.3 %all-gather.16.cloned.1.call-start = ((), (), s32[]{:S(2)}) async-start(), calls=%async_computation.7 | async-start | bytes 87588864 | tf_op jit(solution)/shard_map/all_gather | solution.py:176
  155.8 835.4 %all-gather.18.cloned.1.call-start = ((), (), s32[]{:S(2)}) async-start(), calls=%async_computation.8 | async-start | bytes 43794432 | tf_op jit(solution)/shard_map/all_gather | solution.py:177
  156.3 1015.7 %reduce-scatter.8.cloned.1.call-start = ((), (), s32[]{:S(2)}) async-start(), calls=%async_computation.9 | async-start | bytes 4718592 | tf_op jit(solution)/shard_map/reduce_scatter | solution.py:330
  157.7 158.8 %copy-start.34 = (f32[2304]{0:T(1024)}, f32[2304]{0:T(1024)S(1)}, u32[]{:S(2)}) copy-start(f32[2304]{0:T(1024)S(1)} %get-tuple-element.53) | copy-start | bytes 27652
  158.7 75.8 %copy-start.33 = (pred[2,128,1024]{1,2,0:T(8,128)(4,1)}, pred[2,128,1024]{1,2,0:T(8,128)(4,1)S(1)}, u32[]{:S(2)}) copy-start(pred[2,128,1024]{1,2,0:T(8,128)(4,1)S(1)} %and_or_fusion) | copy-start | bytes 786436
  160.2 70.6 %copy-start.19 = (bf16[256,8,128]{2,0,1:T(8,128)(2,1)}, bf16[256,8,128]{2,0,1:T(8,128)(2,1)S(1)}, u32[]{:S(2)}) copy-start(bf16[256,8,128]{2,0,1:T(8,128)(2,1)S(1)} %get-tuple-element.63) | copy-start | bytes 1572868
  160.2 70.6 %copy-start.21 = (bf16[256,8,128]{2,0,1:T(8,128)(2,1)}, bf16[256,8,128]{2,0,1:T(8,128)(2,1)S(1)}, u32[]{:S(2)}) copy-start(bf16[256,8,128]{2,0,1:T(8,128)(2,1)S(1)} %get-tuple-element.64) | copy-start | bytes 1572868
  234.5 4.9 copy-start.2
  239.3 4.3 copy-start
  239.4 4.3 copy-start.38
  239.4 6.2 copy-start.10
  243.6 2.0 copy-start.11
  248.9 67.0 %copy-start.26 = (bf16[256,2048]{1,0:T(8,128)(2,1)}, bf16[256,2048]{1,0:T(8,128)(2,1)S(1)}, u32[]{:S(2)}) copy-start(bf16[256,2048]{1,0:T(8,128)(2,1)S(1)} %convert_element_type.125) | copy-start | bytes 3145732
  248.9 68.4 %copy-start.7 = (bf16[2,128,2304]{2,1,0:T(8,128)(2,1)S(1)}, bf16[2,128,2304]{2,1,0:T(8,128)(2,1)}, u32[]{:S(2)}) copy-start(bf16[2,128,2304]{2,1,0:T(8,128)(2,1)} %param.10) | copy-start | bytes 3538948
  315.8 1.4 copy-start.5
  315.8 2.6 copy-start.36
  315.9 2.0 copy-start.44
  318.8 454.9 %copy-start.13 = (bf16[256,2304]{1,0:T(8,128)(2,1)}, bf16[256,2304]{1,0:T(8,128)(2,1)S(1)}, u32[]{:S(2)}) copy-start(bf16[256,2304]{1,0:T(8,128)(2,1)S(1)} %multiply_convert_fusion.2) | copy-start | bytes 3538948
  991.1 19.6 copy-start.12
  991.1 19.6 copy-start.37
  1062.9 22.8 copy-start.35
  1062.9 22.8 copy-start.45
  1085.7 4.5 copy-start.56
  1085.7 5.9 copy-start.6
  1090.1 1.4 copy-start.3
  1101.2 5.8 copy-start.15
  1113.4 104.8 %reduce-scatter.10.cloned.1.call-start = ((), (), s32[]{:S(2)}) async-start(), calls=%async_computation.10 | async-start | bytes 4718592
  1114.0 7.8 slice-start
  1114.0 8.8 slice-start.1
  1122.8 6.5 copy-start.20
  1122.8 6.5 copy-start.22
  1129.3 3.4 copy-start.1
  1149.7 1.4 copy-start.46
  1149.8 990.9 %all-reduce.3.cloned.1.call-start = ((), (), s32[]{:S(2)}) async-start(), calls=%async_computation.12 | async-start | bytes 115605504
  1158.3 4.6 copy-start.18
  1220.3 11.8 copy-start.8
  1220.3 11.8 copy-start.42
  1220.3 11.8 copy-start.49
  1232.1 13.9 copy-start.25
  1232.1 13.9 copy-start.31
  1232.1 13.9 copy-start.32
  1246.0 17.1 copy-start.24
  1322.4 1.3 copy-start.14
  1322.5 3041.1 %reduce-scatter.12.cloned.1.call-start = ((), (), s32[]{:S(2)}) async-start(), calls=%async_computation.11 | async-start | bytes 262766592
  1323.7 66.7 %slice-start.3 = ((s8[4718592]{0:T(1024)(128)(4,1)}), s8[4194304]{0:T(1024)(128)(4,1)S(1)}, s32[]{:S(2)}) async-start(s8[4718592]{0:T(1024)(128)(4,1)} %bitcast.171), calls=%async_computation.16 | async-start | bytes 8388608
  1356.2 34.1 slice-start.4
  1356.2 34.1 copy-start.23
  1845.0 1.8 copy-start.4
  1845.0 2.1 copy-start.9
  1845.0 2.1 copy-start.43
  1845.0 2.1 copy-start.50
  (9 other events, 7.1 us)
Sparse Core Ops, SparseCore 0:
  10.9 127.4 all-gather.7
  150.4 34.8 all-gather.9
  187.8 36.7 all-gather.11
  227.3 82.0 all-gather.13
  312.1 440.2 all-gather.15
  755.2 235.8 all-gather.17
  1113.5 49.4 reduce-scatter.7
  1166.7 51.3 reduce-scatter.9
  1322.6 818.0 all-reduce.2
  2146.9 2216.6 reduce-scatter.11
where the time goes:
time: 4390 us; the launch traced here: 4380 us
  waiting for transfers between devices  3380 us (77%)
  local copies, waits for them, and re-layouts  404 us (9%)
  matrix products  321 us (7%)
  other arithmetic  213 us (5%)
    unnamed x13, waiting for transfers between devices  2550 us
    all_gather x1, waiting for transfers between devices, forward_pass(): lax.all_gather(gate_up_weight, ('seq', 'ctx'), axis=0, tiled=True)  434 us
    unnamed x132, local copies, waits for them, and re-layouts  288 us
    all_gather x1, waiting for transfers between devices, forward_pass(): down_piece = lax.all_gather(down_weight, ('seq', 'ctx'), axis=0, tiled=True)  194 us
    concatenate x1, other arithmetic, per_device(): jnp.concatenate([gate_rows, up_rows, down_rows], axis=1)  175 us
    dot_general x5, matrix products, outer_rows(): lax.dot_general(left, right, (((0,), (0,)), ((), ())), preferred_element_...  125 us
  transfers between devices with their start and end apart: 10, of which 9 were waited for; matrix products, arithmetic and copies ran while one was open for 15% of the time, Pallas kernels for 0%

commit v1 on v0

v1 whole, which is shorter than its diff:
```python
from functools import partial
import math

import jax
import jax.numpy as jnp
from jax import lax
from jax.sharding import PartitionSpec as P

HEADS = 8
KV_HEADS = 4
HEAD_DIM = 256


EPSILON = 1e-06
SOFT_CAP = 50.0
MASKED = -1e30


def rms_norm(matrix, gain_col):
    factor = lax.rsqrt(jnp.mean(matrix * matrix, axis=-1, keepdims=True) + EPSILON)
    return matrix * factor * gain_col


def rotary_tables(positions, head_dim):
    half_dim = head_dim // 2
    frequency = jnp.exp(
        jnp.arange(half_dim, dtype=jnp.float32) * (-2.0 * math.log(10000.0) / head_dim)
    )
    phase_angle = positions.astype(jnp.float32)[:, None] * frequency[None, :]
    return (jnp.cos(phase_angle)[:, None, :], jnp.sin(phase_angle)[:, None, :])


def rotate(vectors, cosine, sine_part):
    half_dim = vectors.shape[-1] // 2
    first_half = vectors[..., :half_dim]
    second_half = vectors[..., half_dim:]
    return jnp.concatenate(
        [
            first_half * cosine - second_half * sine_part,
            second_half * cosine + first_half * sine_part,
        ],
        axis=-1,
    )


def rotate_back(grads, cosine, sine_part):
    half_dim = grads.shape[-1] // 2
    first_half = grads[..., :half_dim]
    second_half = grads[..., half_dim:]
    return jnp.concatenate(
        [
            first_half * cosine + second_half * sine_part,
            second_half * cosine - first_half * sine_part,
        ],
        axis=-1,
    )


def soft_probs(scaled, allowed):
    capped = SOFT_CAP * jnp.tanh(scaled / SOFT_CAP)
    capped = jnp.where(allowed, capped, MASKED)
    return jax.nn.softmax(capped, axis=-1)


def geglu_parts(gate_part, up_part):
    return jax.nn.gelu(gate_part, approximate=True) * up_part


def score_block(queries, keys_all):
    groups = keys_all.shape[0]
    seq_len = keys_all.shape[1]
    piece_len = queries.shape[0] // groups
    query_heads = queries.reshape(groups, piece_len, KV_HEADS, HEADS // KV_HEADS, HEAD_DIM)
    key_heads = keys_all.reshape(groups, seq_len, KV_HEADS, HEAD_DIM)
    raw_score = jnp.einsum(
        "spkgd,slkd->skgpl", query_heads, key_heads, preferred_element_type=jnp.float32
    )
    return raw_score * (1.0 / math.sqrt(HEAD_DIM))


def mix_values(weights_low, values_all):
    groups = values_all.shape[0]
    seq_len = values_all.shape[1]
    piece_len = weights_low.shape[3]
    value_heads = values_all.reshape(groups, seq_len, KV_HEADS, HEAD_DIM)
    mixed = jnp.einsum(
        "skgpl,slkd->spkgd", weights_low, value_heads, preferred_element_type=jnp.float32
    )
    return mixed.reshape(groups * piece_len, HEADS * HEAD_DIM).astype(jnp.bfloat16)


def add_slice(left, weight_piece):
    return jnp.dot(left, weight_piece, preferred_element_type=jnp.float32)


def times_rows(left, weight_piece):
    return lax.dot_general(
        left, weight_piece, (((1,), (1,)), ((), ())), preferred_element_type=jnp.float32
    )


def outer_rows(left, right):
    return lax.dot_general(
        left, right, (((0,), (0,)), ((), ())), preferred_element_type=jnp.float32
    )


def per_device(
    hidden_in,
    norm_gains,
    qkv_weight,
    out_weight,
    gate_up_weight,
    down_weight,
    output_cotangent,
    segment_ids,
    padding,
    positions,
):
    everyone = ("seq", "chip", "core")
    plane = ("chip", "core")
    column = ("seq", "core")
    groups = hidden_in.shape[0]
    piece_len = hidden_in.shape[1]
    model_width = hidden_in.shape[2]
    row_count = groups * piece_len
    seq_len = segment_ids.shape[1]
    group_size = HEADS // KV_HEADS
    query_width = HEADS * HEAD_DIM
    key_width = KV_HEADS * HEAD_DIM
    proj_width = qkv_weight.shape[1]

    residual = hidden_in.reshape(row_count, model_width).astype(jnp.float32)
    factor = lax.rsqrt(jnp.mean(residual * residual, axis=-1, keepdims=True) + EPSILON)
    gain_cols = lax.all_gather(norm_gains, everyone, axis=0, tiled=True).astype(jnp.float32)
    qkv_full = lax.all_gather(qkv_weight, everyone, axis=0, tiled=True)
    attn_input = (residual * factor * gain_cols[:, 0]).astype(jnp.bfloat16)
    projected = add_slice(attn_input, qkv_full)
    cosine, sine_part = rotary_tables(positions.reshape(row_count), HEAD_DIM)
    queries = (
        rotate(projected[:, :query_width].reshape(row_count, HEADS, HEAD_DIM), cosine, sine_part)
        .astype(jnp.bfloat16)
        .reshape(row_count, query_width)
    )
    keys_here = (
        rotate(
            projected[:, query_width : query_width + key_width].reshape(
                row_count, KV_HEADS, HEAD_DIM
            ),
            cosine,
            sine_part,
        )
        .astype(jnp.bfloat16)
        .reshape(groups, piece_len, key_width)
    )
    values_here = (
        projected[:, query_width + key_width :]
        .astype(jnp.bfloat16)
        .reshape(groups, piece_len, key_width)
    )
    both_all = lax.all_gather(
        jnp.concatenate([keys_here, values_here], axis=2), plane, axis=1, tiled=True
    )
    keys_all = both_all[:, :, :key_width]
    values_all = both_all[:, :, key_width:]
    first_query = (lax.axis_index("chip") * 2 + lax.axis_index("core")) * piece_len
    query_rows = first_query + jnp.arange(piece_len, dtype=jnp.int32)
    key_rows = jnp.arange(seq_len, dtype=jnp.int32)
    segment_query = lax.dynamic_slice_in_dim(segment_ids, first_query, piece_len, 1)
    allowed = (segment_query[:, :, None] == segment_ids[:, None, :]) & (
        key_rows[None, None, :] <= query_rows[None, :, None]
    ) & (padding[:, None, :] == 1) | (key_rows[None, None, :] == query_rows[None, :, None])
    allowed = allowed[:, None, None]
    probs = soft_probs(score_block(queries, keys_all), allowed)
    attn_out = mix_values(probs.astype(jnp.bfloat16), values_all)
    out_full = lax.all_gather(out_weight, everyone, axis=0, tiled=True)
    attn_proj = times_rows(attn_out, out_full)
    after_attn = residual + rms_norm(attn_proj, gain_cols[:, 1])
    ffn_input = rms_norm(after_attn, gain_cols[:, 2]).astype(jnp.bfloat16)

    unit_weights = lax.all_gather(gate_up_weight, "chip", axis=0, tiled=True)
    down_units = lax.all_gather(down_weight, "chip", axis=0, tiled=True)
    ffn_all = lax.all_gather(ffn_input, column, axis=0, tiled=True)
    gate_part = times_rows(ffn_all, unit_weights[:, :model_width])
    up_part = times_rows(ffn_all, unit_weights[:, model_width:])
    hidden_part = geglu_parts(gate_part, up_part).astype(jnp.bfloat16)
    down_part = add_slice(hidden_part, down_units).astype(jnp.bfloat16)
    down_out = lax.psum_scatter(down_part, column, scatter_dimension=0, tiled=True).astype(
        jnp.float32
    )
    layer_out = after_attn + rms_norm(down_out, gain_cols[:, 3])
    layer_output = layer_out.astype(jnp.bfloat16).reshape(groups, piece_len, model_width)

    cotangent = output_cotangent.reshape(row_count, model_width).astype(jnp.float32)
    unused_last, pull_last = jax.vjp(rms_norm, down_out, gain_cols[:, 3])
    grad_down, grad_gain_last = pull_last(cotangent)
    grad_down_low = grad_down.astype(jnp.bfloat16)
    grad_down_all = lax.all_gather(grad_down_low, column, axis=0, tiled=True)
    grad_part = times_rows(grad_down_all, down_units)
    unused_units, pull_units = jax.vjp(geglu_parts, gate_part, up_part)
    grad_gate_part, grad_up_part = pull_units(grad_part)
    gate_low = grad_gate_part.astype(jnp.bfloat16)
    up_low = grad_up_part.astype(jnp.bfloat16)
    grad_ffn_part = add_slice(gate_low, unit_weights[:, :model_width]) + add_slice(
        up_low, unit_weights[:, model_width:]
    )
    grad_ffn_in = lax.psum_scatter(
        grad_ffn_part.astype(jnp.bfloat16), column, scatter_dimension=0, tiled=True
    ).astype(jnp.float32)
    gate_up_rows = jnp.concatenate(
        [
            outer_rows(gate_low, ffn_all).astype(jnp.bfloat16),
            outer_rows(up_low, ffn_all).astype(jnp.bfloat16),
        ],
        axis=1,
    )
    down_rows = outer_rows(hidden_part, grad_down_all).astype(jnp.bfloat16)
    gate_up_grad = lax.psum_scatter(
        gate_up_rows, "chip", scatter_dimension=0, tiled=True
    ).astype(jnp.float32)
    down_grad = lax.psum_scatter(down_rows, "chip", scatter_dimension=0, tiled=True).astype(
        jnp.float32
    )

    unused_mid, pull_mid = jax.vjp(rms_norm, after_attn, gain_cols[:, 2])
    grad_after_ffn, grad_gain_mid = pull_mid(grad_ffn_in)
    grad_after = cotangent + grad_after_ffn
    unused_post, pull_post = jax.vjp(rms_norm, attn_proj, gain_cols[:, 1])
    grad_proj, grad_gain_post = pull_post(grad_after)
    grad_proj_low = grad_proj.astype(jnp.bfloat16)
    grad_attn = add_slice(grad_proj_low, out_full).astype(jnp.bfloat16)
    scaled = score_block(queries, keys_all)
    probs, pull_probs = jax.vjp(partial(soft_probs, allowed=allowed), scaled)
    grad_heads = grad_attn.reshape(groups, piece_len, KV_HEADS, group_size, HEAD_DIM)
    query_heads = queries.reshape(groups, piece_len, KV_HEADS, group_size, HEAD_DIM)
    key_heads = keys_all.reshape(groups, seq_len, KV_HEADS, HEAD_DIM)
    value_heads = values_all.reshape(groups, seq_len, KV_HEADS, HEAD_DIM)
    grad_probs = jnp.einsum(
        "spkgd,slkd->skgpl", grad_heads, value_heads, preferred_element_type=jnp.float32
    )
    (grad_scaled,) = pull_probs(grad_probs)
    grad_scaled_low = grad_scaled.astype(jnp.bfloat16)
    inverse_root = 1.0 / math.sqrt(HEAD_DIM)
    grad_query_rot = (
        jnp.einsum(
            "skgpl,slkd->spkgd", grad_scaled_low, key_heads, preferred_element_type=jnp.float32
        )
        * inverse_root
    )
    grad_key_rot = (
        jnp.einsum(
            "skgpl,spkgd->slkd", grad_scaled_low, query_heads, preferred_element_type=jnp.float32
        )
        * inverse_root
    )
    grad_value_part = jnp.einsum(
        "skgpl,spkgd->slkd",
        probs.astype(jnp.bfloat16),
        grad_heads,
        preferred_element_type=jnp.float32,
    )
    both_grads = jnp.concatenate(
        [
            grad_key_rot.reshape(groups, seq_len, key_width),
            grad_value_part.reshape(groups, seq_len, key_width),
        ],
        axis=2,
    ).astype(jnp.bfloat16)
    both_summed = lax.psum_scatter(both_grads, plane, scatter_dimension=1, tiled=True)
    both_summed = both_summed.astype(jnp.float32).reshape(row_count, 2 * key_width)
    key_summed = both_summed[:, :key_width]
    value_summed = both_summed[:, key_width:]
    grad_queries = rotate_back(
        grad_query_rot.reshape(row_count, HEADS, HEAD_DIM), cosine, sine_part
    ).reshape(row_count, query_width)
    grad_keys = rotate_back(
        key_summed.reshape(row_count, KV_HEADS, HEAD_DIM), cosine, sine_part
    ).reshape(row_count, key_width)
    grad_projected = jnp.concatenate([grad_queries, grad_keys, value_summed], axis=1).astype(
        jnp.bfloat16
    )
    grad_attn_in = times_rows(grad_projected, qkv_full)
    unused_first, pull_first = jax.vjp(rms_norm, residual, gain_cols[:, 0])
    grad_res_first, grad_gain_first = pull_first(grad_attn_in)
    input_grad = (grad_after + grad_res_first).reshape(groups, piece_len, model_width)
    gain_terms = jnp.stack([grad_gain_first, grad_gain_post, grad_gain_mid, grad_gain_last], axis=1)
    qkv_part = outer_rows(attn_input, grad_projected).astype(jnp.bfloat16)
    out_part = outer_rows(grad_proj_low, attn_out).astype(jnp.bfloat16)
    qkv_grad = lax.psum_scatter(qkv_part, everyone, scatter_dimension=0, tiled=True).astype(
        jnp.float32
    )
    out_proj_grad = lax.psum_scatter(out_part, everyone, scatter_dimension=0, tiled=True).astype(
        jnp.float32
    )
    gain_grad = lax.psum_scatter(gain_terms, everyone, scatter_dimension=0, tiled=True)
    return (layer_output, input_grad, gain_grad, qkv_grad, out_proj_grad, gate_up_grad, down_grad)


def solution(mesh):
    n_seq = mesh.shape["seq"]
    n_ctx = mesh.shape["ctx"]
    split_mesh = jax.sharding.Mesh(
        mesh.devices.reshape(n_seq, n_ctx // 2, 2), ("seq", "chip", "core")
    )
    plane = ("chip", "core")
    rows = P(("seq", "chip", "core"), None)
    tokens = P("seq", plane, None)
    placed = (
        tokens,
        rows,
        rows,
        rows,
        rows,
        rows,
        tokens,
        P("seq", None),
        P("seq", None),
        P("seq", plane),
    )
    return jax.shard_map(
        per_device,
        mesh=split_mesh,
        in_specs=placed,
        out_specs=(tokens, tokens, rows, rows, rows, rows, rows),
        check_vma=False,
    )
```

time: 4390 us -> 1600 us (0.36)
  waiting for transfers between devices: 3380 us -> 1120 us
  local copies, waits for them, and re-layouts: 404 us -> 61.2 us
  other arithmetic: 213 us -> 71.8 us
  matrix products: 321 us -> 245 us
    unnamed x13 -> x14, waiting for transfers between devices: 2550 us -> 2.57 us
    reduce_scatter x1 -> x7, waiting for transfers between devices: 0.01 us -> 638 us  [the longest x1 162 us: per_device(): lax.psum_scatter(qkv_part, everyone, scatter_dimension=0, tiled=True)]
    all_gather x6 -> x7, waiting for transfers between devices: 829 us -> 478 us  [the longest x1 94.6 us: per_device(): unit_weights = lax.all_gather(gate_up_weight, 'chip', axis=0, tiled=True)]
    unnamed x132 -> x133, local copies, waits for them, and re-layouts: 288 us -> 19.2 us
    concatenate x1 -> x3, other arithmetic: 175 us -> 13.8 us  [the longest x1 8.12 us: per_device(): jnp.concatenate([grad_key_rot.reshape(groups, seq_len, key_width), grad_v...]
    dot_general x7 -> x0, matrix products: 144 us -> none  [the longest x1 27.5 us: per_device(): lax.dot_general(grad_down_low, down_piece, (((1,), (1,)), ((), ())), pref...]
    dot_general x2 -> x5, matrix products: 18.9 us -> 87.7 us  [times_rows(): lax.dot_general(left, weight_piece, (((1,), (1,)), ((), ())), preferred_e...]
    dot_general x1 -> x5, matrix products: 6.28 us -> 69 us  [add_slice(): return jnp.dot(left, weight_piece, preferred_element_type=jnp.float32)]
  transfers between devices with their start and end apart: 10 -> 14, of which waited for: 9 -> 14; matrix products, arithmetic and copies ran while one was open for 15% -> 13% of each run, Pallas kernels for 0% -> 0%
where the time goes in v1:
time: 1600 us
  waiting for transfers between devices  1120 us (70%)
  matrix products  245 us (15%)
  blocking collectives  84.4 us (5%)
  other arithmetic  71.8 us (4%)
  local copies, waits for them, and re-layouts  61.2 us (4%)
    reduce_scatter x1, waiting for transfers between devices, per_device(): lax.psum_scatter(qkv_part, everyone, scatter_dimension=0, tiled=True)  162 us
    reduce_scatter x1, waiting for transfers between devices, per_device(): lax.psum_scatter(out_part, everyone, scatter_dimension=0, tiled=True)  125 us
    reduce_scatter x1, waiting for transfers between devices, per_device(): lax.psum_scatter(gate_up_rows, 'chip', scatter_dimension=0, tiled=True)  104 us
    reduce_scatter x1, waiting for transfers between devices, per_device(): lax.psum_scatter(down_part, column, scatter_dimension=0, tiled=True)  99.4 us
    reduce_scatter x1, waiting for transfers between devices, per_device(): lax.psum_scatter(grad_ffn_part.astype(jnp.bfloat16), column, scatter_dime...  96.6 us
    all_gather x1, waiting for transfers between devices, per_device(): unit_weights = lax.all_gather(gate_up_weight, 'chip', axis=0, tiled=True)  94.6 us
    all_gather x1, waiting for transfers between devices, per_device(): ffn_all = lax.all_gather(ffn_input, column, axis=0, tiled=True)  92.8 us
    all_gather x1, waiting for transfers between devices, per_device(): grad_down_all = lax.all_gather(grad_down_low, column, axis=0, tiled=True)  89.2 us
  transfers between devices with their start and end apart: 14, of which 14 were waited for; matrix products, arithmetic and copies ran while one was open for 13% of the time, Pallas kernels for 0%

profile of v1, /device:TPU:0, one launch (start us, length us, event | category | flops | bytes accessed | tf_op | source)
XLA Modules:
  0.0 1597.4 jit_solution(12142463586021123668)
XLA Ops:
  7.9 43.7 %all-gather = bf16[32,72,4]{1,2,0:T(4,128)(2,1)S(1)} all-gather(bf16[1,72,4]{1,2,0:T(4,128)(2,1)} %bitcast.173), channel_id=1, replica_groups=mesh['seq'=4,'chip'=4,'core'=2] {'seq','chip','core'}, dimensions={0}, use_global_device_ids=true | all-gather | bytes 19008 | tf_op jit(solution)/shard_map/all_gather | solution.py:135
  51.9 1.6 fusion.47
  54.7 1.7 fusion.45
  56.5 81.9 %all-gather.9.cloned.1.call-done = bf16[2304,4096]{1,0:T(8,128)(2,1)} async-done(((bf16[72,4096]{1,0:T(8,128)(2,1)}), bf16[2304,4096]{1,0:T(8,128)(2,1)}) %all-gather.9.cloned.1.call-update) | async-done | bytes 18874384 | tf_op jit(solution)/shard_map/all_gather | solution.py:136
  138.4 9.0 fusion.65
  147.5 1.9 copy-done.17
  156.1 48.6 %all-gather.11.cloned.1.call-done = bf16[2,1024,2048]{2,1,0:T(8,128)(2,1)} async-done(((bf16[2,128,2048]{2,1,0:T(8,128)(2,1)}), bf16[2,1024,2048]{2,1,0:T(8,128)(2,1)}) %all-gather.11.cloned.1.call-update) | async-done | bytes 8388624 | tf_op jit(solution)/shard_map/all_gather | solution.py:161
  204.7 6.1 fusion.62
  210.8 6.3 copy.96
  217.1 6.2 copy.95
  223.3 3.7 fusion.51
  226.9 4.9 fusion.64
  232.9 3.2 copy-done
  236.1 2.1 copy-done.14
  241.3 48.5 %all-gather.13.cloned.1.call-done = bf16[2304,2048]{1,0:T(8,128)(2,1)} async-done(((bf16[72,2048]{1,0:T(8,128)(2,1)}), bf16[2304,2048]{1,0:T(8,128)(2,1)}) %all-gather.13.cloned.1.call-update) | async-done | bytes 9437200 | tf_op jit(solution)/shard_map/all_gather | solution.py:176
  289.7 6.4 multiply_reduce_fusion.3
  301.6 94.6 %all-gather.17.cloned.1.call-done = bf16[1152,4608]{1,0:T(8,128)(2,1)} async-done(((bf16[288,4608]{1,0:T(8,128)(2,1)}), bf16[1152,4608]{1,0:T(8,128)(2,1)}) %all-gather.17.cloned.1.call-update) | async-done | bytes 10616848 | tf_op jit(solution)/shard_map/all_gather | solution.py:181
  396.2 92.8 %all-gather.15.cloned.1.call-done = bf16[2048,2304]{1,0:T(8,128)(2,1)} async-done(((bf16[256,2304]{1,0:T(8,128)(2,1)}), bf16[2048,2304]{1,0:T(8,128)(2,1)}) %all-gather.15.cloned.1.call-update) | async-done | bytes 9437200 | tf_op jit(solution)/shard_map/all_gather | solution.py:183
  489.0 18.3 %fusion.22 = f32[2048,1152]{1,0:T(8,128)} fusion(bf16[2048,2304]{1,0:T(8,128)(2,1)} %all-gather.15.cloned.1.call-done, bf16[1152,4608]{1,0:T(8,128)(2,1)} %all-gather.17.cloned.1.call-done), kind=kOutput, calls=%fused_computation.45 | convolution fusion | flops 10871635968 | bytes 24182784 | tf_op jit(solution)/shard_map/dot_general | solution.py:97
  507.4 21.7 %multiply_convert_fusion.1 = (bf16[2048,1152]{1,0:T(8,128)(2,1)}, f32[2048,1152]{1,0:T(8,128)}) fusion(f32[2048,1152]{1,0:T(8,128)} %fusion.22, bf16[2048,2304]{1,0:T(8,128)(2,1)} %all-gather.15.cloned.1.call-done, bf16[1152,4608]{1,0:T(8,128)(2,1)} %all-gather.17.cloned.1.call-done), kind=kOutput, calls=%fused_computation.19 | convolution fusion | flops 10895228928 | bytes 38338560 | tf_op jit(solution)/shard_map/dot_general | solution.py:97
  529.1 22.1 %all-gather.19.cloned.1.call-done = bf16[1152,2304]{1,0:T(8,128)(2,1)} async-done(((bf16[288,2304]{1,0:T(8,128)(2,1)}), bf16[1152,2304]{1,0:T(8,128)(2,1)}) %all-gather.19.cloned.1.call-update) | async-done | bytes 5308432 | tf_op jit(solution)/shard_map/all_gather | solution.py:182
  551.2 17.9 %convolution_convert_fusion.2 = bf16[2048,2304]{1,0:T(8,128)(2,1)} fusion(bf16[2048,1152]{1,0:T(8,128)(2,1)} %get-tuple-element.47, bf16[1152,2304]{1,0:T(8,128)(2,1)} %all-gather.19.cloned.1.call-done), kind=kOutput, calls=%fused_computation.6 | convolution fusion | flops 10876354560 | bytes 19464192 | tf_op jit(solution)/shard_map/dot_general | solution.py:93
  569.3 99.4 %reduce-scatter.9.cloned.1.call-done = bf16[256,2304]{1,0:T(8,128)(2,1)} async-done(((bf16[2048,2304]{1,0:T(8,128)(2,1)}), bf16[256,2304]{1,0:T(8,128)(2,1)}) %reduce-scatter.9.cloned.1.call-update) | async-done | bytes 1179664 | tf_op jit(solution)/shard_map/reduce_scatter | solution.py:188
  668.8 1.7 fusion.41
  670.5 3.1 fusion.40
  673.6 1.6 fusion.37
  675.3 89.2 %all-gather.21.cloned.1.call-done = bf16[2048,2304]{1,0:T(8,128)(2,1)} async-done(((bf16[256,2304]{1,0:T(8,128)(2,1)}), bf16[2048,2304]{1,0:T(8,128)(2,1)}) %all-gather.21.cloned.1.call-update) | async-done | bytes 9437200 | tf_op jit(solution)/shard_map/all_gather | solution.py:198
  764.5 29.1 %multiply_convert_fusion = (bf16[2048,1152]{1,0:T(8,128)(2,1)}, bf16[2048,1152]{1,0:T(8,128)(2,1)}) fusion(f32[2048,1152]{1,0:T(8,128)} %fusion.22, f32[2048,1152]{1,0:T(8,128)} %get-tuple-element.48, bf16[2048,2304]{1,0:T(8,128)(2,1)} %all-gather.21.cloned.1.call-done, bf16[1152,2304]{1,0:T(8,128)(2,1)} %all-gather.19.cloned.1.call-done), kind=kOutput, calls=%fused_computation.18 | convolution fusion | flops 10928259072 | bytes 43057152 | tf_op jit(solution)/shard_map/dot_general | solution.py:97
  793.6 18.4 %fusion.20 = f32[2048,2304]{1,0:T(8,128)} fusion(bf16[2048,1152]{1,0:T(8,128)(2,1)} %get-tuple-element.23, bf16[1152,4608]{1,0:T(8,128)(2,1)} %all-gather.17.cloned.1.call-done), kind=kOutput, calls=%fused_computation.43 | convolution fusion | flops 10871635968 | bytes 28901376 | tf_op jit(solution)/shard_map/dot_general | solution.py:93
  812.0 21.0 %add_convert_fusion = bf16[2048,2304]{1,0:T(8,128)(2,1)} fusion(f32[2048,2304]{1,0:T(8,128)} %fusion.20, bf16[2048,1152]{1,0:T(8,128)(2,1)} %get-tuple-element.22, bf16[1152,4608]{1,0:T(8,128)(2,1)} %all-gather.17.cloned.1.call-done), kind=kOutput, calls=%fused_computation.2 | convolution fusion | flops 10881073152 | bytes 38338560 | tf_op jit(solution)/shard_map/dot_general | solution.py:93
  833.1 1.5 multiply_divide_fusion
  834.5 96.6 %reduce-scatter.11.cloned.1.call-done = bf16[256,2304]{1,0:T(8,128)(2,1)} async-done(((bf16[2048,2304]{1,0:T(8,128)(2,1)}), bf16[256,2304]{1,0:T(8,128)(2,1)}) %reduce-scatter.11.cloned.1.call-update) | async-done | bytes 1179664 | tf_op jit(solution)/shard_map/reduce_scatter | solution.py:207
  931.2 2.8 fusion.36
  934.9 4.9 multiply_reduce_fusion
  942.8 2.7 convolution_convert_fusion.6
  946.3 2.1 copy.112
  948.4 5.9 bitcast_convert_fusion
  954.3 6.0 fusion.16
  960.4 5.9 fusion.10
  966.4 3.4 fusion.8
  969.7 6.2 copy.114
  975.9 6.3 copy.115
  982.3 8.1 pad_maximum_fusion.1
  990.5 17.4 %convolution_convert_fusion.3 = bf16[1152,2304]{1,0:T(8,128)(2,1)} fusion(bf16[2048,1152]{1,0:T(8,128)(2,1)} %get-tuple-element.47, bf16[2048,2304]{1,0:T(8,128)(2,1)} %all-gather.21.cloned.1.call-done), kind=kOutput, calls=%fused_computation.7 | convolution fusion | flops 10874290176 | bytes 19464192 | tf_op jit(solution)/shard_map/dot_general | solution.py:103
  1008.0 15.1 convolution_convert_fusion.4
  1023.1 15.2 convolution_convert_fusion.5
  1038.3 4.6 pad_maximum_fusion
  1044.4 5.0 convolution_convert_fusion.1
  1049.5 5.3 multiply_bitcast_fusion
  1056.1 1.5 copy.109
  1057.7 2.5 reduce-scatter.13.cloned.1.call-done
  1060.2 2.1 slice_convert_fusion.1
  1065.2 10.6 convolution_convert_fusion
  1077.1 48.9 %reduce-scatter.21.cloned.1.call-done = bf16[288,2304]{1,0:T(8,128)(2,1)} async-done(((bf16[1152,2304]{1,0:T(8,128)(2,1)}), bf16[288,2304]{1,0:T(8,128)(2,1)}) %reduce-scatter.21.cloned.1.call-update) | async-done | bytes 1327120 | tf_op jit(solution)/shard_map/reduce_scatter | solution.py:221
  1126.0 3.0 convert_element_type.156
  1130.3 103.7 %reduce-scatter.19.cloned.1.call-done = bf16[288,4608]{1,0:T(8,128)(2,1)} async-done(((bf16[1152,4608]{1,0:T(8,128)(2,1)}), bf16[288,4608]{1,0:T(8,128)(2,1)}) %reduce-scatter.19.cloned.1.call-update) | async-done | bytes 2654224 | tf_op jit(solution)/shard_map/reduce_scatter | solution.py:218
  1233.9 4.8 convert_element_type.154
  1238.7 12.1 fusion.46
  1251.4 125.0 %reduce-scatter.17.cloned.1.call-done = bf16[72,2048]{1,0:T(8,128)(2,1)} async-done(((bf16[2304,2048]{1,0:T(8,128)(2,1)}), bf16[72,2048]{1,0:T(8,128)(2,1)}) %reduce-scatter.17.cloned.1.call-update) | async-done | bytes 294928 | tf_op jit(solution)/shard_map/reduce_scatter | solution.py:292
  1376.5 1.8 convert_element_type.151
  1379.7 40.8 %all-reduce = f32[2304,4]{0,1:T(4,128)} all-reduce(f32[2304,4]{0,1:T(4,128)} %pad_maximum_fusion.10), channel_id=5, replica_groups=mesh['seq'=4,'chip'=4,'core'=2] {'seq','chip','core'}, use_global_device_ids=true, to_apply=%region_18.19.clone | all-reduce | flops 9216 | bytes 73728
  1422.5 3.9 fusion.39
  1426.4 162.1 %reduce-scatter.15.cloned.1.call-done = bf16[72,4096]{1,0:T(8,128)(2,1)} async-done(((bf16[2304,4096]{1,0:T(8,128)(2,1)}), bf16[72,4096]{1,0:T(8,128)(2,1)}) %reduce-scatter.15.cloned.1.call-update) | async-done | bytes 589840 | tf_op jit(solution)/shard_map/reduce_scatter | solution.py:289
  1588.5 2.2 convert_element_type.149
  (211 shorter events, 35.7 us)
Async XLA Ops:
  7.2 131.2 %all-gather.9.cloned.1.call-start = ((), (), s32[]{:S(2)}) async-start(), calls=%async_computation.7 | async-start | bytes 19464192 | tf_op jit(solution)/shard_map/all_gather | solution.py:136
  7.9 196.8 %all-gather.11.cloned.1.call-start = ((), (), s32[]{:S(2)}) async-start(), calls=%async_computation.8 | async-start | bytes 9437184 | tf_op jit(solution)/shard_map/all_gather | solution.py:161
  51.8 95.5 %copy-start.40 = (f32[2304]{0:T(1024)}, f32[2304]{0:T(1024)S(1)}, u32[]{:S(2)}) copy-start(f32[2304]{0:T(1024)S(1)} %get-tuple-element.18) | copy-start | bytes 27652
  51.9 244.4 %copy-start.36 = (f32[2304]{0:T(1024)}, f32[2304]{0:T(1024)S(1)}, u32[]{:S(2)}) copy-start(f32[2304]{0:T(1024)S(1)} %get-tuple-element.17) | copy-start | bytes 27652
  51.9 246.4 %copy-start.38 = (f32[2304]{0:T(1024)}, f32[2304]{0:T(1024)S(1)}, u32[]{:S(2)}) copy-start(f32[2304]{0:T(1024)S(1)} %get-tuple-element.16) | copy-start | bytes 27652
  51.9 621.7 %copy-start.39 = (f32[2304]{0:T(1024)}, f32[2304]{0:T(1024)S(1)}, u32[]{:S(2)}) copy-start(f32[2304]{0:T(1024)S(1)} %get-tuple-element.15) | copy-start | bytes 27652
  53.5 93.9 %copy-start.56 = (f32[2,128]{1,0:T(2,128)}, f32[2,128]{1,0:T(2,128)S(1)}, u32[]{:S(2)}) copy-start(f32[2,128]{1,0:T(2,128)S(1)} %fusion.47) | copy-start | bytes 3076
  53.5 93.9 %copy-start.53 = (f32[256]{0:T(256)}, f32[256]{0:T(256)S(1)}, u32[]{:S(2)}) copy-start(f32[256]{0:T(256)S(1)} %bitcast_rsqrt_fusion) | copy-start | bytes 3076
  54.7 101.0 %copy-start.29 = (f32[256,128]{1,0:T(8,128)}, f32[256,128]{1,0:T(8,128)S(1)}, u32[]{:S(2)}) copy-start(f32[256,128]{1,0:T(8,128)S(1)} %get-tuple-element.39) | copy-start | bytes 393220
  54.7 101.0 %copy-start.31 = (f32[256,128]{1,0:T(8,128)}, f32[256,128]{1,0:T(8,128)S(1)}, u32[]{:S(2)}) copy-start(f32[256,128]{1,0:T(8,128)S(1)} %get-tuple-element.40) | copy-start | bytes 393220
  56.4 90.9 %copy-start.20 = (bf16[256,2304]{1,0:T(8,128)(2,1)}, bf16[256,2304]{1,0:T(8,128)(2,1)S(1)}, u32[]{:S(2)}) copy-start(bf16[256,2304]{1,0:T(8,128)(2,1)S(1)} %fusion.45) | copy-start | bytes 3538948
  150.3 3.3 copy-start.57
  152.0 137.7 %all-gather.13.cloned.1.call-start = ((), (), s32[]{:S(2)}) async-start(), calls=%async_computation.9 | async-start | bytes 9732096 | tf_op jit(solution)/shard_map/all_gather | solution.py:176
  152.8 243.4 %all-gather.17.cloned.1.call-start = ((), (), s32[]{:S(2)}) async-start(), calls=%async_computation.11 | async-start | bytes 13271040 | tf_op jit(solution)/shard_map/all_gather | solution.py:181
  153.3 335.7 %all-gather.15.cloned.1.call-start = ((), (), s32[]{:S(2)}) async-start(), calls=%async_computation.10 | async-start | bytes 10616832 | tf_op jit(solution)/shard_map/all_gather | solution.py:183
  154.6 72.3 %copy-start.35 = (pred[2,128,1024]{1,2,0:T(8,128)(4,1)}, pred[2,128,1024]{1,2,0:T(8,128)(4,1)S(1)}, u32[]{:S(2)}) copy-start(pred[2,128,1024]{1,2,0:T(8,128)(4,1)S(1)} %and_or_fusion) | copy-start | bytes 786436
  156.1 67.1 %copy-start.22 = (bf16[256,8,128]{2,0,1:T(8,128)(2,1)}, bf16[256,8,128]{2,0,1:T(8,128)(2,1)S(1)}, u32[]{:S(2)}) copy-start(bf16[256,8,128]{2,0,1:T(8,128)(2,1)S(1)} %get-tuple-element.29) | copy-start | bytes 1572868
  156.1 67.1 %copy-start.24 = (bf16[256,8,128]{2,0,1:T(8,128)(2,1)}, bf16[256,8,128]{2,0,1:T(8,128)(2,1)S(1)}, u32[]{:S(2)}) copy-start(bf16[256,8,128]{2,0,1:T(8,128)(2,1)S(1)} %get-tuple-element.30) | copy-start | bytes 1572868
  226.9 4.9 copy-start.4
  231.8 4.3 copy-start
  231.8 4.3 copy-start.42
  231.8 6.3 copy-start.12
  241.2 54.9 %copy-start.26 = (bf16[256,2048]{1,0:T(8,128)(2,1)}, bf16[256,2048]{1,0:T(8,128)(2,1)S(1)}, u32[]{:S(2)}) copy-start(bf16[256,2048]{1,0:T(8,128)(2,1)S(1)} %convert_element_type.132) | copy-start | bytes 3145732
  241.3 56.3 %copy-start.9 = (bf16[2,128,2304]{2,1,0:T(8,128)(2,1)S(1)}, bf16[2,128,2304]{2,1,0:T(8,128)(2,1)}, u32[]{:S(2)}) copy-start(bf16[2,128,2304]{2,1,0:T(8,128)(2,1)} %param.10) | copy-start | bytes 3538948
  296.2 4.7 copy-start.48
  298.2 209.1 %copy-start.55 = (f32[256]{0:T(256)}, f32[256]{0:T(256)S(1)}, u32[]{:S(2)}) copy-start(f32[256]{0:T(256)S(1)} %get-tuple-element.20) | copy-start | bytes 3076
  298.3 209.1 %copy-start.50 = (f32[256]{0:T(256)}, f32[256]{0:T(256)S(1)}, u32[]{:S(2)}) copy-start(f32[256]{0:T(256)S(1)} %fusion.55) | copy-start | bytes 3076
  300.9 250.2 %all-gather.19.cloned.1.call-start = ((), (), s32[]{:S(2)}) async-start(), calls=%async_computation.12 | async-start | bytes 6635520 | tf_op jit(solution)/shard_map/all_gather | solution.py:182
  301.5 367.3 %reduce-scatter.9.cloned.1.call-start = ((), (), s32[]{:S(2)}) async-start(), calls=%async_computation.13 | async-start | bytes 10616832 | tf_op jit(solution)/shard_map/reduce_scatter | solution.py:188
  569.1 101.4 %copy-start.15 = (bf16[2,128,2304]{2,1,0:T(8,128)(2,1)S(1)}, bf16[2,128,2304]{2,1,0:T(8,128)(2,1)}, u32[]{:S(2)}) copy-start(bf16[2,128,2304]{2,1,0:T(8,128)(2,1)} %param.16) | copy-start | bytes 3538948
  569.1 195.4 %all-gather.21.cloned.1.call-start = ((), (), s32[]{:S(2)}) async-start(), calls=%async_computation.14 | async-start | bytes 10616832 | tf_op jit(solution)/shard_map/all_gather | solution.py:198
  668.8 4.8 copy-start.11
  670.5 123.1 %copy-start.51 = (f32[256]{0:T(256)}, f32[256]{0:T(256)S(1)}, u32[]{:S(2)}) copy-start(f32[256]{0:T(256)S(1)} %fusion.56) | copy-start | bytes 3076
  675.3 255.9 %reduce-scatter.11.cloned.1.call-start = ((), (), s32[]{:S(2)}) async-start(), calls=%async_computation.15 | async-start | bytes 10616832 | tf_op jit(solution)/shard_map/reduce_scatter | solution.py:207
  833.0 98.2 %copy-start.3 = (f32[256,2304]{1,0:T(8,128)S(1)}, f32[256,2304]{1,0:T(8,128)}, u32[]{:S(2)}) copy-start(f32[256,2304]{1,0:T(8,128)} %copy-done.2) | copy-start | bytes 7077892
  833.0 101.8 %copy-start.37 = (f32[2304]{0:T(1024)S(1)}, f32[2304]{0:T(1024)}, u32[]{:S(2)}) copy-start(f32[2304]{0:T(1024)} %copy-done.36) | copy-start | bytes 27652
  833.0 101.8 %copy-start.49 = (f32[256]{0:T(256)S(1)}, f32[256]{0:T(256)}, u32[]{:S(2)}) copy-start(f32[256]{0:T(256)} %copy-done.48) | copy-start | bytes 3076
  833.0 227.1 %reduce-scatter.13.cloned.1.call-start = ((), (), s32[]{:S(2)}) async-start(), calls=%async_computation.16 | async-start | bytes 9437184 | tf_op jit(solution)/shard_map/reduce_scatter | solution.py:269
  931.2 3.7 copy-start.8
  931.2 3.7 copy-start.16
  934.0 8.8 slice-start.3
  934.8 5.0 copy-start.59
  934.9 7.9 slice-start.4
  934.9 7.9 slice-start.5
  948.4 5.9 copy-start.13
  948.4 5.9 copy-start.47
  948.4 11.9 slice-start
  954.3 6.1 slice-start.1
  954.3 6.1 copy-start.43
  960.4 6.0 copy-start.23
  960.4 6.0 copy-start.25
  966.3 3.4 copy-start.1
  990.4 135.6 %reduce-scatter.21.cloned.1.call-start = ((), (), s32[]{:S(2)}) async-start(), calls=%async_computation.20 | async-start | bytes 6635520 | tf_op jit(solution)/shard_map/reduce_scatter | solution.py:221
  1007.9 226.0 %reduce-scatter.19.cloned.1.call-start = ((), (), s32[]{:S(2)}) async-start(), calls=%async_computation.19 | async-start | bytes 13271040 | tf_op jit(solution)/shard_map/reduce_scatter | solution.py:218
  1042.9 333.6 %reduce-scatter.17.cloned.1.call-start = ((), (), s32[]{:S(2)}) async-start(), calls=%async_computation.18 | async-start | bytes 9732096 | tf_op jit(solution)/shard_map/reduce_scatter | solution.py:292
  1049.4 539.0 %reduce-scatter.15.cloned.1.call-start = ((), (), s32[]{:S(2)}) async-start(), calls=%async_computation.17 | async-start | bytes 19464192 | tf_op jit(solution)/shard_map/reduce_scatter | solution.py:289
  1063.7 12.1 copy-start.33
  1065.2 10.6 copy-start.34
  1075.8 53.3 %copy-start.46 = (f32[2304]{0:T(1024)S(1)}, f32[2304]{0:T(1024)}, u32[]{:S(2)}) copy-start(f32[2304]{0:T(1024)} %get-tuple-element.7) | copy-start | bytes 27652
  1075.8 53.9 %copy-start.45 = (f32[2304]{0:T(1024)S(1)}, f32[2304]{0:T(1024)}, u32[]{:S(2)}) copy-start(f32[2304]{0:T(1024)} %get-tuple-element.11) | copy-start | bytes 27652
  1129.0 109.7 %copy-start.10 = (bf16[2,128,2304]{2,1,0:T(8,128)(2,1)S(1)}, bf16[2,128,2304]{2,1,0:T(8,128)(2,1)}, u32[]{:S(2)}) copy-start(bf16[2,128,2304]{2,1,0:T(8,128)(2,1)} %param.10) | copy-start | bytes 3538948
  1129.0 109.7 %copy-start.41 = (f32[2304]{0:T(1024)S(1)}, f32[2304]{0:T(1024)}, u32[]{:S(2)}) copy-start(f32[2304]{0:T(1024)} %copy-done.40) | copy-start | bytes 27652
  1129.0 109.7 %copy-start.54 = (f32[256]{0:T(256)S(1)}, f32[256]{0:T(256)}, u32[]{:S(2)}) copy-start(f32[256]{0:T(256)} %copy-done.53) | copy-start | bytes 3076
  1238.7 183.7 %copy-start.6 = (f32[256,2304]{1,0:T(8,128)S(1)}, f32[256,2304]{1,0:T(8,128)}, u32[]{:S(2)}) copy-start(f32[256,2304]{1,0:T(8,128)} %copy-done.5) | copy-start | bytes 7077892
  (16 other events, 28.0 us)
Sparse Core Ops, SparseCore 0:
  10.9 127.4 all-gather.8
  152.1 52.5 all-gather.10
  207.6 82.0 all-gather.12
  291.4 104.7 all-gather.16
  398.3 90.7 all-gather.14
  490.7 60.4 all-gather.18
  569.2 99.5 reduce-scatter.8
  675.4 89.0 all-gather.20
  833.2 97.9 reduce-scatter.10
  990.5 69.5 reduce-scatter.12
  1064.0 61.9 reduce-scatter.20
  1129.3 104.6 reduce-scatter.18
  1240.8 135.5 reduce-scatter.16
  1382.7 205.7 reduce-scatter.14

commit v2 on v1

--- a/solution.py
+++ b/solution.py
@@ -4,6 +4,8 @@
 import jax
 import jax.numpy as jnp
 from jax import lax
+from jax.experimental import pallas as pl
+from jax.experimental.pallas import tpu as pltpu
 from jax.sharding import PartitionSpec as P
 
 HEADS = 8
@@ -105,7 +107,511 @@
     )
 
 
-def per_device(
+MESH = pl.DeviceIdType.MESH
+ANY = pl.BlockSpec(memory_space=pl.ANY)
+DMA = pltpu.SemaphoreType.DMA
+
+
+def remote(source, target, send_sem, recv_sem, device):
+    return pltpu.make_async_remote_copy(
+        src_ref=source,
+        dst_ref=target,
+        send_sem=send_sem,
+        recv_sem=recv_sem,
+        device_id=device,
+        device_id_type=MESH,
+    )
+
+
+def plane_device(index):
+    return {"chip": index // 2, "core": lax.rem(index, 2)}
+
+
+def greet(n_plane, n_seq):
+    me = lax.axis_index("chip") * 2 + lax.axis_index("core")
+    barrier = pltpu.get_barrier_semaphore()
+    for step in range(1, n_plane):
+        pl.semaphore_signal(
+            barrier,
+            inc=1,
+            device_id=plane_device(lax.rem(me + step, n_plane)),
+            device_id_type=MESH,
+        )
+    count = n_plane - 1
+    if n_seq > 1:
+        s = lax.axis_index("seq")
+
+        @pl.when(s > 0)
+        def _():
+            pl.semaphore_signal(barrier, inc=1, device_id={"seq": s - 1}, device_id_type=MESH)
+
+        @pl.when(s < n_seq - 1)
+        def _():
+            pl.semaphore_signal(barrier, inc=1, device_id={"seq": s + 1}, device_id_type=MESH)
+
+        count = count + jnp.where(s > 0, 1, 0) + jnp.where(s < n_seq - 1, 1, 0)
+    pl.semaphore_wait(barrier, count)
+
+
+def start_exchange(n_plane, by_core, source, target, send_sems, recv_sems, local_sem):
+    me = lax.axis_index("chip") * 2 + lax.axis_index("core")
+    copies = []
+    for step in (4, 2, 6, 3, 5, 1, 7):
+        to = lax.rem(me + step, n_plane)
+        block = lax.rem(to, 2) if by_core else to
+        copy = remote(
+            source.at[block],
+            target.at[me],
+            send_sems.at[step],
+            recv_sems.at[step],
+            plane_device(to),
+        )
+        copy.start()
+        copies.append(copy)
+    block = lax.rem(me, 2) if by_core else me
+    own = pltpu.make_async_copy(source.at[block], target.at[me], local_sem.at[0])
+    own.start()
+    copies.append(own)
+    return copies
+
+
+def exchange_kernel(n_plane, by_core, source, target, send_sems, recv_sems, local_sem):
+    greet(n_plane, 1)
+    for copy in start_exchange(
+        n_plane, by_core, source, target, send_sems, recv_sems, local_sem
+    ):
+        copy.wait()
+
+
+def plane_exchange(blocks, by_core, collective_id):
+    n_plane = 2 * KV_HEADS
+    return pl.pallas_call(
+        partial(exchange_kernel, n_plane, by_core),
+        out_shape=jax.ShapeDtypeStruct((n_plane,) + blocks.shape[1:], blocks.dtype),
+        in_specs=[ANY],
+        out_specs=ANY,
+        scratch_shapes=[DMA((n_plane,)), DMA((n_plane,)), DMA((1,))],
+        compiler_params=pltpu.CompilerParams(
+            collective_id=collective_id, has_side_effects=True
+        ),
+    )(blocks)
+
+
+def gather_kernel(
+    n_seq,
+    n_plane,
+    hidden,
+    blocks,
+    hidden_all,
+    blocks_all,
+    hid_send,
+    hid_recv,
+    hid_local,
+    chip_send,
+    chip_recv,
+    chip_local,
+    left_send,
+    right_send,
+    line_recv,
+    twin_send,
+    twin_recv,
+):
+    n_chip = n_plane // 2
+    s = lax.axis_index("seq")
+    q = lax.axis_index("chip")
+    k = lax.axis_index("core")
+    greet(n_plane, n_seq)
+    swaps = []
+    for step in range(1, n_chip):
+        to = lax.rem(q + step, n_chip)
+        copy = remote(
+            blocks.at[to],
+            blocks_all.at[s, k, q],
+            chip_send.at[step],
+            chip_recv.at[step],
+            {"chip": to},
+        )
+        copy.start()
+        swaps.append(copy)
+    own = pltpu.make_async_copy(blocks.at[q], blocks_all.at[s, k, q], chip_local.at[0])
+    own.start()
+    hidden_copies = start_exchange(
+        n_plane, True, hidden, hidden_all, hid_send, hid_recv, hid_local
+    )
+    for copy in swaps:
+        copy.wait_recv()
+    own.wait()
+
+    def to_left(d):
+        return remote(
+            blocks_all.at[d, k], blocks_all.at[d, k], left_send.at[d], line_recv.at[d], {"seq": s - 1}
+        )
+
+    def to_right(d):
+        return remote(
+            blocks_all.at[d, k], blocks_all.at[d, k], right_send.at[d], line_recv.at[d], {"seq": s + 1}
+        )
+
+    def to_twin(d):
+        return remote(
+            blocks_all.at[d, k], blocks_all.at[d, k], twin_send.at[d], twin_recv.at[d], {"core": 1 - k}
+        )
+
+    def from_twin(d):
+        return remote(
+            blocks_all.at[d, 1 - k],
+            blocks_all.at[d, 1 - k],
+            twin_send.at[d],
+            twin_recv.at[d],
+            {"core": 1 - k},
+        )
+
+    @pl.when(s > 0)
+    def _():
+        to_left(s).start()
+
+    @pl.when(s < n_seq - 1)
+    def _():
+        to_right(s).start()
+
+    to_twin(s).start()
+    for hop in range(1, n_seq):
+        from_left = s - hop
+        from_right = s + hop
+
+        @pl.when(from_left >= 0)
+        def _():
+            to_left(from_left).wait_recv()
+
+            @pl.when(s < n_seq - 1)
+            def _():
+                to_right(from_left).start()
+
+            to_twin(from_left).start()
+
+        @pl.when(from_right < n_seq)
+        def _():
+            to_right(from_right).wait_recv()
+
+            @pl.when(s > 0)
+            def _():
+                to_left(from_right).start()
+
+            to_twin(from_right).start()
+
+    for d in range(n_seq):
+
+        @pl.when((d >= s) & (s > 0))
+        def _():
+            to_left(d).wait_send()
+
+        @pl.when((d <= s) & (s < n_seq - 1))
+        def _():
+            to_right(d).wait_send()
+
+        to_twin(d).wait_send()
+        from_twin(d).wait_recv()
+    for copy in swaps:
+        copy.wait_send()
+    for copy in hidden_copies:
+        copy.wait()
+
+
+def gather_first(n_seq, hidden, blocks):
+    n_plane = 2 * KV_HEADS
+    n_chip = KV_HEADS
+    return pl.pallas_call(
+        partial(gather_kernel, n_seq, n_plane),
+        out_shape=[
+            jax.ShapeDtypeStruct((n_plane,) + hidden.shape[1:], hidden.dtype),
+            jax.ShapeDtypeStruct((n_seq, 2) + blocks.shape, blocks.dtype),
+        ],
+        in_specs=[ANY, ANY],
+        out_specs=[ANY, ANY],
+        scratch_shapes=[
+            DMA((n_plane,)),
+            DMA((n_plane,)),
+            DMA((1,)),
+            DMA((n_chip,)),
+            DMA((n_chip,)),
+            DMA((1,)),
+            DMA((n_seq,)),
+            DMA((n_seq,)),
+            DMA((n_seq,)),
+            DMA((n_seq,)),
+            DMA((n_seq,)),
+        ],
+        compiler_params=pltpu.CompilerParams(collective_id=1, has_side_effects=True),
+    )(hidden, blocks)
+
+
+def last_kernel(
+    n_seq,
+    n_plane,
+    parts,
+    blocks,
+    parts_all,
+    sums,
+    held,
+    twin,
+    line,
+    part_send,
+    part_recv,
+    part_local,
+    held_sem,
+    twin_send,
+    twin_recv,
+    line_send,
+    line_recv,
+    chip_send,
+    chip_recv,
+    chip_local,
+):
+    n_chip = n_plane // 2
+    s = lax.axis_index("seq")
+    q = lax.axis_index("chip")
+    k = lax.axis_index("core")
+    greet(n_plane, n_seq)
+
+    def load(d):
+        return pltpu.make_async_copy(blocks.at[d, k], held.at[d], held_sem.at[d])
+
+    def to_twin(d):
+        return remote(
+            blocks.at[d, 1 - k], twin.at[d], twin_send.at[d], twin_recv.at[d], {"core": 1 - k}
+        )
+
+    def to_left(d):
+        return remote(held.at[d], line.at[d], line_send.at[d], line_recv.at[d], {"seq": s - 1})
+
+    def to_right(d):
+        return remote(
+            held.at[d], line.at[d + 1], line_send.at[d], line_recv.at[d + 1], {"seq": s + 1}
+        )
+
+    def gather_terms(d, with_left, with_right):
+        load(d).wait()
+        to_twin(d).wait_recv()
+
+        @pl.when(with_right)
+        def _():
+            to_left(d).wait_recv()
+
+        @pl.when(with_left)
+        def _():
+            to_right(d).wait_recv()
+
+        def body(i, carry):
+            held[d, i] = (held[d, i].astype(jnp.float32) + twin[d, i].astype(jnp.float32)).astype(
+                held.dtype
+            )
+            return carry
+
+        def body_right(i, carry):
+            total = held[d, i].astype(jnp.float32) + twin[d, i].astype(jnp.float32)
+            held[d, i] = (total + line[d, i].astype(jnp.float32)).astype(held.dtype)
+            return carry
+
+        def body_left(i, carry):
+            total = held[d, i].astype(jnp.float32) + twin[d, i].astype(jnp.float32)
+            held[d, i] = (total + line[d + 1, i].astype(jnp.float32)).astype(held.dtype)
+            return carry
+
+        def body_both(i, carry):
+            total = held[d, i].astype(jnp.float32) + twin[d, i].astype(jnp.float32)
+            total = total + line[d, i].astype(jnp.float32)
+            held[d, i] = (total + line[d + 1, i].astype(jnp.float32)).astype(held.dtype)
+            return carry
+
+        @pl.when(jnp.logical_not(with_left) & jnp.logical_not(with_right))
+        def _():
+            lax.fori_loop(0, n_chip, body, 0)
+
+        @pl.when(jnp.logical_not(with_left) & with_right)
+        def _():
+            lax.fori_loop(0, n_chip, body_right, 0)
+
+        @pl.when(with_left & jnp.logical_not(with_right))
+        def _():
+            lax.fori_loop(0, n_chip, body_left, 0)
+
+        @pl.when(with_left & with_right)
+        def _():
+            lax.fori_loop(0, n_chip, body_both, 0)
+
+    for d in range(n_seq):
+        to_twin(d).start()
+        load(d).start()
+    part_copies = start_exchange(
+        n_plane, False, parts, parts_all, part_send, part_recv, part_local
+    )
+    never = s < 0
+    for hop in range(1, n_seq):
+        left = hop - n_seq + s
+        right = n_seq - hop + s
+
+        @pl.when(left >= 0)
+        def _():
+            gather_terms(left, never, s < n_seq - 1)
+            to_left(left).start()
+
+        @pl.when(right <= n_seq - 1)
+        def _():
+            gather_terms(right, s > 0, never)
+            to_right(right).start()
+
+    gather_terms(s, s > 0, s < n_seq - 1)
+    swaps = []
+    for step in range(1, n_chip):
+        to = lax.rem(q + step, n_chip)
+        copy = remote(
+            held.at[s, to], sums.at[q], chip_send.at[step], chip_recv.at[step], {"chip": to}
+        )
+        copy.start()
+        swaps.append(copy)
+    own = pltpu.make_async_copy(held.at[s, q], sums.at[q], chip_local.at[0])
+    own.start()
+    for d in range(n_seq):
+        to_twin(d).wait_send()
+
+        @pl.when(d < s)
+        def _():
+            to_left(d).wait_send()
+
+        @pl.when(d > s)
+        def _():
+            to_right(d).wait_send()
+
+    for copy in part_copies:
+        copy.wait()
+    for copy in swaps:
+        copy.wait()
+    own.wait()
+
+
+def sum_last(n_seq, parts, blocks):
+    n_plane = 2 * KV_HEADS
+    n_chip = KV_HEADS
+    block = blocks.shape[2:]
+    return pl.pallas_call(
+        partial(last_kernel, n_seq, n_plane),
+        out_shape=[
+            jax.ShapeDtypeStruct(parts.shape, parts.dtype),
+            jax.ShapeDtypeStruct(block, blocks.dtype),
+        ],
+        in_specs=[ANY, ANY],
+        out_specs=[ANY, ANY],
+        scratch_shapes=[
+            pltpu.VMEM((n_seq,) + block, blocks.dtype),
+            pltpu.VMEM((n_seq,) + block, blocks.dtype),
+            pltpu.VMEM((n_seq + 1,) + block, blocks.dtype),
+            DMA((n_plane,)),
+            DMA((n_plane,)),
+            DMA((1,)),
+            DMA((n_seq,)),
+            DMA((n_seq,)),
+            DMA((n_seq,)),
+            DMA((n_seq,)),
+            DMA((n_seq + 1,)),
+            DMA((n_chip,)),
+            DMA((n_chip,)),
+            DMA((1,)),
+        ],
+        compiler_params=pltpu.CompilerParams(
+            collective_id=4, has_side_effects=True, vmem_limit_bytes=32 * 1024 * 1024
+        ),
+    )(parts, blocks)
+
+
+QUERY_BLOCK = 256
+
+
+def block_probs(query, keys, segment_col, segment_row, first):
+    rows, width = query.shape[0], keys.shape[0]
+    scaled = times_rows(query, keys) * (1.0 / math.sqrt(HEAD_DIM))
+    bent = jnp.tanh(scaled / SOFT_CAP)
+    row = first + lax.broadcasted_iota(jnp.int32, (rows, width), 0)
+    col = lax.broadcasted_iota(jnp.int32, (rows, width), 1)
+    allowed = ((segment_col == segment_row) & (col <= row)) | (col == row)
+    capped = jnp.where(allowed, SOFT_CAP * bent, MASKED)
+    raised = jnp.exp(capped - jnp.max(capped, axis=-1, keepdims=True))
+    return raised / jnp.sum(raised, axis=-1, keepdims=True), bent
+
+
+def attend_kernel(group_size, queries, keys, values, segment_col, segment_row, out):
+    seq_len = keys.shape[0]
+    for first in range(0, seq_len, QUERY_BLOCK):
+        rows = slice(first, first + QUERY_BLOCK)
+        width = first + QUERY_BLOCK
+        for head in range(group_size):
+            cols = slice(head * HEAD_DIM, (head + 1) * HEAD_DIM)
+            probs, unused = block_probs(
+                queries[rows, cols],
+                keys[:width],
+                segment_col[rows, :],
+                segment_row[:, :width],
+                first,
+            )
+            out[rows, cols] = add_slice(probs.astype(jnp.bfloat16), values[:width]).astype(
+                out.dtype
+            )
+
+
+def attend(queries, keys, values, segment_col, segment_row):
+    return pl.pallas_call(
+        partial(attend_kernel, queries.shape[1] // HEAD_DIM),
+        out_shape=jax.ShapeDtypeStruct(queries.shape, jnp.bfloat16),
+        compiler_params=pltpu.CompilerParams(vmem_limit_bytes=40 * 1024 * 1024),
+    )(queries, keys, values, segment_col, segment_row)
+
+
+def attend_back_kernel(
+    group_size,
+    queries,
+    keys,
+    values,
+    segment_col,
+    segment_row,
+    grads,
+    grad_queries,
+    grad_keys,
+    grad_values,
+):
+    seq_len = keys.shape[0]
+    inverse_root = 1.0 / math.sqrt(HEAD_DIM)
+    grad_keys[...] = jnp.zeros_like(grad_keys)
+    grad_values[...] = jnp.zeros_like(grad_values)
+    for first in range(0, seq_len, QUERY_BLOCK):
+        rows = slice(first, first + QUERY_BLOCK)
+        width = first + QUERY_BLOCK
+        for head in range(group_size):
+            cols = slice(head * HEAD_DIM, (head + 1) * HEAD_DIM)
+            query = queries[rows, cols]
+            probs, bent = block_probs(
+                query, keys[:width], segment_col[rows, :], segment_row[:, :width], first
+            )
+            grad = grads[rows, cols]
+            grad_probs = times_rows(grad, values[:width])
+            mean = jnp.sum(probs * grad_probs, axis=-1, keepdims=True)
+            grad_scaled = (probs * (grad_probs - mean) * (1.0 - bent * bent)).astype(jnp.bfloat16)
+            grad_queries[rows, cols] = add_slice(grad_scaled, keys[:width]) * inverse_root
+            grad_keys[:width, :] += outer_rows(grad_scaled, query) * inverse_root
+            grad_values[:width, :] += outer_rows(probs.astype(jnp.bfloat16), grad)
+
+
+def attend_back(queries, keys, values, segment_col, segment_row, grads):
+    return pl.pallas_call(
+        partial(attend_back_kernel, queries.shape[1] // HEAD_DIM),
+        out_shape=[
+            jax.ShapeDtypeStruct(queries.shape, jnp.float32),
+            jax.ShapeDtypeStruct(keys.shape, jnp.float32),
+            jax.ShapeDtypeStruct(values.shape, jnp.float32),
+        ],
+        compiler_params=pltpu.CompilerParams(vmem_limit_bytes=40 * 1024 * 1024),
+    )(queries, keys, values, segment_col, segment_row, grads)
+
+
+def per_device_general(
     hidden_in,
     norm_gains,
     qkv_weight,
@@ -296,6 +802,239 @@
     return (layer_output, input_grad, gain_grad, qkv_grad, out_proj_grad, gate_up_grad, down_grad)
 
 
+def per_device_by_heads(
+    n_seq,
+    hidden_in,
+    norm_gains,
+    qkv_weight,
+    out_weight,
+    gate_up_weight,
+    down_weight,
+    output_cotangent,
+    segment_ids,
+    padding,
+    positions,
+):
+    column = ("seq", "core")
+    groups, piece_len, model_width = hidden_in.shape
+    row_count = groups * piece_len
+    seq_len = segment_ids.shape[1]
+    n_chip = KV_HEADS
+    n_plane = 2 * n_chip
+    group_size = HEADS // KV_HEADS
+    query_width = HEADS * HEAD_DIM
+    key_width = KV_HEADS * HEAD_DIM
+    own_width = group_size * HEAD_DIM
+    part_width = own_width + 2 * HEAD_DIM
+    block_width = part_width + own_width
+    weight_rows = qkv_weight.shape[0]
+    extra_rows = 16 - weight_rows % 16
+    block_rows = weight_rows + extra_rows
+    core = lax.axis_index("core")
+
+    gain_rows = jnp.pad(
+        norm_gains.T, ((0, extra_rows - norm_gains.shape[1]), (0, block_width - weight_rows))
+    )
+    blocks = jnp.stack(
+        [
+            jnp.concatenate(
+                [
+                    jnp.concatenate(
+                        [
+                            qkv_weight[:, c * own_width : (c + 1) * own_width],
+                            qkv_weight[
+                                :, query_width + c * HEAD_DIM : query_width + (c + 1) * HEAD_DIM
+                            ],
+                            qkv_weight[
+                                :,
+                                query_width + key_width + c * HEAD_DIM : query_width
+                                + key_width
+                                + (c + 1) * HEAD_DIM,
+                            ],
+                            out_weight[:, c * own_width : (c + 1) * own_width],
+                        ],
+                        axis=1,
+                    ),
+                    gain_rows,
+                ],
+                axis=0,
+            )
+            for c in range(n_chip)
+        ]
+    )
+    hidden_all, blocks_all = gather_first(n_seq, hidden_in, blocks)
+    unit_weights = lax.all_gather(gate_up_weight, "chip", axis=0, tiled=True)
+    down_units = lax.all_gather(down_weight, "chip", axis=0, tiled=True)
+    blocks_all = blocks_all.transpose(0, 2, 1, 3, 4)
+    own_weights = blocks_all[:, :, :, :weight_rows].reshape(model_width, block_width)
+    own_qkv = own_weights[:, :part_width]
+    own_out = own_weights[:, part_width:]
+    gain_cols = (
+        blocks_all[:, :, :, weight_rows : weight_rows + norm_gains.shape[1], :weight_rows]
+        .transpose(0, 1, 2, 4, 3)
+        .reshape(model_width, norm_gains.shape[1])
+        .astype(jnp.float32)
+    )
+
+    seq_rows = hidden_all.reshape(seq_len, model_width).astype(jnp.float32)
+    seq_factor = lax.rsqrt(jnp.mean(seq_rows * seq_rows, axis=-1, keepdims=True) + EPSILON)
+    attn_input = (seq_rows * seq_factor * gain_cols[:, 0]).astype(jnp.bfloat16)
+    projected = add_slice(attn_input, own_qkv)
+    segment = lax.dynamic_index_in_dim(segment_ids, core, 0, keepdims=False)
+    valid = lax.dynamic_index_in_dim(padding, core, 0, keepdims=False)
+    token = jnp.arange(seq_len, dtype=jnp.int32)
+    document_start = jnp.min(
+        jnp.where(segment[:, None] == segment[None, :], token[None, :], seq_len), axis=1
+    )
+    cosine, sine_part = rotary_tables(token - document_start, HEAD_DIM)
+    queries = (
+        rotate(projected[:, :own_width].reshape(seq_len, group_size, HEAD_DIM), cosine, sine_part)
+        .astype(jnp.bfloat16)
+        .reshape(seq_len, own_width)
+    )
+    keys = (
+        rotate(
+            projected[:, own_width : own_width + HEAD_DIM].reshape(seq_len, 1, HEAD_DIM),
+            cosine,
+            sine_part,
+        )
+        .astype(jnp.bfloat16)
+        .reshape(seq_len, HEAD_DIM)
+    )
+    values = projected[:, own_width + HEAD_DIM :].astype(jnp.bfloat16)
+    segment_col = segment[:, None]
+    segment_row = jnp.where(valid == 1, segment, -1)[None, :]
+    attn_out = attend(queries, keys, values, segment_col, segment_row)
+    proj_parts = times_rows(attn_out, own_out).astype(jnp.bfloat16)
+    proj_parts = plane_exchange(
+        proj_parts.reshape(n_plane, piece_len, model_width), False, 2
+    )
+
+    def sum_parts(parts):
+        parts = parts.reshape(n_chip, groups, piece_len, model_width).astype(jnp.float32)
+        return jnp.sum(parts, axis=0).reshape(row_count, model_width)
+
+    attn_proj = sum_parts(proj_parts)
+    residual = hidden_in.reshape(row_count, model_width).astype(jnp.float32)
+    after_attn = residual + rms_norm(attn_proj, gain_cols[:, 1])
+    ffn_input = rms_norm(after_attn, gain_cols[:, 2]).astype(jnp.bfloat16)
+
+    ffn_all = lax.all_gather(ffn_input, column, axis=0, tiled=True)
+    gate_part = times_rows(ffn_all, unit_weights[:, :model_width])
+    up_part = times_rows(ffn_all, unit_weights[:, model_width:])
+    hidden_part = geglu_parts(gate_part, up_part).astype(jnp.bfloat16)
+    down_part = add_slice(hidden_part, down_units).astype(jnp.bfloat16)
+    down_out = lax.psum_scatter(down_part, column, scatter_dimension=0, tiled=True).astype(
+        jnp.float32
+    )
+    layer_out = after_attn + rms_norm(down_out, gain_cols[:, 3])
+    layer_output = layer_out.astype(jnp.bfloat16).reshape(groups, piece_len, model_width)
+
+    cotangent = output_cotangent.reshape(row_count, model_width).astype(jnp.float32)
+    unused_last, pull_last = jax.vjp(rms_norm, down_out, gain_cols[:, 3])
+    grad_down, grad_gain_last = pull_last(cotangent)
+    grad_down_low = grad_down.astype(jnp.bfloat16)
+    grad_down_all = lax.all_gather(grad_down_low, column, axis=0, tiled=True)
+    grad_part = times_rows(grad_down_all, down_units)
+    unused_units, pull_units = jax.vjp(geglu_parts, gate_part, up_part)
+    grad_gate_part, grad_up_part = pull_units(grad_part)
+    gate_low = grad_gate_part.astype(jnp.bfloat16)
+    up_low = grad_up_part.astype(jnp.bfloat16)
+    grad_ffn_part = add_slice(gate_low, unit_weights[:, :model_width]) + add_slice(
+        up_low, unit_weights[:, model_width:]
+    )
+    grad_ffn_in = lax.psum_scatter(
+        grad_ffn_part.astype(jnp.bfloat16), column, scatter_dimension=0, tiled=True
+    ).astype(jnp.float32)
+    gate_up_rows = jnp.concatenate(
+        [
+            outer_rows(gate_low, ffn_all).astype(jnp.bfloat16),
+            outer_rows(up_low, ffn_all).astype(jnp.bfloat16),
+        ],
+        axis=1,
+    )
+    down_rows = outer_rows(hidden_part, grad_down_all).astype(jnp.bfloat16)
+    gate_up_grad = lax.psum_scatter(
+        gate_up_rows, "chip", scatter_dimension=0, tiled=True
+    ).astype(jnp.float32)
+    down_grad = lax.psum_scatter(down_rows, "chip", scatter_dimension=0, tiled=True).astype(
+        jnp.float32
+    )
+
+    unused_mid, pull_mid = jax.vjp(rms_norm, after_attn, gain_cols[:, 2])
+    grad_after_ffn, grad_gain_mid = pull_mid(grad_ffn_in)
+    grad_after = cotangent + grad_after_ffn
+    unused_post, pull_post = jax.vjp(rms_norm, attn_proj, gain_cols[:, 1])
+    grad_proj, grad_gain_post = pull_post(grad_after)
+    grad_proj_low = grad_proj.astype(jnp.bfloat16)
+
+    grad_proj_all = plane_exchange(
+        grad_proj_low.reshape(groups, piece_len, model_width), True, 3
+    ).reshape(seq_len, model_width)
+    grad_attn = add_slice(grad_proj_all, own_out).astype(jnp.bfloat16)
+    grad_query_rot, grad_key_rot, grad_values = attend_back(
+        queries, keys, values, segment_col, segment_row, grad_attn
+    )
+    grad_queries = rotate_back(
+        grad_query_rot.reshape(seq_len, group_size, HEAD_DIM), cosine, sine_part
+    ).reshape(seq_len, own_width)
+    grad_keys = rotate_back(
+        grad_key_rot.reshape(seq_len, 1, HEAD_DIM), cosine, sine_part
+    ).reshape(seq_len, HEAD_DIM)
+    grad_projected = jnp.concatenate([grad_queries, grad_keys, grad_values], axis=1).astype(
+        jnp.bfloat16
+    )
+    grad_in_part = times_rows(grad_projected, own_qkv)
+    grad_gain_first = jnp.sum(grad_in_part * seq_rows * seq_factor, axis=0)
+    weight_part = jnp.concatenate(
+        [
+            outer_rows(attn_input, grad_projected).astype(jnp.bfloat16),
+            outer_rows(grad_proj_all, attn_out).astype(jnp.bfloat16),
+        ],
+        axis=1,
+    ).reshape(n_seq, n_chip, 2, weight_rows, block_width)
+    gain_terms = (
+        jnp.stack([grad_gain_first, grad_gain_post, grad_gain_mid, grad_gain_last])
+        .astype(jnp.bfloat16)
+        .reshape(-1, n_seq, n_chip, 2, weight_rows)
+        .transpose(1, 2, 3, 0, 4)
+    )
+    gain_terms = jnp.pad(
+        gain_terms,
+        ((0, 0),) * 3
+        + ((0, extra_rows - gain_terms.shape[3]), (0, block_width - weight_rows)),
+    )
+    grad_blocks = jnp.concatenate([weight_part, gain_terms], axis=3).transpose(0, 2, 1, 3, 4)
+    grad_in_parts, grad_sums = sum_last(
+        n_seq,
+        grad_in_part.astype(jnp.bfloat16).reshape(n_plane, piece_len, model_width),
+        grad_blocks,
+    )
+    grad_attn_in = sum_parts(grad_in_parts)
+    factor = lax.rsqrt(jnp.mean(residual * residual, axis=-1, keepdims=True) + EPSILON)
+    unused_first, pull_first = jax.vjp(rms_norm, residual, gain_cols[:, 0])
+    grad_res_first, unused_gain = pull_first(grad_attn_in)
+    input_grad = (grad_after + grad_res_first).reshape(groups, piece_len, model_width)
+
+    weight_sums = grad_sums[:, :weight_rows].astype(jnp.float32)
+    qkv_grad = jnp.concatenate(
+        [weight_sums[c, :, :own_width] for c in range(n_chip)]
+        + [weight_sums[c, :, own_width : own_width + HEAD_DIM] for c in range(n_chip)]
+        + [weight_sums[c, :, own_width + HEAD_DIM : part_width] for c in range(n_chip)],
+        axis=1,
+    )
+    out_proj_grad = jnp.concatenate(
+        [weight_sums[c, :, part_width:] for c in range(n_chip)], axis=1
+    )
+    gain_grad = jnp.sum(
+        grad_sums[:, weight_rows : weight_rows + norm_gains.shape[1], :weight_rows].astype(
+            jnp.float32
+        ),
+        axis=0,
+    ).T
+    return (layer_output, input_grad, gain_grad, qkv_grad, out_proj_grad, gate_up_grad, down_grad)
+
+
 def solution(mesh):
     n_seq = mesh.shape["seq"]
     n_ctx = mesh.shape["ctx"]
@@ -317,8 +1056,15 @@
         P("seq", None),
         P("seq", plane),
     )
+
+    def step(*arrays):
+        groups = arrays[0].shape[0]
+        if n_ctx // 2 == KV_HEADS and groups == 2:
+            return per_device_by_heads(n_seq, *arrays)
+        return per_device_general(*arrays)
+
     return jax.shard_map(
-        per_device,
+        step,
         mesh=split_mesh,
         in_specs=placed,
         out_specs=(tokens, tokens, rows, rows, rows, rows, rows),

time: 1600 us -> 1080 us (0.68)
  waiting for transfers between devices: 1120 us -> 362 us
  Pallas kernels: 0 us -> 361 us
  blocking collectives: 84.4 us -> 0 us
  matrix products: 245 us -> 214 us
  local copies, waits for them, and re-layouts: 61.2 us -> 39.4 us
    reduce_scatter x7 -> x4, waiting for transfers between devices: 638 us -> 160 us  [the longest x1 99.4 us: per_device_by_heads(): lax.psum_scatter(down_part, column, scatter_dimension=0, tiled=True)]
    pallas_call x0 -> x6, Pallas kernels: none -> 361 us  [the longest x2 171 us: plane_exchange(): pl.pallas_call(partial(exchange_kernel, n_plane, by_core), out_shape=jax....]
    all_gather x7 -> x4, waiting for transfers between devices: 478 us -> 201 us  [the longest x1 89.2 us: per_device_by_heads(): ffn_all = lax.all_gather(ffn_input, column, axis=0, tiled=True)]
    all_gather x1 -> x0, blocking collectives: 43.7 us -> none  [per_device(): lax.all_gather(norm_gains, everyone, axis=0, tiled=True).astype(jnp.float32)]
    unnamed x1 -> x0, blocking collectives: 40.8 us -> none
    dot_general x6 -> x0, matrix products: 25.4 us -> none  [the longest x1 6.03 us: per_device(): jnp.einsum('spkgd,slkd->skgpl', grad_heads, value_heads, preferred_elemen...]
  transfers between devices with their start and end apart: 14 -> 8, of which waited for: 14 -> 5; matrix products, arithmetic and copies ran while one was open for 13% -> 26% of each run, Pallas kernels for 0% -> 34%
where the time goes in v2:
time: 1080 us; the launch traced here: 1070 us
  waiting for transfers between devices  362 us (34%)
  Pallas kernels  361 us (33%)
  matrix products  214 us (20%)
  other arithmetic  73.2 us (7%)
  local copies, waits for them, and re-layouts  39.4 us (4%)
  between operations  15.8 us (1%)
    pallas_call x2, Pallas kernels, plane_exchange(): pl.pallas_call(partial(exchange_kernel, n_plane, by_core), out_shape=jax....  171 us
    reduce_scatter x1, waiting for transfers between devices, per_device_by_heads(): lax.psum_scatter(down_part, column, scatter_dimension=0, tiled=True)  99.4 us
    pallas_call x1, Pallas kernels, gather_first(): pl.pallas_call(partial(gather_kernel, n_seq, n_plane), out_shape=[jax.Sha...  95.1 us
    all_gather x1, waiting for transfers between devices, per_device_by_heads(): ffn_all = lax.all_gather(ffn_input, column, axis=0, tiled=True)  89.2 us
    all_gather x1, waiting for transfers between devices, per_device_by_heads(): grad_down_all = lax.all_gather(grad_down_low, column, axis=0, tiled=True)  89.2 us
    dot_general x5, matrix products, times_rows(): lax.dot_general(left, weight_piece, (((1,), (1,)), ((), ())), preferred_e...  86.3 us
    pallas_call x1, Pallas kernels, sum_last(): pl.pallas_call(partial(last_kernel, n_seq, n_plane), out_shape=[jax.Shape...  83.2 us
    dot_general x5, matrix products, add_slice(): return jnp.dot(left, weight_piece, preferred_element_type=jnp.float32)  68.6 us
  transfers between devices with their start and end apart: 8, of which 5 were waited for; matrix products, arithmetic and copies ran while one was open for 26% of the time, Pallas kernels for 34%

profile of v2, /device:TPU:0, one launch (start us, length us, event | category | flops | bytes accessed | tf_op | source)
XLA Modules:
  0.0 1065.6 jit_solution(2225997080689911074)
XLA Ops:
  8.9 1.2 fusion.97
  10.2 1.1 pad_maximum_fusion.5.blocks
  11.3 95.1 %shard_map.144 = (bf16[8,128,2304]{2,1,0:T(8,128)(2,1)}, bf16[4,2,4,80,1536]{4,3,2,1,0:T(8,128)(2,1)}) custom-call(bf16[2,128,2304]{2,1,0:T(8,128)(2,1)} %hidden.1, bf16[4,80,1536]{2,1,0:T(8,128)(2,1)} %pad_maximum_fusion.5.blocks), custom_call_target="tpu_custom_call" | custom-call | tf_op jit(solution)/shard_map/pallas_call | solution.py:323
  106.4 3.7 slice.229
  110.1 5.0 copy.35
  116.3 3.5 fusion.8
  119.9 3.6 fusion.10
  123.5 5.1 fusion.24
  128.6 1.1 slice.234
  130.7 1.6 copy.50
  132.3 1.5 fusion.96
  133.8 1.7 copy.48
  135.5 1.5 copy.49
  137.9 1.9 multiply_cosine_fusion.1
  140.6 1.2 subtract_convert_fusion.1
  141.8 1.1 pad_maximum_fusion.3
  143.2 1.2 copy.51.values
  144.7 2.4 fusion.70
  147.2 3.7 shard_map.145
  150.8 6.3 convolution_convert_fusion.4
  157.2 65.6 %shard_map.146 = bf16[8,128,2304]{2,1,0:T(8,128)(2,1)} custom-call(bf16[8,128,2304]{2,1,0:T(8,128)(2,1)} %bitcast.214), custom_call_target="tpu_custom_call" | custom-call | tf_op jit(solution)/shard_map/pallas_call | solution.py:188
  222.8 3.5 convert_reduce_fusion.1
  226.6 1.3 fusion.44
  227.9 2.5 multiply_convert_fusion.2
  231.2 89.2 %all-gather.5.cloned.1.call-done = bf16[2048,2304]{1,0:T(8,128)(2,1)} async-done(((bf16[256,2304]{1,0:T(8,128)(2,1)}), bf16[2048,2304]{1,0:T(8,128)(2,1)}) %all-gather.5.cloned.1.call-update) | async-done | bytes 9437200 | tf_op jit(solution)/shard_map/all_gather | solution.py:922
  320.4 18.5 %fusion.20 = f32[2048,1152]{1,0:T(8,128)} fusion(bf16[2048,2304]{1,0:T(8,128)(2,1)} %all-gather.5.cloned.1.call-done, bf16[1152,4608]{1,0:T(8,128)(2,1)} %all-gather.7.cloned.1.call-done), kind=kOutput, calls=%fused_computation.40 | convolution fusion | flops 10871635968 | bytes 24182784 | tf_op jit(solution)/shard_map/dot_general | solution.py:99
  338.9 21.5 %multiply_convert_fusion.1 = (bf16[2048,1152]{1,0:T(8,128)(2,1)}, f32[2048,1152]{1,0:T(8,128)}) fusion(f32[2048,1152]{1,0:T(8,128)} %fusion.20, bf16[2048,2304]{1,0:T(8,128)(2,1)} %all-gather.5.cloned.1.call-done, bf16[1152,4608]{1,0:T(8,128)(2,1)} %all-gather.7.cloned.1.call-done), kind=kOutput, calls=%fused_computation.28 | convolution fusion | flops 10895228928 | bytes 38338560 | tf_op jit(solution)/shard_map/dot_general | solution.py:99
  360.4 22.3 %all-gather.9.cloned.1.call-done = bf16[1152,2304]{1,0:T(8,128)(2,1)} async-done(((bf16[288,2304]{1,0:T(8,128)(2,1)}), bf16[1152,2304]{1,0:T(8,128)(2,1)}) %all-gather.9.cloned.1.call-update) | async-done | bytes 5308432 | tf_op jit(solution)/shard_map/all_gather | solution.py:867
  382.7 18.0 %convolution_convert_fusion = bf16[2048,2304]{1,0:T(8,128)(2,1)} fusion(bf16[2048,1152]{1,0:T(8,128)(2,1)} %get-tuple-element.80, bf16[1152,2304]{1,0:T(8,128)(2,1)} %all-gather.9.cloned.1.call-done), kind=kOutput, calls=%fused_computation.5 | convolution fusion | flops 10876354560 | bytes 19464192 | tf_op jit(solution)/shard_map/dot_general | solution.py:95
  400.9 99.4 %reduce-scatter.5.cloned.1.call-done = bf16[256,2304]{1,0:T(8,128)(2,1)} async-done(((bf16[2048,2304]{1,0:T(8,128)(2,1)}), bf16[256,2304]{1,0:T(8,128)(2,1)}) %reduce-scatter.5.cloned.1.call-update) | async-done | bytes 1179664 | tf_op jit(solution)/shard_map/reduce_scatter | solution.py:927
  500.4 1.7 fusion.38
  502.1 2.9 fusion.37
  505.0 2.9 fusion.34
  508.0 89.2 %all-gather.11.cloned.1.call-done = bf16[2048,2304]{1,0:T(8,128)(2,1)} async-done(((bf16[256,2304]{1,0:T(8,128)(2,1)}), bf16[2048,2304]{1,0:T(8,128)(2,1)}) %all-gather.11.cloned.1.call-update) | async-done | bytes 9437200 | tf_op jit(solution)/shard_map/all_gather | solution.py:937
  597.2 17.1 %convolution_convert_fusion.1 = bf16[1152,2304]{1,0:T(8,128)(2,1)} fusion(bf16[2048,1152]{1,0:T(8,128)(2,1)} %get-tuple-element.80, bf16[2048,2304]{1,0:T(8,128)(2,1)} %all-gather.11.cloned.1.call-done), kind=kOutput, calls=%fused_computation.6 | convolution fusion | flops 10874290176 | bytes 19464192 | tf_op jit(solution)/shard_map/dot_general | solution.py:105
  614.3 30.0 %multiply_convert_fusion = (bf16[2048,1152]{1,0:T(8,128)(2,1)}, bf16[2048,1152]{1,0:T(8,128)(2,1)}) fusion(f32[2048,1152]{1,0:T(8,128)} %fusion.20, f32[2048,1152]{1,0:T(8,128)} %get-tuple-element.81, bf16[2048,2304]{1,0:T(8,128)(2,1)} %all-gather.11.cloned.1.call-done, bf16[1152,2304]{1,0:T(8,128)(2,1)} %all-gather.9.cloned.1.call-done), kind=kOutput, calls=%fused_computation.27 | convolution fusion | flops 10928259072 | bytes 43057152 | tf_op jit(solution)/shard_map/dot_general | solution.py:99
  644.3 18.4 %fusion.18 = f32[2048,2304]{1,0:T(8,128)} fusion(bf16[2048,1152]{1,0:T(8,128)(2,1)} %get-tuple-element.39, bf16[1152,4608]{1,0:T(8,128)(2,1)} %all-gather.7.cloned.1.call-done), kind=kOutput, calls=%fused_computation.38 | convolution fusion | flops 10871635968 | bytes 28901376 | tf_op jit(solution)/shard_map/dot_general | solution.py:95
  662.7 21.3 %add_convert_fusion = bf16[2048,2304]{1,0:T(8,128)(2,1)} fusion(f32[2048,2304]{1,0:T(8,128)} %fusion.18, bf16[2048,1152]{1,0:T(8,128)(2,1)} %get-tuple-element.38, bf16[1152,4608]{1,0:T(8,128)(2,1)} %all-gather.7.cloned.1.call-done), kind=kOutput, calls=%fused_computation | convolution fusion | flops 10881073152 | bytes 38338560 | tf_op jit(solution)/shard_map/dot_general | solution.py:95
  684.1 15.1 %convolution_convert_fusion.2 = bf16[1152,2304]{1,0:T(8,128)(2,1)S(1)} fusion(bf16[2048,1152]{1,0:T(8,128)(2,1)} %get-tuple-element.38, bf16[2048,2304]{1,0:T(8,128)(2,1)} %all-gather.5.cloned.1.call-done), kind=kOutput, calls=%fused_computation.7 | convolution fusion | flops 10874290176 | bytes 19464192 | tf_op jit(solution)/shard_map/dot_general | solution.py:105
  699.2 15.2 %convolution_convert_fusion.3 = bf16[1152,2304]{1,0:T(8,128)(2,1)S(1)} fusion(bf16[2048,1152]{1,0:T(8,128)(2,1)} %get-tuple-element.39, bf16[2048,2304]{1,0:T(8,128)(2,1)} %all-gather.5.cloned.1.call-done), kind=kOutput, calls=%fused_computation.8 | convolution fusion | flops 10874290176 | bytes 19464192 | tf_op jit(solution)/shard_map/dot_general | solution.py:105
  714.4 4.7 pad_maximum_fusion
  719.2 3.0 convert_element_type.183
  722.2 60.0 %reduce-scatter.7.cloned.1.call-done = bf16[256,2304]{1,0:T(8,128)(2,1)} async-done(((bf16[2048,2304]{1,0:T(8,128)(2,1)}), bf16[256,2304]{1,0:T(8,128)(2,1)}) %reduce-scatter.7.cloned.1.call-update) | async-done | bytes 1179664 | tf_op jit(solution)/shard_map/reduce_scatter | solution.py:946
  782.3 3.0 fusion.33
  785.3 4.3 multiply_reduce_fusion
  789.7 1.8 fusion.35
  791.5 105.6 %shard_map.147 = bf16[8,128,2304]{2,1,0:T(8,128)(2,1)} custom-call(bf16[2,128,2304]{2,1,0:T(8,128)(2,1)} %bitcast.215), custom_call_target="tpu_custom_call" | custom-call | tf_op jit(solution)/shard_map/pallas_call | solution.py:188
  897.1 5.8 fusion.49.grads
  902.9 7.5 shard_map.148
  910.5 1.3 copy-done.2
  911.8 1.0 copy-done.3
  912.7 2.6 reshape.361
  915.3 2.3 add_convert_fusion.1
  917.7 1.1 pad_maximum_fusion.4
  919.1 2.6 fusion.65
  921.8 6.5 convolution_convert_fusion.6
  928.3 5.6 convolution_convert_fusion.5
  933.9 5.0 pad_maximum_fusion.1
  938.9 10.4 copy.42
  949.3 10.0 fusion.12
  959.8 4.2 fusion.14.blocks
  964.2 83.2 %shard_map.149 = (bf16[8,128,2304]{2,1,0:T(8,128)(2,1)S(1)}, bf16[4,80,1536]{2,1,0:T(8,128)(2,1)S(1)}) custom-call(bf16[8,128,2304]{2,1,0:T(8,128)(2,1)S(1)} %bitcast.196, bf16[4,2,4,80,1536]{4,3,2,1,0:T(8,128)(2,1)S(1)} %fusion.14.blocks), custom_call_target="tpu_custom_call" | custom-call | tf_op jit(solution)/shard_map/pallas_call | solution.py:496
  1051.4 2.1 fusion.36
  1053.5 4.8 convert_element_type.181
  (190 shorter events, 12.7 us)
Async XLA Ops:
  7.2 2.9 copy-start.47
  7.2 224.0 %all-gather.7.cloned.1.call-start = ((), (), s32[]{:S(2)}) async-start(), calls=%async_computation.5 | async-start | bytes 13271040 | tf_op jit(solution)/shard_map/all_gather | solution.py:866
  7.9 312.5 %all-gather.5.cloned.1.call-start = ((), (), s32[]{:S(2)}) async-start(), calls=%async_computation.4 | async-start | bytes 10616832 | tf_op jit(solution)/shard_map/all_gather | solution.py:922
  116.3 7.2 copy-start.28
  116.3 111.5 %copy-start.26 = (f32[2304]{0:T(1024)}, f32[2304]{0:T(1024)S(1)}, u32[]{:S(2)}) copy-start(f32[2304]{0:T(1024)S(1)} %get-tuple-element.31) | copy-start | bytes 27652
  116.3 111.5 %copy-start.30 = (f32[2304]{0:T(1024)}, f32[2304]{0:T(1024)S(1)}, u32[]{:S(2)}) copy-start(f32[2304]{0:T(1024)S(1)} %get-tuple-element.30) | copy-start | bytes 27652
  116.3 7.2 slice-start.2
  119.8 3.7 copy-start.37
  119.8 3.7 slice-start.3
  123.5 5.1 copy-start.17
  132.3 4.8 copy-start.49
  132.3 4.8 copy-start.50
  137.1 7.6 copy-start.45
  137.1 10.0 copy-start.7
  137.9 6.8 copy-start.32
  139.8 2.0 copy-start.19
  147.1 10.0 copy-start
  150.8 6.3 copy-start.5
  222.8 3.8 copy-start.11
  226.3 4.1 copy-start.9
  226.5 3.8 copy-start.39
  226.6 3.8 copy-start.35
  227.8 3.3 copy-start.43
  227.9 3.3 copy-start.41
  230.4 152.3 %all-gather.9.cloned.1.call-start = ((), (), s32[]{:S(2)}) async-start(), calls=%async_computation.6 | async-start | bytes 6635520 | tf_op jit(solution)/shard_map/all_gather | solution.py:867
  231.1 269.2 %reduce-scatter.5.cloned.1.call-start = ((), (), s32[]{:S(2)}) async-start(), calls=%async_computation.7 | async-start | bytes 10616832 | tf_op jit(solution)/shard_map/reduce_scatter | solution.py:927
  400.7 196.4 %all-gather.11.cloned.1.call-start = ((), (), s32[]{:S(2)}) async-start(), calls=%async_computation.8 | async-start | bytes 10616832 | tf_op jit(solution)/shard_map/all_gather | solution.py:937
  500.4 4.6 copy-start.15
  507.9 211.3 %reduce-scatter.11.cloned.1.call-start = ((), (), s32[]{:S(2)}) async-start(), calls=%async_computation.11 | async-start | bytes 6635520 | tf_op jit(solution)/shard_map/reduce_scatter | solution.py:960
  614.3 168.0 %reduce-scatter.7.cloned.1.call-start = ((), (), s32[]{:S(2)}) async-start(), calls=%async_computation.9 | async-start | bytes 10616832 | tf_op jit(solution)/shard_map/reduce_scatter | solution.py:946
  684.1 369.4 %reduce-scatter.9.cloned.1.call-start = ((), (), s32[]{:S(2)}) async-start(), calls=%async_computation.10 | async-start | bytes 13271040 | tf_op jit(solution)/shard_map/reduce_scatter | solution.py:957
  719.0 63.3 %copy-start.31 = (f32[2304]{0:T(1024)S(1)}, f32[2304]{0:T(1024)}, u32[]{:S(2)}) copy-start(f32[2304]{0:T(1024)} %copy-done.30) | copy-start | bytes 27652
  719.0 63.3 %copy-start.42 = (f32[256]{0:T(256)S(1)}, f32[256]{0:T(256)}, u32[]{:S(2)}) copy-start(f32[256]{0:T(256)} %copy-done.41) | copy-start | bytes 3076
  719.1 66.2 %copy-start.44 = (f32[2,128]{1,0:T(2,128)S(1)}, f32[2,128]{1,0:T(2,128)}, u32[]{:S(2)}) copy-start(f32[2,128]{1,0:T(2,128)} %copy-done.43) | copy-start | bytes 3076
  719.1 66.2 %copy-start.27 = (f32[2304]{0:T(1024)S(1)}, f32[2304]{0:T(1024)}, u32[]{:S(2)}) copy-start(f32[2304]{0:T(1024)} %copy-done.26) | copy-start | bytes 27652
  719.1 66.2 %copy-start.36 = (f32[256]{0:T(256)S(1)}, f32[256]{0:T(256)}, u32[]{:S(2)}) copy-start(f32[256]{0:T(256)} %copy-done.35) | copy-start | bytes 3076
  782.3 3.0 copy-start.10
  782.3 3.0 copy-start.16
  785.3 4.4 copy-start.40
  789.7 1.8 copy-start.13
  897.0 5.8 copy-start.1
  897.1 5.8 copy-start.8
  910.5 1.3 copy-start.2
  911.8 1.0 copy-start.3
  915.3 3.8 copy-start.4
  915.3 3.8 copy-start.33
  915.3 3.8 copy-start.46
  917.6 4.2 copy-start.6
  918.8 9.5 slice-start.4
  919.0 9.3 copy-start.20
  919.1 9.2 copy-start.22
  921.8 6.5 copy-start.24
  921.8 6.5 slice-start.5
  938.9 10.4 copy-start.21
  938.9 10.4 copy-start.23
  938.9 10.4 copy-start.25
  938.9 10.4 copy-start.38
  959.5 4.5 slice-start
  959.8 4.4 slice-start.1
  1047.4 1.4 copy-start.12
  1047.4 1.4 copy-start.29
  1048.0 1.2 copy-start.48
  1049.2 2.3 copy-start.14
  1049.6 3.9 copy-start.34
  (1 other events, 0.8 us)
Sparse Core Ops, SparseCore 0:
  9.8 184.2 all-gather.6
  230.5 89.8 all-gather.4
  322.2 60.4 all-gather.8
  400.8 99.5 reduce-scatter.4
  508.0 89.0 all-gather.10
  614.4 60.4 reduce-scatter.10
  684.2 98.0 reduce-scatter.6
  785.4 153.4 reduce-scatter.8

commit v3 on v2

--- a/solution.py
+++ b/solution.py
@@ -611,6 +611,401 @@
     )(queries, keys, values, segment_col, segment_row, grads)
 
 
+GELU_SCALE = math.sqrt(2.0 / math.pi)
+
+
+def gelu_pieces(gate):
+    bend = jnp.tanh(GELU_SCALE * (gate + 0.044715 * gate * gate * gate))
+    value = 0.5 * gate * (1.0 + bend)
+    slope = 0.5 * (1.0 + bend) + 0.5 * gate * (1.0 - bend * bend) * GELU_SCALE * (
+        1.0 + 3.0 * 0.044715 * gate * gate
+    )
+    return value, slope
+
+
+def units_kernel(n_seq, backward, *refs):
+    if backward:
+        tokens, units, downs, kept_gate, kept_up = refs[:5]
+        out, tokens_all, first_out, second_out = refs[5:9]
+        stage_outs = (first_out, second_out)
+        scratch = refs[9:]
+    else:
+        tokens, units, downs = refs[:3]
+        out, tokens_all, first_out, second_out, third_out = refs[3:8]
+        stage_outs = (first_out, second_out, third_out)
+        scratch = refs[8:]
+    units_v, downs_v, held, own_sum, twin_sum, twin_out, line, stage = scratch[:8]
+    scratch = scratch[8:]
+    if backward:
+        kept, kept_sem = scratch[:2]
+        scratch = scratch[2:]
+    (
+        weight_sem,
+        own_sem,
+        left_send,
+        right_send,
+        token_recv,
+        twin_send,
+        twin_recv,
+        part_send,
+        part_recv,
+        line_send,
+        line_recv,
+        stage_sem,
+        all_sem,
+        out_sem,
+    ) = scratch
+    n = n_seq
+    s = lax.axis_index("seq")
+    k = lax.axis_index("core")
+    twin = {"core": 1 - k}
+    n_units, width = downs_v.shape
+    piece_len = tokens.shape[1]
+    at_end = (s == 0) | (s == n - 1)
+
+    def token_left(d, h, source):
+        return remote(
+            source, held.at[d, h, 0], left_send.at[d, h], token_recv.at[d, h], {"seq": s - 1}
+        )
+
+    def token_right(d, h, source):
+        return remote(
+            source, held.at[d, h, 0], right_send.at[d, h], token_recv.at[d, h], {"seq": s + 1}
+        )
+
+    def token_twin(d, h, source):
+        return remote(source, held.at[d, h, 1], twin_send.at[d, h], twin_recv.at[d, h], twin)
+
+    def part_twin(d, h):
+        return remote(
+            twin_out.at[d, h], twin_sum.at[d, h], part_send.at[d, h], part_recv.at[d, h], twin
+        )
+
+    def part_line(d, h):
+        to_left = d < s
+        slot = jnp.where(to_left, d, d + 1)
+        return remote(
+            twin_sum.at[d, h],
+            line.at[slot, h],
+            line_send.at[d, h],
+            line_recv.at[slot, h],
+            {"seq": jnp.where(to_left, s - 1, s + 1)},
+        )
+
+    def line_arrival(slot, h):
+        return remote(
+            twin_sum.at[0, h],
+            line.at[slot, h],
+            line_send.at[0, h],
+            line_recv.at[slot, h],
+            {"seq": s},
+        )
+
+    def own_load(h):
+        return pltpu.make_async_copy(tokens.at[h], held.at[s, h, 0], own_sem.at[h])
+
+    def all_store(d, h):
+        return pltpu.make_async_copy(held.at[d, h], tokens_all.at[d, h], all_sem.at[d, h])
+
+    def stage_store(i, d, h, slot):
+        return pltpu.make_async_copy(
+            stage.at[i, slot], stage_outs[i].at[2 * d + h], stage_sem.at[i, slot]
+        )
+
+    def kept_load(i, d, h, slot):
+        source = (kept_gate, kept_up)[i]
+        return pltpu.make_async_copy(source.at[2 * d + h], kept.at[i, slot], kept_sem.at[i, slot])
+
+    def source(p):
+        inner = jnp.minimum(s, n - 1 - s)
+        near = lax.div(p + 1, 2)
+        paired = jnp.where(lax.rem(p, 2) == 1, s - near, s + near)
+        far = p - inner
+        single = jnp.where(s < n - 1 - s, s + far, s - far)
+        return jnp.where(p <= 2 * inner, paired, single)
+
+    barrier = pltpu.get_barrier_semaphore()
+    pl.semaphore_signal(barrier, inc=1, device_id=twin, device_id_type=MESH)
+
+    @pl.when(s > 0)
+    def _():
+        pl.semaphore_signal(barrier, inc=1, device_id={"seq": s - 1}, device_id_type=MESH)
+
+    @pl.when(s < n - 1)
+    def _():
+        pl.semaphore_signal(barrier, inc=1, device_id={"seq": s + 1}, device_id_type=MESH)
+
+    pl.semaphore_wait(barrier, 1 + jnp.where(s > 0, 1, 0) + jnp.where(s < n - 1, 1, 0))
+
+    for h in range(2):
+
+        @pl.when(s < n - 1)
+        def _():
+            token_right(s, h, tokens.at[h]).start()
+
+        @pl.when(s > 0)
+        def _():
+            token_left(s, h, tokens.at[h]).start()
+
+        token_twin(s, h, tokens.at[h]).start()
+        own_load(h).start()
+    load_units = pltpu.make_async_copy(units, units_v, weight_sem.at[0])
+    load_downs = pltpu.make_async_copy(downs, downs_v, weight_sem.at[1])
+    load_units.start()
+    load_downs.start()
+    if backward:
+        for i in range(2):
+            kept_load(i, s, 0, 0).start()
+    load_units.wait()
+    load_downs.wait()
+
+    def add_rows(d, h, into_own, use_line):
+        step = 16
+
+        def body(i, carry):
+            rows = pl.ds(pl.multiple_of(i * step, step), step)
+            total = own_sum[d, h, rows, :] + twin_sum[d, h, rows, :].astype(jnp.float32)
+            for slot in use_line:
+                total = total + line[slot, h, rows, :].astype(jnp.float32)
+            if into_own:
+                own_sum[d, h, rows, :] = total
+            else:
+                twin_sum[d, h, rows, :] = total.astype(twin_sum.dtype)
+            return carry
+
+        lax.fori_loop(0, piece_len // step, body, 0)
+
+    def combine(d, h):
+        to_left = d < s
+        slot = jnp.where(to_left, d, d + 1)
+        more = jnp.where(to_left, s < n - 1, s > 0)
+        part_twin(d, h).wait_recv()
+
+        @pl.when(more)
+        def _():
+            line_arrival(slot, h).wait_recv()
+            add_rows(d, h, False, (slot,))
+
+        @pl.when(jnp.logical_not(more))
+        def _():
+            add_rows(d, h, False, ())
+
+        part_line(d, h).start()
+
+    columns = width // 3
+    chunk = n_units // 3
+
+    def compute_forward(d, h, slot):
+        rows = held[d, h].reshape(2 * piece_len, width)
+        for c in range(3):
+            cols = slice(c * chunk, (c + 1) * chunk)
+            gate = times_rows(rows, units_v[cols, :width])
+            up = times_rows(rows, units_v[cols, width:])
+            value, unused = gelu_pieces(gate)
+            stage[0, slot, :, cols] = gate.astype(stage.dtype)
+            stage[1, slot, :, cols] = up.astype(stage.dtype)
+            stage[2, slot, :, cols] = (value * up).astype(stage.dtype)
+        for c in range(3):
+            cols = slice(c * columns, (c + 1) * columns)
+            part = add_slice(stage[2, slot], downs_v[:, cols])
+            own_sum[d, h, :, cols] = part[:piece_len]
+            twin_out[d, h, :, cols] = part[piece_len:].astype(twin_out.dtype)
+
+    def compute_backward(d, h, slot):
+        rows = held[d, h].reshape(2 * piece_len, width)
+        for c in range(3):
+            cols = slice(c * chunk, (c + 1) * chunk)
+            grad = times_rows(rows, downs_v[cols, :])
+            value, slope = gelu_pieces(kept[0, slot, :, cols].astype(jnp.float32))
+            up = kept[1, slot, :, cols].astype(jnp.float32)
+            stage[0, slot, :, cols] = (grad * up * slope).astype(stage.dtype)
+            stage[1, slot, :, cols] = (grad * value).astype(stage.dtype)
+        for c in range(3):
+            cols = slice(c * columns, (c + 1) * columns)
+            later = slice(width + c * columns, width + (c + 1) * columns)
+            part = add_slice(stage[0, slot], units_v[:, cols])
+            part = part + add_slice(stage[1, slot], units_v[:, later])
+            own_sum[d, h, :, cols] = part[:piece_len]
+            twin_out[d, h, :, cols] = part[piece_len:].astype(twin_out.dtype)
+
+    def unit(t, carry):
+        d = source(lax.div(t, 2))
+        h = lax.rem(t, 2)
+        slot = lax.rem(t, 2)
+
+        @pl.when(t < 2)
+        def _():
+            own_load(h).wait()
+
+        @pl.when(t >= 2)
+        def _():
+            piece = held.at[d, h, 0]
+            token_left(d, h, piece).wait_recv()
+
+            @pl.when((d < s) & (s < n - 1))
+            def _():
+                token_right(d, h, piece).start()
+
+            @pl.when((d > s) & (s > 0))
+            def _():
+                token_left(d, h, piece).start()
+
+            token_twin(d, h, piece).start()
+            for i in range(len(stage_outs)):
+                stage_store(i, d, h, slot).wait()
+
+        if backward:
+
+            @pl.when(t < 2 * n - 1)
+            def _():
+                for i in range(2):
+                    kept_load(
+                        i, source(lax.div(t + 1, 2)), lax.rem(t + 1, 2), 1 - slot
+                    ).start()
+
+            for i in range(2):
+                kept_load(i, d, h, slot).wait()
+        token_twin(d, h, held.at[d, h, 0]).wait_recv()
+        if backward:
+            compute_backward(d, h, slot)
+        else:
+            compute_forward(d, h, slot)
+        part_twin(d, h).start()
+        all_store(d, h).start()
+        for i in range(len(stage_outs)):
+            stage_store(i, d, h, slot).start()
+
+        @pl.when(at_end & (t >= 3))
+        def _():
+            combine(source(lax.div(t - 1, 2)), lax.rem(t - 1, 2))
+
+        return carry
+
+    lax.fori_loop(0, 2 * n, unit, 0)
+
+    @pl.when(at_end)
+    def _():
+        combine(source(n - 1), 1)
+
+    @pl.when(jnp.logical_not(at_end))
+    def _():
+        right_first = 2 * s < n - 1
+
+        def middle(i, carry):
+            h = lax.rem(i, 2)
+            j = lax.rem(lax.div(i, 2), n - 1) + 1
+            to_right = jnp.where(i < 2 * (n - 1), right_first, jnp.logical_not(right_first))
+            d = jnp.where(to_right, s + j, s - j)
+
+            @pl.when((d >= 0) & (d <= n - 1))
+            def _():
+                combine(d, h)
+
+            return carry
+
+        lax.fori_loop(0, 4 * (n - 1), middle, 0)
+
+    def finish(h, carry):
+        part_twin(s, h).wait_recv()
+
+        @pl.when(s < n - 1)
+        def _():
+            line_arrival(s, h).wait_recv()
+
+        @pl.when(s > 0)
+        def _():
+            line_arrival(s + 1, h).wait_recv()
+
+        @pl.when(s == 0)
+        def _():
+            add_rows(s, h, True, (s,))
+
+        @pl.when(s == n - 1)
+        def _():
+            add_rows(s, h, True, (s + 1,))
+
+        @pl.when(jnp.logical_not(at_end))
+        def _():
+            add_rows(s, h, True, (s, s + 1))
+
+        pltpu.make_async_copy(own_sum.at[s, h], out.at[h], out_sem.at[h]).start()
+        return carry
+
+    lax.fori_loop(0, 2, finish, 0)
+
+    def drain(t, carry):
+        d = lax.div(t, 2)
+        h = lax.rem(t, 2)
+        piece = held.at[d, h, 0]
+
+        @pl.when((d <= s) & (s < n - 1))
+        def _():
+            token_right(d, h, piece).wait_send()
+
+        @pl.when((d >= s) & (s > 0))
+        def _():
+            token_left(d, h, piece).wait_send()
+
+        token_twin(d, h, piece).wait_send()
+        part_twin(d, h).wait_send()
+
+        @pl.when(d != s)
+        def _():
+            part_line(d, h).wait_send()
+
+        all_store(d, h).wait()
+        return carry
+
+    lax.fori_loop(0, 2 * n, drain, 0)
+    for h in range(2):
+        for i in range(len(stage_outs)):
+            stage_store(i, 0, h, h).wait()
+        pltpu.make_async_copy(own_sum.at[s, h], out.at[h], out_sem.at[h]).wait()
+
+
+def run_units(n_seq, tokens, units, downs, kept=None):
+    backward = kept is not None
+    low = tokens.dtype
+    n_units = downs.shape[0]
+    halves, piece_len, width = tokens.shape
+    n_stage = 2 if backward else 3
+    held = (n_seq, halves, 2, piece_len, width)
+    unit_rows = (2 * n_seq, 2 * piece_len, n_units)
+    sums = (n_seq, halves, piece_len, width)
+    scratch = [
+        pltpu.VMEM(units.shape, low),
+        pltpu.VMEM(downs.shape, low),
+        pltpu.VMEM(held, low),
+        pltpu.VMEM(sums, jnp.float32),
+        pltpu.VMEM(sums, low),
+        pltpu.VMEM(sums, low),
+        pltpu.VMEM((n_seq + 1,) + sums[1:], low),
+        pltpu.VMEM((n_stage, 2) + unit_rows[1:], low),
+    ]
+    if backward:
+        scratch += [pltpu.VMEM((2, 2) + unit_rows[1:], low), DMA((2, 2))]
+    pairs = DMA((n_seq, halves))
+    scratch += [DMA((2,)), DMA((halves,))] + [pairs] * 8
+    scratch += [DMA((n_seq + 1, halves)), DMA((n_stage, 2)), pairs, DMA((halves,))]
+    operands = (tokens, units, downs) + (tuple(kept) if backward else ())
+    return pl.pallas_call(
+        partial(units_kernel, n_seq, backward),
+        out_shape=[
+            jax.ShapeDtypeStruct(tokens.shape, jnp.float32),
+            jax.ShapeDtypeStruct(held, low),
+        ]
+        + [jax.ShapeDtypeStruct(unit_rows, low)] * n_stage,
+        in_specs=[ANY] * len(operands),
+        out_specs=[ANY] * (2 + n_stage),
+        scratch_shapes=scratch,
+        compiler_params=pltpu.CompilerParams(
+            collective_id=6 if backward else 5,
+            has_side_effects=True,
+            vmem_limit_bytes=62 * 1024 * 1024,
+        ),
+    )(*operands)
+
+
 def per_device_general(
     hidden_in,
     norm_gains,
@@ -815,7 +1210,6 @@
     padding,
     positions,
 ):
-    column = ("seq", "core")
     groups, piece_len, model_width = hidden_in.shape
     row_count = groups * piece_len
     seq_len = segment_ids.shape[1]
@@ -919,33 +1313,31 @@
     after_attn = residual + rms_norm(attn_proj, gain_cols[:, 1])
     ffn_input = rms_norm(after_attn, gain_cols[:, 2]).astype(jnp.bfloat16)
 
-    ffn_all = lax.all_gather(ffn_input, column, axis=0, tiled=True)
-    gate_part = times_rows(ffn_all, unit_weights[:, :model_width])
-    up_part = times_rows(ffn_all, unit_weights[:, model_width:])
-    hidden_part = geglu_parts(gate_part, up_part).astype(jnp.bfloat16)
-    down_part = add_slice(hidden_part, down_units).astype(jnp.bfloat16)
-    down_out = lax.psum_scatter(down_part, column, scatter_dimension=0, tiled=True).astype(
-        jnp.float32
-    )
+    pieces = (groups, piece_len, model_width)
+    down_out, ffn_all, gate_part, up_part, hidden_part = run_units(
+        n_seq, ffn_input.reshape(pieces), unit_weights, down_units
+    )
+    down_out = down_out.reshape(row_count, model_width)
     layer_out = after_attn + rms_norm(down_out, gain_cols[:, 3])
-    layer_output = layer_out.astype(jnp.bfloat16).reshape(groups, piece_len, model_width)
+    layer_output = layer_out.astype(jnp.bfloat16).reshape(pieces)
 
     cotangent = output_cotangent.reshape(row_count, model_width).astype(jnp.float32)
     unused_last, pull_last = jax.vjp(rms_norm, down_out, gain_cols[:, 3])
     grad_down, grad_gain_last = pull_last(cotangent)
-    grad_down_low = grad_down.astype(jnp.bfloat16)
-    grad_down_all = lax.all_gather(grad_down_low, column, axis=0, tiled=True)
-    grad_part = times_rows(grad_down_all, down_units)
-    unused_units, pull_units = jax.vjp(geglu_parts, gate_part, up_part)
-    grad_gate_part, grad_up_part = pull_units(grad_part)
-    gate_low = grad_gate_part.astype(jnp.bfloat16)
-    up_low = grad_up_part.astype(jnp.bfloat16)
-    grad_ffn_part = add_slice(gate_low, unit_weights[:, :model_width]) + add_slice(
-        up_low, unit_weights[:, model_width:]
-    )
-    grad_ffn_in = lax.psum_scatter(
-        grad_ffn_part.astype(jnp.bfloat16), column, scatter_dimension=0, tiled=True
-    ).astype(jnp.float32)
+    grad_ffn_in, grad_down_all, gate_low, up_low = run_units(
+        n_seq,
+        grad_down.astype(jnp.bfloat16).reshape(pieces),
+        unit_weights,
+        down_units,
+        (gate_part, up_part),
+    )
+    grad_ffn_in = grad_ffn_in.reshape(row_count, model_width)
+    ffn_all = ffn_all.reshape(-1, model_width)
+    grad_down_all = grad_down_all.reshape(-1, model_width)
+    n_units = down_units.shape[0]
+    gate_low, up_low, hidden_part = (
+        array.reshape(-1, n_units) for array in (gate_low, up_low, hidden_part)
+    )
     gate_up_rows = jnp.concatenate(
         [
             outer_rows(gate_low, ffn_all).astype(jnp.bfloat16),

time: 1080 us -> 909 us (0.84)
  waiting for transfers between devices: 362 us -> 19.7 us
  Pallas kernels: 361 us -> 657 us
  matrix products: 214 us -> 85.5 us
    pallas_call x0 -> x2, Pallas kernels: none -> 305 us  [run_units(): pl.pallas_call(partial(units_kernel, n_seq, backward), out_shape=[jax.Sha...]
    all_gather x2 -> x0, waiting for transfers between devices: 178 us -> none  [the longest x1 89.2 us: per_device_by_heads(): ffn_all = lax.all_gather(ffn_input, column, axis=0, tiled=True)]
    reduce_scatter x2 -> x0, waiting for transfers between devices: 159 us -> none  [the longest x1 99.4 us: per_device_by_heads(): lax.psum_scatter(down_part, column, scatter_dimension=0, tiled=True)]
    dot_general x5 -> x2, matrix products: 86.3 us -> 16.7 us  [times_rows(): lax.dot_general(left, weight_piece, (((1,), (1,)), ((), ())), preferred_e...]
    dot_general x5 -> x2, matrix products: 68.6 us -> 11.2 us  [add_slice(): return jnp.dot(left, weight_piece, preferred_element_type=jnp.float32)]
    all_gather x1, waiting for transfers between devices: 22.3 us -> 0.01 us  [per_device_by_heads(): down_units = lax.all_gather(down_weight, 'chip', axis=0, tiled=True)]
    all_gather x1, waiting for transfers between devices: 0.02 us -> 18.3 us  [per_device_by_heads(): unit_weights = lax.all_gather(gate_up_weight, 'chip', axis=0, tiled=True)]
  transfers between devices with their start and end apart: 8 -> 4, of which waited for: 5 -> 1; matrix products, arithmetic and copies ran while one was open for 26% -> 18% of each run, Pallas kernels for 34% -> 39%
where the time goes in v3:
time: 909 us; the launch traced here: 900 us
  Pallas kernels  657 us (72%)
  matrix products  85.5 us (9%)
  other arithmetic  74.6 us (8%)
  local copies, waits for them, and re-layouts  47.2 us (5%)
  waiting for transfers between devices  19.7 us (2%)
  between operations  15.1 us (2%)
    pallas_call x2, Pallas kernels, run_units(): pl.pallas_call(partial(units_kernel, n_seq, backward), out_shape=[jax.Sha...  305 us
    pallas_call x2, Pallas kernels, plane_exchange(): pl.pallas_call(partial(exchange_kernel, n_plane, by_core), out_shape=jax....  161 us
    pallas_call x1, Pallas kernels, gather_first(): pl.pallas_call(partial(gather_kernel, n_seq, n_plane), out_shape=[jax.Sha...  94.4 us
    pallas_call x1, Pallas kernels, sum_last(): pl.pallas_call(partial(last_kernel, n_seq, n_plane), out_shape=[jax.Shape...  85.6 us
    dot_general x5, matrix products, outer_rows(): lax.dot_general(left, right, (((0,), (0,)), ((), ())), preferred_element_...  57.6 us
    unnamed x111, local copies, waits for them, and re-layouts  20.6 us
    all_gather x1, waiting for transfers between devices, per_device_by_heads(): unit_weights = lax.all_gather(gate_up_weight, 'chip', axis=0, tiled=True)  18.3 us
  transfers between devices with their start and end apart: 4, of which 1 were waited for; matrix products, arithmetic and copies ran while one was open for 18% of the time, Pallas kernels for 39%

profile of v3, /device:TPU:0, one launch (start us, length us, event | category | flops | bytes accessed | tf_op | source)
XLA Modules:
  0.0 899.7 jit_solution(12542160064783612747)
XLA Ops:
  8.0 0.7 all-gather.3.cloned.1.call-update
  8.9 1.1 pad_maximum_fusion.5.blocks
  10.0 94.4 %shard_map.144 = (bf16[8,128,2304]{2,1,0:T(8,128)(2,1)}, bf16[4,2,4,80,1536]{4,3,2,1,0:T(8,128)(2,1)}) custom-call(bf16[2,128,2304]{2,1,0:T(8,128)(2,1)} %hidden.1, bf16[4,80,1536]{2,1,0:T(8,128)(2,1)} %pad_maximum_fusion.5.blocks), custom_call_target="tpu_custom_call" | custom-call | tf_op jit(solution)/shard_map/pallas_call | solution.py:323
  104.4 3.7 slice.219
  108.1 3.8 copy.35
  111.9 0.8 convert_bitcast_fusion
  113.0 3.5 fusion.1
  116.8 1.1 fusion.3
  117.9 3.6 copy-done.21
  121.5 5.4 fusion.10
  127.1 1.5 slice.221
  129.0 1.3 copy.50
  130.3 3.4 fusion.72
  133.7 1.9 copy.49
  135.6 2.2 copy.48
  137.8 0.8 select_reduce_fusion
  138.6 1.9 multiply_cosine_fusion.1
  140.5 0.8 copy-done.24
  141.3 2.2 subtract_convert_fusion.1
  143.5 1.1 pad_maximum_fusion.3
  144.9 2.4 fusion.45
  147.4 3.8 shard_map.145
  151.2 6.7 convolution_convert_fusion.3
  157.9 86.0 %shard_map.146 = bf16[8,128,2304]{2,1,0:T(8,128)(2,1)} custom-call(bf16[8,128,2304]{2,1,0:T(8,128)(2,1)} %bitcast.149), custom_call_target="tpu_custom_call" | custom-call | tf_op jit(solution)/shard_map/pallas_call | solution.py:188
  243.9 3.4 convert_reduce_fusion.1
  247.6 1.9 copy-done.16
  250.1 1.4 copy-done.11
  251.5 1.3 multiply_convert_fusion.refs_0_
  252.7 18.3 %all-gather.3.cloned.1.call-done.refs_1_ = bf16[1152,4608]{1,0:T(8,128)(2,1)} async-done(((bf16[288,4608]{1,0:T(8,128)(2,1)}), bf16[1152,4608]{1,0:T(8,128)(2,1)}) %all-gather.3.cloned.1.call-update) | async-done | bytes 10616848 | tf_op jit(solution)/shard_map/all_gather | solution.py:1260
  271.1 152.2 %shard_map.147 = (f32[2,128,2304]{2,1,0:T(8,128)}, bf16[4,2,2,128,2304]{4,3,2,1,0:T(8,128)(2,1)}, bf16[8,256,1152]{2,1,0:T(8,128)(2,1)}, bf16[8,256,1152]{2,1,0:T(8,128)(2,1)}, bf16[8,256,1152]{2,1,0:T(8,128)(2,1)}) custom-call(bf16[2,128,2304]{2,1,0:T(8,128)(2,1)} %multiply_convert_fusion.refs_0_, bf16[1152,4608]{1,0:T(8,128)(2,1)} %all-gather.3.cloned.1.call-done.refs_1_, ...), custom_call_target="tpu_custom_call" | custom-call | tf_op jit(solution)/shard_map/pallas_call | solution.py:991
  423.2 2.1 multiply_reduce_fusion.4
  425.6 2.3 fusion.15
  427.9 3.3 fusion.16
  431.2 152.8 %shard_map.148 = (f32[2,128,2304]{2,1,0:T(8,128)}, bf16[4,2,2,128,2304]{4,3,2,1,0:T(8,128)(2,1)}, bf16[8,256,1152]{2,1,0:T(8,128)(2,1)}, bf16[8,256,1152]{2,1,0:T(8,128)(2,1)}) custom-call(bf16[2,128,2304]{2,1,0:T(8,128)(2,1)} %get-tuple-element.62.refs_0_, bf16[1152,4608]{1,0:T(8,128)(2,1)} %all-gather.3.cloned.1.call-done.refs_1_, ...), custom_call_target="tpu_custom_call" | custom-call | tf_op jit(solution)/shard_map/pallas_call | solution.py:991
  584.0 17.1 %convolution_convert_fusion = bf16[1152,2304]{1,0:T(8,128)(2,1)} fusion(bf16[2048,1152]{1,0:T(8,128)(2,1)} %bitcast.165, bf16[2048,2304]{1,0:T(8,128)(2,1)} %bitcast.164), kind=kOutput, calls=%fused_computation.2 | convolution fusion | flops 10874290176 | bytes 19464192 | tf_op jit(solution)/shard_map/dot_general | solution.py:105
  601.2 15.4 %convolution_convert_fusion.1 = bf16[1152,2304]{1,0:T(8,128)(2,1)S(1)} fusion(bf16[2048,1152]{1,0:T(8,128)(2,1)} %bitcast.167, bf16[2048,2304]{1,0:T(8,128)(2,1)} %bitcast.160), kind=kOutput, calls=%fused_computation.3 | convolution fusion | flops 10874290176 | bytes 19464192 | tf_op jit(solution)/shard_map/dot_general | solution.py:105
  616.7 13.1 %convolution_convert_fusion.2 = bf16[1152,2304]{1,0:T(8,128)(2,1)S(1)} fusion(bf16[2048,1152]{1,0:T(8,128)(2,1)} %bitcast.166, bf16[2048,2304]{1,0:T(8,128)(2,1)S(1)} %bitcast.163), kind=kOutput, calls=%fused_computation.4 | convolution fusion | flops 10874290176 | bytes 19464192 | tf_op jit(solution)/shard_map/dot_general | solution.py:105
  629.8 5.0 pad_maximum_fusion
  635.0 3.2 multiply_reduce_fusion
  638.4 0.7 copy-done.13
  639.2 4.5 multiply_reduce_fusion.1
  644.0 4.8 fusion.17.source
  648.7 75.1 %shard_map.149 = bf16[8,128,2304]{2,1,0:T(8,128)(2,1)} custom-call(bf16[2,128,2304]{2,1,0:T(8,128)(2,1)} %fusion.17.source), custom_call_target="tpu_custom_call" | custom-call | tf_op jit(solution)/shard_map/pallas_call | solution.py:188
  723.9 5.9 fusion.24.grads
  729.8 7.5 shard_map.150
  737.4 1.3 copy-done.4
  738.7 1.0 copy-done.5
  739.6 2.6 reshape.577
  742.2 2.4 add_convert_fusion.1
  744.6 1.1 pad_maximum_fusion.4
  746.1 1.1 copy-done.6
  747.2 2.3 fusion.40
  749.7 6.5 convolution_convert_fusion.5
  756.2 5.6 convolution_convert_fusion.4
  761.7 5.0 pad_maximum_fusion.1
  766.7 10.5 %copy.42 = bf16[2304,1536]{1,0:T(8,128)(2,1)} copy(bf16[2304,1536]{0,1:T(8,128)(2,1)} %pad_maximum_fusion.1) | data formatting | bytes 14155776 | tf_op jit(solution)/shard_map/concatenate | solution.py:1381
  777.2 10.0 %fusion.5 = (bf16[2304]{0:T(1024)(128)(2,1)S(1)}, bf16[1024,2304]{1,0:T(8,128)(2,1)}) fusion(bf16[8,128,2304]{2,1,0:T(8,128)(2,1)} %get-tuple-element.23, f32[1024]{0:T(1024)S(1)} %rsqrt_bitcast_fusion, bf16[2304,1536]{1,0:T(8,128)(2,1)} %bitcast.141, bf16[1024,256]{1,0:T(8,128)(2,1)S(1)} %copy-done.30, bf16[1024,256]{1,0:T(8,128)(2,1)S(1)} %copy-done.32, ...), kind=kOutput, calls=%fused_computation.15 | convolution fusion | flops 4849924096 | bytes 16261632 | tf_op jit(solution)/shard_map/dot_general | solution.py:99
  787.4 5.0 fusion.7.blocks
  792.4 85.6 %shard_map.151 = (bf16[8,128,2304]{2,1,0:T(8,128)(2,1)S(1)}, bf16[4,80,1536]{2,1,0:T(8,128)(2,1)S(1)}) custom-call(bf16[8,128,2304]{2,1,0:T(8,128)(2,1)S(1)} %bitcast.133, bf16[4,2,4,80,1536]{4,3,2,1,0:T(8,128)(2,1)S(1)} %fusion.7.blocks), custom_call_target="tpu_custom_call" | custom-call | tf_op jit(solution)/shard_map/pallas_call | solution.py:496
  881.0 0.9 pad_maximum_fusion.8
  881.9 1.2 copy-done.15
  883.1 2.1 fusion.18
  885.1 3.0 convert_element_type.163
  888.1 4.8 convert_element_type.161
  (153 shorter events, 7.8 us)
Async XLA Ops:
  7.2 1.6 copy-start.28
  7.2 1.6 copy-start.33
  7.2 245.5 %all-gather.5.cloned.1.call-start = ((), (), s32[]{:S(2)}) async-start(), calls=%async_computation.3 | async-start | bytes 6635520 | tf_op jit(solution)/shard_map/all_gather | solution.py:1261
  7.9 0.9 copy-start.37
  7.9 263.1 %all-gather.3.cloned.1.call-start = ((), (), s32[]{:S(2)}) async-start(), calls=%async_computation.2 | async-start | bytes 13271040 | tf_op jit(solution)/shard_map/all_gather | solution.py:1260
  8.7 876.5 %reduce-scatter.5.cloned.1.call-start = ((), (), s32[]{:S(2)}) async-start(), calls=%async_computation.5 | async-start | bytes 6635520 | tf_op jit(solution)/shard_map/reduce_scatter | solution.py:1352
  113.0 3.5 copy-start.34
  113.0 3.8 copy-start.18
  116.8 4.7 copy-start.21
  117.9 8.9 copy-start.22
  127.0 1.5 copy-start.38
  127.0 1.5 copy-start.39
  129.0 18.4 %copy-start = (bf16[1024,256]{1,0:T(8,128)(2,1)}, bf16[1024,256]{1,0:T(8,128)(2,1)S(1)}, u32[]{:S(2)}) copy-start(bf16[1024,256]{1,0:T(8,128)(2,1)S(1)} %copy.51.values) | copy-start | bytes 1572868
  140.5 0.8 copy-start.24
  140.5 4.1 copy-start.23
  143.5 1.4 copy-start.25
  147.4 10.5 %copy-start.2 = (bf16[1024,256]{1,0:T(8,128)(2,1)}, bf16[1024,256]{1,0:T(8,128)(2,1)S(1)}, u32[]{:S(2)}) copy-start(bf16[1024,256]{1,0:T(8,128)(2,1)S(1)} %pad_maximum_fusion.9.keys) | copy-start | bytes 1572868
  151.2 6.7 copy-start.7
  247.3 2.8 copy-start.9
  247.3 2.1 copy-start.16
  250.0 1.4 copy-start.11
  423.2 2.4 copy-start.14
  425.3 2.6 copy-start.12
  425.3 2.6 copy-start.19
  601.1 15.5 %slice-start.4 = ((s8[9437184]{0:T(1024)(128)(4,1)}), s8[1048576]{0:T(1024)(128)(4,1)S(1)}, s32[]{:S(2)}) async-start(s8[9437184]{0:T(1024)(128)(4,1)} %bitcast.161), calls=%async_computation.10 | async-start | bytes 2097152
  601.2 287.0 %reduce-scatter.3.cloned.1.call-start = ((), (), s32[]{:S(2)}) async-start(), calls=%async_computation.4 | async-start | bytes 13271040 | tf_op jit(solution)/shard_map/reduce_scatter | solution.py:1349
  601.2 15.5 %slice-start.5 = ((s8[9437184]{0:T(1024)(128)(4,1)}), s8[4194304]{0:T(1024)(128)(4,1)S(1)}, s32[]{:S(2)}) async-start(s8[9437184]{0:T(1024)(128)(4,1)} %bitcast.161), calls=%async_computation.11 | async-start | bytes 8388608
  601.2 15.5 %slice-start.6 = ((s8[9437184]{0:T(1024)(128)(4,1)}), s8[4194304]{0:T(1024)(128)(4,1)S(1)}, s32[]{:S(2)}) async-start(s8[9437184]{0:T(1024)(128)(4,1)} %bitcast.161), calls=%async_computation.12 | async-start | bytes 8388608
  634.8 3.4 copy-start.20
  635.0 3.5 copy-start.10
  635.0 4.2 copy-start.13
  723.9 5.9 copy-start.1
  723.9 5.9 copy-start.3
  737.3 1.3 copy-start.4
  738.7 1.0 copy-start.5
  745.7 1.5 copy-start.6
  746.0 10.1 %copy-start.26 = (bf16[128,8,2,256]{3,1,2,0:T(8,128)(2,1)}, bf16[128,8,2,256]{3,1,2,0:T(8,128)(2,1)S(1)}, u32[]{:S(2)}) copy-start(bf16[128,8,2,256]{3,1,2,0:T(8,128)(2,1)S(1)} %copy.53) | copy-start | bytes 3145732
  746.0 3.6 copy-start.8
  746.0 10.1 %slice-start.2 = ((s8[4718592]{0:T(1024)(128)(4,1)}), s8[4194304]{0:T(1024)(128)(4,1)S(1)}, s32[]{:S(2)}) async-start(s8[4718592]{0:T(1024)(128)(4,1)} %bitcast.145), calls=%async_computation.8 | async-start | bytes 8388608
  746.1 10.1 %copy-start.29 = (bf16[1024,256]{1,0:T(8,128)(2,1)}, bf16[1024,256]{1,0:T(8,128)(2,1)S(1)}, u32[]{:S(2)}) copy-start(bf16[1024,256]{1,0:T(8,128)(2,1)S(1)} %convert.66) | copy-start | bytes 1572868
  749.6 6.5 copy-start.31
  749.7 6.5 slice-start.3
  766.7 10.5 %copy-start.27 = (bf16[128,8,2,256]{3,1,2,0:T(8,128)(2,1)S(1)}, bf16[128,8,2,256]{3,1,2,0:T(8,128)(2,1)}, u32[]{:S(2)}) copy-start(bf16[128,8,2,256]{3,1,2,0:T(8,128)(2,1)} %copy-done.26) | copy-start | bytes 3145732
  766.7 10.5 %copy-start.30 = (bf16[1024,256]{1,0:T(8,128)(2,1)S(1)}, bf16[1024,256]{1,0:T(8,128)(2,1)}, u32[]{:S(2)}) copy-start(bf16[1024,256]{1,0:T(8,128)(2,1)} %copy-done.29) | copy-start | bytes 1572868
  766.7 10.5 %copy-start.32 = (bf16[1024,256]{1,0:T(8,128)(2,1)S(1)}, bf16[1024,256]{1,0:T(8,128)(2,1)}, u32[]{:S(2)}) copy-start(bf16[1024,256]{1,0:T(8,128)(2,1)} %copy-done.31) | copy-start | bytes 1572868
  787.4 5.0 slice-start
  787.4 5.0 slice-start.1
  878.7 1.3 copy-start.17
  878.7 1.3 copy-start.35
  880.8 2.3 copy-start.15
  881.0 4.2 copy-start.36
Sparse Core Ops, SparseCore 0:
  9.9 109.9 all-gather.4
  121.7 149.3 all-gather.2
  601.3 83.6 reduce-scatter.4
  687.9 142.2 reduce-scatter.2

commit v4 on v3

--- a/solution.py
+++ b/solution.py
@@ -611,6 +611,40 @@
     )(queries, keys, values, segment_col, segment_row, grads)
 
 
+def unit_orders(n):
+    units, sums = [], []
+    for s in range(n):
+        keyed = []
+        for d in range(n):
+            if d != s:
+                near = abs(s - d)
+                behind, past = (s, d) if d < s else (n - 1 - s, n - 1 - d)
+                keyed += [(near, d, 0), (behind + past + 1, d, 1)]
+        order = [(s, 0), (s, 1)] + [(d, h) for unused, d, h in sorted(keyed)]
+        units.append([2 * d + h for d, h in order])
+        if s in (0, n - 1):
+            sums.append(units[-1][2:])
+            continue
+        keyed = []
+        for d in range(n):
+            if d != s:
+                hops, place = (n - 2 - s, d) if d < s else (s - 1, n - 1 - d)
+                keyed += [(n - 2 - place + hops, d, 0), (n - 1 + place + hops, d, 1)]
+        sums.append([2 * d + h for unused, d, h in sorted(keyed)])
+    return units, sums
+
+
+def pick(table, s, i):
+    width = len(table[0])
+    place = s * width + i
+    value = 0
+    for k, entry in enumerate(entry for row in table for entry in row):
+        value = jnp.where(place == k, entry, value)
+    return value
+
+
+SUBS = 1
+SUM_TURNS = (0, 1, 5, 6, 11, 12)
 GELU_SCALE = math.sqrt(2.0 / math.pi)
 
 
@@ -625,10 +659,10 @@
 
 def units_kernel(n_seq, backward, *refs):
     if backward:
-        tokens, units, downs, kept_gate, kept_up = refs[:5]
-        out, tokens_all, first_out, second_out = refs[5:9]
+        tokens, units, downs, kept_gate, kept_up, kept_hidden, inputs = refs[:7]
+        out, first_out, second_out, unit_grads, down_grads = refs[7:12]
         stage_outs = (first_out, second_out)
-        scratch = refs[9:]
+        scratch = refs[12:]
     else:
         tokens, units, downs = refs[:3]
         out, tokens_all, first_out, second_out, third_out = refs[3:8]
@@ -637,8 +671,8 @@
     units_v, downs_v, held, own_sum, twin_sum, twin_out, line, stage = scratch[:8]
     scratch = scratch[8:]
     if backward:
-        kept, kept_sem = scratch[:2]
-        scratch = scratch[2:]
+        kept, kept_sem, tile, tile_sem, load_sem, rows_sem = scratch[:6]
+        scratch = scratch[6:]
     (
         weight_sem,
         own_sem,
@@ -681,23 +715,27 @@
             twin_out.at[d, h], twin_sum.at[d, h], part_send.at[d, h], part_recv.at[d, h], twin
         )
 
-    def part_line(d, h):
+    sub_len = piece_len // SUBS
+
+    def part_line(d, h, sub):
         to_left = d < s
         slot = jnp.where(to_left, d, d + 1)
+        rows = pl.ds(sub * sub_len, sub_len)
         return remote(
-            twin_sum.at[d, h],
-            line.at[slot, h],
-            line_send.at[d, h],
-            line_recv.at[slot, h],
+            twin_sum.at[d, h, rows],
+            line.at[slot, h, rows],
+            line_send.at[d, h, sub],
+            line_recv.at[slot, h, sub],
             {"seq": jnp.where(to_left, s - 1, s + 1)},
         )
 
-    def line_arrival(slot, h):
+    def line_arrival(slot, h, sub):
+        rows = pl.ds(sub * sub_len, sub_len)
         return remote(
-            twin_sum.at[0, h],
-            line.at[slot, h],
-            line_send.at[0, h],
-            line_recv.at[slot, h],
+            twin_sum.at[0, h, rows],
+            line.at[slot, h, rows],
+            line_send.at[0, h, sub],
+            line_recv.at[slot, h, sub],
             {"seq": s},
         )
 
@@ -716,13 +754,17 @@
         source = (kept_gate, kept_up)[i]
         return pltpu.make_async_copy(source.at[2 * d + h], kept.at[i, slot], kept_sem.at[i, slot])
 
-    def source(p):
-        inner = jnp.minimum(s, n - 1 - s)
-        near = lax.div(p + 1, 2)
-        paired = jnp.where(lax.rem(p, 2) == 1, s - near, s + near)
-        far = p - inner
-        single = jnp.where(s < n - 1 - s, s + far, s - far)
-        return jnp.where(p <= 2 * inner, paired, single)
+    unit_table, sum_table = unit_orders(n)
+    right_table = [
+        [2 if d == 0 else unit_table[d].index(2 * (d - 1) + 1) + 1 for d in range(n)]
+    ]
+    left_table = [
+        [2 if d == n - 1 else unit_table[d].index(2 * (d + 1) + 1) + 1 for d in range(n)]
+    ]
+
+    def source(t):
+        unit = pick(unit_table, s, t)
+        return lax.div(unit, 2), lax.rem(unit, 2)
 
     barrier = pltpu.get_barrier_semaphore()
     pl.semaphore_signal(barrier, inc=1, device_id=twin, device_id_type=MESH)
@@ -737,16 +779,28 @@
 
     pl.semaphore_wait(barrier, 1 + jnp.where(s > 0, 1, 0) + jnp.where(s < n - 1, 1, 0))
 
+    def second_half(t):
+        @pl.when((s < n - 1) & (t == pick(right_table, 0, s)))
+        def _():
+            d, h = jnp.maximum(s - 1, 0), jnp.where(s > 0, 1, 0)
+            token_right(d, h, held.at[d, h, 0]).wait_send()
+            token_right(s, 1, tokens.at[1]).start()
+
+        @pl.when((s > 0) & (t == pick(left_table, 0, s)))
+        def _():
+            d, h = jnp.minimum(s + 1, n - 1), jnp.where(s < n - 1, 1, 0)
+            token_left(d, h, held.at[d, h, 0]).wait_send()
+            token_left(s, 1, tokens.at[1]).start()
+
+    @pl.when(s < n - 1)
+    def _():
+        token_right(s, 0, tokens.at[0]).start()
+
+    @pl.when(s > 0)
+    def _():
+        token_left(s, 0, tokens.at[0]).start()
+
     for h in range(2):
-
-        @pl.when(s < n - 1)
-        def _():
-            token_right(s, h, tokens.at[h]).start()
-
-        @pl.when(s > 0)
-        def _():
-            token_left(s, h, tokens.at[h]).start()
-
         token_twin(s, h, tokens.at[h]).start()
         own_load(h).start()
     load_units = pltpu.make_async_copy(units, units_v, weight_sem.at[0])
@@ -759,11 +813,11 @@
     load_units.wait()
     load_downs.wait()
 
-    def add_rows(d, h, into_own, use_line):
+    def add_rows(d, h, sub, into_own, use_line):
         step = 16
 
         def body(i, carry):
-            rows = pl.ds(pl.multiple_of(i * step, step), step)
+            rows = pl.ds(pl.multiple_of(sub * sub_len + i * step, step), step)
             total = own_sum[d, h, rows, :] + twin_sum[d, h, rows, :].astype(jnp.float32)
             for slot in use_line:
                 total = total + line[slot, h, rows, :].astype(jnp.float32)
@@ -773,7 +827,7 @@
                 twin_sum[d, h, rows, :] = total.astype(twin_sum.dtype)
             return carry
 
-        lax.fori_loop(0, piece_len // step, body, 0)
+        lax.fori_loop(0, sub_len // step, body, 0)
 
     def combine(d, h):
         to_left = d < s
@@ -783,14 +837,16 @@
 
         @pl.when(more)
         def _():
-            line_arrival(slot, h).wait_recv()
-            add_rows(d, h, False, (slot,))
+            for sub in range(SUBS):
+                line_arrival(slot, h, sub).wait_recv()
+                add_rows(d, h, sub, False, (slot,))
+                part_line(d, h, sub).start()
 
         @pl.when(jnp.logical_not(more))
         def _():
-            add_rows(d, h, False, ())
-
-        part_line(d, h).start()
+            for sub in range(SUBS):
+                add_rows(d, h, sub, False, ())
+                part_line(d, h, sub).start()
 
     columns = width // 3
     chunk = n_units // 3
@@ -828,10 +884,118 @@
             own_sum[d, h, :, cols] = part[:piece_len]
             twin_out[d, h, :, cols] = part[piece_len:].astype(twin_out.dtype)
 
+    row_tile, col_tile = n_units // 3, width // 3
+
+    def weight_gradients(between):
+        unit_rows = 2 * piece_len
+
+        def left_load(i, u):
+            source = (kept_hidden, first_out, second_out)[i].at[u]
+            if i == 1:
+                place = kept.at[u // 2, u % 2] if u < n else stage.at[(u - n) // 2, u % 2]
+            else:
+                place = downs_v.at[
+                    pl.ds((u % n) * unit_rows, unit_rows), pl.ds((u // n) * n_units, n_units)
+                ]
+            return pltpu.make_async_copy(source, place, load_sem.at[i, u])
+
+        def input_load(u):
+            place = units_v.at[
+                pl.ds((u % n) * unit_rows, unit_rows), pl.ds((u // n) * width, width)
+            ]
+            source = inputs.at[u // 2, u % 2]
+            return [
+                pltpu.make_async_copy(
+                    source.at[half],
+                    place.at[pl.ds(half * piece_len, piece_len)],
+                    rows_sem.at[u, half],
+                )
+                for half in range(2)
+            ]
+
+        def left_rows(i, u, cols):
+            if i == 1:
+                return kept[u // 2, u % 2, :, cols] if u < n else stage[(u - n) // 2, u % 2, :, cols]
+            return downs_v[
+                (u % n) * unit_rows : (u % n + 1) * unit_rows,
+                pl.ds(pl.multiple_of((u // n) * n_units + cols.start, 128), row_tile),
+            ]
+
+        def right_rows(i, u, cols):
+            if i == 0:
+                return held[u // 2, u % 2, :, :, cols].reshape(unit_rows, col_tile)
+            return units_v[
+                (u % n) * unit_rows : (u % n + 1) * unit_rows,
+                pl.ds(pl.multiple_of((u // n) * width + cols.start, 128), col_tile),
+            ]
+
+        def tile_store(i, r, c, slot):
+            rows = pl.ds(pl.multiple_of(r * row_tile, 16), row_tile)
+            if i == 0:
+                cols = pl.ds(pl.multiple_of(c * col_tile, 128), col_tile)
+                place = down_grads.at[rows, cols]
+            else:
+                cols = pl.ds(pl.multiple_of((i - 1) * width + c * col_tile, 128), col_tile)
+                place = unit_grads.at[rows, cols]
+            return pltpu.make_async_copy(tile.at[slot], place, tile_sem.at[slot])
+
+        for u in range(2 * n):
+            left_load(0, u).start()
+        for h in range(2):
+            for i in range(2):
+                stage_store(i, 0, h, h).wait()
+        for u in range(2 * n):
+            for load in input_load(u):
+                load.start()
+            left_load(1, u).start()
+        for i in range(3):
+            for u in range(2 * n):
+                left_load(i, u).wait()
+            if i == 1:
+                for u in range(2 * n):
+                    for load in input_load(u):
+                        load.wait()
+                for u in range(2 * n):
+                    left_load(2, u).start()
+
+            def one_tile(j, carry, i=i):
+                count = 9 * i + j
+                slot = lax.rem(count, 2)
+                r, c = lax.div(j, 3), lax.rem(j, 3)
+                row_cols = pl.ds(pl.multiple_of(r * row_tile, 128), row_tile)
+                col_cols = pl.ds(pl.multiple_of(c * col_tile, 128), col_tile)
+                total = jnp.zeros((row_tile, col_tile), jnp.float32)
+                for u in range(2 * n):
+                    total = total + outer_rows(
+                        left_rows(i, u, row_cols), right_rows(i, u, col_cols)
+                    )
+
+                @pl.when(count >= 2)
+                def _():
+                    tile_store(i, r, c, slot).wait()
+
+                tile[slot] = total.astype(tile.dtype)
+                tile_store(i, r, c, slot).start()
+
+                for step, turn in enumerate(SUM_TURNS):
+
+                    @pl.when(count == turn)
+                    def _():
+                        between(step)
+
+                return carry
+
+            lax.fori_loop(0, 9, one_tile, 0)
+        for slot in range(2):
+            tile_store(0, 0, 0, slot).wait()
+
     def unit(t, carry):
-        d = source(lax.div(t, 2))
-        h = lax.rem(t, 2)
+        d, h = source(t)
         slot = lax.rem(t, 2)
+
+        @pl.when(at_end & (t >= 3))
+        def _():
+            combine(*source(t - 1))
 
         @pl.when(t < 2)
         def _():
@@ -854,14 +1018,13 @@
             for i in range(len(stage_outs)):
                 stage_store(i, d, h, slot).wait()
 
+        second_half(t)
         if backward:
 
             @pl.when(t < 2 * n - 1)
             def _():
                 for i in range(2):
-                    kept_load(
-                        i, source(lax.div(t + 1, 2)), lax.rem(t + 1, 2), 1 - slot
-                    ).start()
+                    kept_load(i, *source(t + 1), 1 - slot).start()
 
             for i in range(2):
                 kept_load(i, d, h, slot).wait()
@@ -871,62 +1034,62 @@
         else:
             compute_forward(d, h, slot)
         part_twin(d, h).start()
-        all_store(d, h).start()
+        if not backward:
+            all_store(d, h).start()
         for i in range(len(stage_outs)):
             stage_store(i, d, h, slot).start()
 
-        @pl.when(at_end & (t >= 3))
-        def _():
-            combine(source(lax.div(t - 1, 2)), lax.rem(t - 1, 2))
-
         return carry
 
     lax.fori_loop(0, 2 * n, unit, 0)
+
+    second_half(2 * n)
 
     @pl.when(at_end)
     def _():
-        combine(source(n - 1), 1)
-
-    @pl.when(jnp.logical_not(at_end))
-    def _():
-        right_first = 2 * s < n - 1
-
-        def middle(i, carry):
-            h = lax.rem(i, 2)
-            j = lax.rem(lax.div(i, 2), n - 1) + 1
-            to_right = jnp.where(i < 2 * (n - 1), right_first, jnp.logical_not(right_first))
-            d = jnp.where(to_right, s + j, s - j)
-
-            @pl.when((d >= 0) & (d <= n - 1))
-            def _():
-                combine(d, h)
-
+        combine(*source(2 * n - 1))
+
+    n_sums = 2 * (n - 1)
+
+    def middle(i):
+        @pl.when(jnp.logical_not(at_end) & (i < n_sums))
+        def _():
+            unit = pick(sum_table, s, i)
+            combine(lax.div(unit, 2), lax.rem(unit, 2))
+
+    if backward:
+        weight_gradients(middle)
+    else:
+
+        def one(i, carry):
+            middle(i)
             return carry
 
-        lax.fori_loop(0, 4 * (n - 1), middle, 0)
+        lax.fori_loop(0, n_sums, one, 0)
 
     def finish(h, carry):
         part_twin(s, h).wait_recv()
-
-        @pl.when(s < n - 1)
-        def _():
-            line_arrival(s, h).wait_recv()
-
-        @pl.when(s > 0)
-        def _():
-            line_arrival(s + 1, h).wait_recv()
-
-        @pl.when(s == 0)
-        def _():
-            add_rows(s, h, True, (s,))
-
-        @pl.when(s == n - 1)
-        def _():
-            add_rows(s, h, True, (s + 1,))
-
-        @pl.when(jnp.logical_not(at_end))
-        def _():
-            add_rows(s, h, True, (s, s + 1))
+        for sub in range(SUBS):
+
+            @pl.when(s < n - 1)
+            def _():
+                line_arrival(s, h, sub).wait_recv()
+
+            @pl.when(s > 0)
+            def _():
+                line_arrival(s + 1, h, sub).wait_recv()
+
+            @pl.when(s == 0)
+            def _():
+                add_rows(s, h, sub, True, (s,))
+
+            @pl.when(s == n - 1)
+            def _():
+                add_rows(s, h, sub, True, (s + 1,))
+
+            @pl.when(jnp.logical_not(at_end))
+            def _():
+                add_rows(s, h, sub, True, (s, s + 1))
 
         pltpu.make_async_copy(own_sum.at[s, h], out.at[h], out_sem.at[h]).start()
         return carry
@@ -938,11 +1101,14 @@
         h = lax.rem(t, 2)
         piece = held.at[d, h, 0]
 
-        @pl.when((d <= s) & (s < n - 1))
+        right_seen = (d == jnp.maximum(s - 1, 0)) & (h == jnp.where(s > 0, 1, 0))
+        left_seen = (d == jnp.minimum(s + 1, n - 1)) & (h == jnp.where(s < n - 1, 1, 0))
+
+        @pl.when((d <= s) & (s < n - 1) & jnp.logical_not(right_seen))
         def _():
             token_right(d, h, piece).wait_send()
 
-        @pl.when((d >= s) & (s > 0))
+        @pl.when((d >= s) & (s > 0) & jnp.logical_not(left_seen))
         def _():
             token_left(d, h, piece).wait_send()
 
@@ -951,15 +1117,18 @@
 
         @pl.when(d != s)
         def _():
-            part_line(d, h).wait_send()
-
-        all_store(d, h).wait()
+            for sub in range(SUBS):
+                part_line(d, h, sub).wait_send()
+
+        if not backward:
+            all_store(d, h).wait()
         return carry
 
     lax.fori_loop(0, 2 * n, drain, 0)
     for h in range(2):
-        for i in range(len(stage_outs)):
-            stage_store(i, 0, h, h).wait()
+        if not backward:
+            for i in range(len(stage_outs)):
+                stage_store(i, 0, h, h).wait()
         pltpu.make_async_copy(own_sum.at[s, h], out.at[h], out_sem.at[h]).wait()
 
 
@@ -982,26 +1151,36 @@
         pltpu.VMEM((n_seq + 1,) + sums[1:], low),
         pltpu.VMEM((n_stage, 2) + unit_rows[1:], low),
     ]
+    outs = [jax.ShapeDtypeStruct(tokens.shape, jnp.float32)]
     if backward:
-        scratch += [pltpu.VMEM((2, 2) + unit_rows[1:], low), DMA((2, 2))]
+        scratch += [
+            pltpu.VMEM((2, 2) + unit_rows[1:], low),
+            DMA((2, 2)),
+            pltpu.VMEM((2, n_units // 3, width // 3), low),
+            DMA((2,)),
+            DMA((3, 2 * n_seq)),
+            DMA((2 * n_seq, 2)),
+        ]
+    else:
+        outs += [jax.ShapeDtypeStruct(held, low)]
+    outs += [jax.ShapeDtypeStruct(unit_rows, low)] * n_stage
+    if backward:
+        outs += [jax.ShapeDtypeStruct(units.shape, low), jax.ShapeDtypeStruct(downs.shape, low)]
     pairs = DMA((n_seq, halves))
-    scratch += [DMA((2,)), DMA((halves,))] + [pairs] * 8
-    scratch += [DMA((n_seq + 1, halves)), DMA((n_stage, 2)), pairs, DMA((halves,))]
+    scratch += [DMA((2,)), DMA((halves,))] + [pairs] * 7
+    scratch += [DMA((n_seq, halves, SUBS)), DMA((n_seq + 1, halves, SUBS))]
+    scratch += [DMA((n_stage, 2)), pairs, DMA((halves,))]
     operands = (tokens, units, downs) + (tuple(kept) if backward else ())
     return pl.pallas_call(
         partial(units_kernel, n_seq, backward),
-        out_shape=[
-            jax.ShapeDtypeStruct(tokens.shape, jnp.float32),
-            jax.ShapeDtypeStruct(held, low),
-        ]
-        + [jax.ShapeDtypeStruct(unit_rows, low)] * n_stage,
+        out_shape=outs,
         in_specs=[ANY] * len(operands),
-        out_specs=[ANY] * (2 + n_stage),
+        out_specs=[ANY] * len(outs),
         scratch_shapes=scratch,
         compiler_params=pltpu.CompilerParams(
             collective_id=6 if backward else 5,
             has_side_effects=True,
-            vmem_limit_bytes=62 * 1024 * 1024,
+            vmem_limit_bytes=63 * 1024 * 1024,
         ),
     )(*operands)
 
@@ -1324,28 +1503,14 @@
     cotangent = output_cotangent.reshape(row_count, model_width).astype(jnp.float32)
     unused_last, pull_last = jax.vjp(rms_norm, down_out, gain_cols[:, 3])
     grad_down, grad_gain_last = pull_last(cotangent)
-    grad_ffn_in, grad_down_all, gate_low, up_low = run_units(
+    grad_ffn_in, unused_gate, unused_up, gate_up_rows, down_rows = run_units(
         n_seq,
         grad_down.astype(jnp.bfloat16).reshape(pieces),
         unit_weights,
         down_units,
-        (gate_part, up_part),
+        (gate_part, up_part, hidden_part, ffn_all),
     )
     grad_ffn_in = grad_ffn_in.reshape(row_count, model_width)
-    ffn_all = ffn_all.reshape(-1, model_width)
-    grad_down_all = grad_down_all.reshape(-1, model_width)
-    n_units = down_units.shape[0]
-    gate_low, up_low, hidden_part = (
-        array.reshape(-1, n_units) for array in (gate_low, up_low, hidden_part)
-    )
-    gate_up_rows = jnp.concatenate(
-        [
-            outer_rows(gate_low, ffn_all).astype(jnp.bfloat16),
-            outer_rows(up_low, ffn_all).astype(jnp.bfloat16),
-        ],
-        axis=1,
-    )
-    down_rows = outer_rows(hidden_part, grad_down_all).astype(jnp.bfloat16)
     gate_up_grad = lax.psum_scatter(
         gate_up_rows, "chip", scatter_dimension=0, tiled=True
     ).astype(jnp.float32)
@@ -1451,7 +1616,7 @@
 
     def step(*arrays):
         groups = arrays[0].shape[0]
-        if n_ctx // 2 == KV_HEADS and groups == 2:
+        if n_ctx // 2 == KV_HEADS and groups == 2 and n_seq == 4:
             return per_device_by_heads(n_seq, *arrays)
         return per_device_general(*arrays)
 

time: 909 us -> 863 us (0.949)
  matrix products: 85.5 us -> 37.7 us
  waiting for transfers between devices: 19.7 us -> 30.6 us
    dot_general x5 -> x2, matrix products: 57.6 us -> 9.47 us  [outer_rows(): lax.dot_general(left, right, (((0,), (0,)), ((), ())), preferred_element_...]
    pallas_call x1, Pallas kernels: 85.6 us -> 96.9 us  [sum_last(): pl.pallas_call(partial(last_kernel, n_seq, n_plane), out_shape=[jax.Shape...]
    pallas_call x2, Pallas kernels: 305 us -> 294 us  [run_units(): pl.pallas_call(partial(units_kernel, n_seq, backward), out_shape=outs, in...]
    reduce_scatter x1, waiting for transfers between devices: 0.01 us -> 9.96 us  [per_device_by_heads(): lax.psum_scatter(gate_up_rows, 'chip', scatter_dimension=0, tiled=True)]
  transfers between devices with their start and end apart: 4 -> 4, of which waited for: 1 -> 2; matrix products, arithmetic and copies ran while one was open for 18% -> 15% of each run, Pallas kernels for 39% -> 42%
where the time goes in v4:
time: 863 us; the launch traced here: 854 us
  Pallas kernels  655 us (76%)
  other arithmetic  69.1 us (8%)
  local copies, waits for them, and re-layouts  46.1 us (5%)
  matrix products  37.7 us (4%)
  waiting for transfers between devices  30.6 us (4%)
  between operations  15 us (2%)
    pallas_call x2, Pallas kernels, run_units(): pl.pallas_call(partial(units_kernel, n_seq, backward), out_shape=outs, in...  294 us
    pallas_call x2, Pallas kernels, plane_exchange(): pl.pallas_call(partial(exchange_kernel, n_plane, by_core), out_shape=jax....  159 us
    pallas_call x1, Pallas kernels, sum_last(): pl.pallas_call(partial(last_kernel, n_seq, n_plane), out_shape=[jax.Shape...  96.9 us
    pallas_call x1, Pallas kernels, gather_first(): pl.pallas_call(partial(gather_kernel, n_seq, n_plane), out_shape=[jax.Sha...  94.4 us
    unnamed x111, local copies, waits for them, and re-layouts  19.4 us
    all_gather x1, waiting for transfers between devices, per_device_by_heads(): unit_weights = lax.all_gather(gate_up_weight, 'chip', axis=0, tiled=True)  18.9 us
  transfers between devices with their start and end apart: 4, of which 2 were waited for; matrix products, arithmetic and copies ran while one was open for 15% of the time, Pallas kernels for 42%

profile of v4, /device:TPU:0, one launch (start us, length us, event | category | flops | bytes accessed | tf_op | source)
XLA Modules:
  0.0 854.1 jit_solution(10982053649757714099)
XLA Ops:
  7.2 0.7 all-gather.5.cloned.1.call-update
  8.0 0.7 all-gather.3.cloned.1.call-update
  8.9 1.1 pad_maximum_fusion.4.blocks
  10.0 94.4 %shard_map.144 = (bf16[8,128,2304]{2,1,0:T(8,128)(2,1)}, bf16[4,2,4,80,1536]{4,3,2,1,0:T(8,128)(2,1)}) custom-call(bf16[2,128,2304]{2,1,0:T(8,128)(2,1)} %hidden.1, bf16[4,80,1536]{2,1,0:T(8,128)(2,1)} %pad_maximum_fusion.4.blocks), custom_call_target="tpu_custom_call" | custom-call | tf_op jit(solution)/shard_map/pallas_call | solution.py:323
  104.4 3.7 slice.219
  108.1 3.9 copy.35
  112.0 0.8 convert_bitcast_fusion
  113.1 3.5 fusion.1
  116.9 1.1 fusion.3
  118.0 3.6 copy-done.23
  121.6 5.4 fusion.10
  127.2 1.5 slice.221
  129.1 1.3 copy.50
  130.4 3.0 fusion.72
  133.4 2.7 copy.49
  136.1 1.3 copy.48
  137.4 0.8 select_reduce_fusion
  138.2 1.9 multiply_cosine_fusion.1
  140.1 2.7 subtract_convert_fusion.1
  142.9 1.1 pad_maximum_fusion.2
  144.3 2.4 fusion.45
  146.7 3.7 shard_map.145
  150.5 6.8 convolution_convert_fusion
  157.3 86.0 %shard_map.146 = bf16[8,128,2304]{2,1,0:T(8,128)(2,1)} custom-call(bf16[8,128,2304]{2,1,0:T(8,128)(2,1)} %bitcast.138), custom_call_target="tpu_custom_call" | custom-call | tf_op jit(solution)/shard_map/pallas_call | solution.py:188
  243.3 3.4 convert_reduce_fusion.1
  246.9 1.9 copy-done.19
  248.8 0.6 multiply_reduce_fusion.5
  249.4 1.4 copy-done.14
  250.8 1.3 multiply_convert_fusion.refs_0_
  252.1 18.9 %all-gather.3.cloned.1.call-done.refs_1_ = bf16[1152,4608]{1,0:T(8,128)(2,1)} async-done(((bf16[288,4608]{1,0:T(8,128)(2,1)}), bf16[1152,4608]{1,0:T(8,128)(2,1)}) %all-gather.3.cloned.1.call-update) | async-done | bytes 10616848 | tf_op jit(solution)/shard_map/all_gather | solution.py:1439
  271.1 131.6 %shard_map.147 = (f32[2,128,2304]{2,1,0:T(8,128)}, bf16[4,2,2,128,2304]{4,3,2,1,0:T(8,128)(2,1)}, bf16[8,256,1152]{2,1,0:T(8,128)(2,1)}, bf16[8,256,1152]{2,1,0:T(8,128)(2,1)}, bf16[8,256,1152]{2,1,0:T(8,128)(2,1)}) custom-call(bf16[2,128,2304]{2,1,0:T(8,128)(2,1)} %multiply_convert_fusion.refs_0_, bf16[1152,4608]{1,0:T(8,128)(2,1)} %all-gather.3.cloned.1.call-done.refs_1_, ...), custom_call_target="tpu_custom_call" | custom-call | tf_op jit(solution)/shard_map/pallas_call | solution.py:1174
  402.7 2.1 multiply_reduce_fusion.4
  405.1 2.3 fusion.15
  407.4 3.3 fusion.16
  410.7 162.6 %shard_map.148 = (f32[2,128,2304]{2,1,0:T(8,128)}, bf16[8,256,1152]{2,1,0:T(8,128)(2,1)}, bf16[8,256,1152]{2,1,0:T(8,128)(2,1)}, bf16[1152,4608]{1,0:T(8,128)(2,1)}, bf16[1152,2304]{1,0:T(8,128)(2,1)}) custom-call(bf16[2,128,2304]{2,1,0:T(8,128)(2,1)} %get-tuple-element.60.refs_0_, bf16[1152,4608]{1,0:T(8,128)(2,1)} %all-gather.3.cloned.1.call-done.refs_1_, ...), custom_call_target="tpu_custom_call" | custom-call | tf_op jit(solution)/shard_map/pallas_call | solution.py:1174
  574.0 3.1 multiply_reduce_fusion
  577.1 1.2 copy-done.16
  578.3 4.7 multiply_reduce_fusion.1
  583.3 3.3 fusion.17.source
  586.6 72.6 %shard_map.149 = bf16[8,128,2304]{2,1,0:T(8,128)(2,1)} custom-call(bf16[2,128,2304]{2,1,0:T(8,128)(2,1)} %fusion.17.source), custom_call_target="tpu_custom_call" | custom-call | tf_op jit(solution)/shard_map/pallas_call | solution.py:188
  659.3 5.8 fusion.24.grads
  665.1 7.5 shard_map.150
  672.6 1.0 copy-done.6
  673.6 1.0 copy-done.8
  674.6 2.7 reshape.562
  677.3 2.5 add_convert_fusion.1
  679.8 1.1 pad_maximum_fusion.3
  681.3 1.0 copy-done.9
  682.3 2.3 fusion.40
  684.7 3.9 convolution_convert_fusion.2
  688.7 5.6 convolution_convert_fusion.1
  694.2 5.0 pad_maximum_fusion
  699.2 10.6 %copy.42 = bf16[2304,1536]{1,0:T(8,128)(2,1)} copy(bf16[2304,1536]{0,1:T(8,128)(2,1)} %pad_maximum_fusion) | data formatting | bytes 14155776 | tf_op jit(solution)/shard_map/concatenate | solution.py:1546
  709.8 10.3 %fusion.5 = (bf16[2304]{0:T(1024)(128)(2,1)S(1)}, bf16[1024,2304]{1,0:T(8,128)(2,1)}) fusion(bf16[8,128,2304]{2,1,0:T(8,128)(2,1)} %get-tuple-element.22, f32[1024]{0:T(1024)S(1)} %rsqrt_bitcast_fusion, bf16[2304,1536]{1,0:T(8,128)(2,1)} %bitcast.130, bf16[1024,256]{1,0:T(8,128)(2,1)S(1)} %copy-done.35, bf16[1024,256]{1,0:T(8,128)(2,1)S(1)} %copy-done.37, ...), kind=kOutput, calls=%fused_computation.11 | convolution fusion | flops 4849924096 | bytes 16261632 | tf_op jit(solution)/shard_map/dot_general | solution.py:99
  720.4 5.2 fusion.7.blocks
  725.6 96.9 %shard_map.151 = (bf16[8,128,2304]{2,1,0:T(8,128)(2,1)S(1)}, bf16[4,80,1536]{2,1,0:T(8,128)(2,1)S(1)}) custom-call(bf16[8,128,2304]{2,1,0:T(8,128)(2,1)S(1)} %bitcast.122, bf16[4,2,4,80,1536]{4,3,2,1,0:T(8,128)(2,1)S(1)} %fusion.7.blocks), custom_call_target="tpu_custom_call" | custom-call | tf_op jit(solution)/shard_map/pallas_call | solution.py:496
  823.1 0.8 convert_reduce_fusion
  824.4 0.6 fusion.19
  825.5 0.9 pad_maximum_fusion.7
  826.4 1.2 copy-done.18
  827.6 2.1 fusion.18
  829.7 3.0 convert_element_type.151
  832.7 10.0 %reduce-scatter.3.cloned.1.call-done = bf16[288,4608]{1,0:T(8,128)(2,1)} async-done(((bf16[1152,4608]{1,0:T(8,128)(2,1)}), bf16[288,4608]{1,0:T(8,128)(2,1)}) %reduce-scatter.3.cloned.1.call-update) | async-done | bytes 2654224 | tf_op jit(solution)/shard_map/reduce_scatter | solution.py:1514
  842.6 4.8 convert_element_type.150
  (148 shorter events, 5.5 us)
Async XLA Ops:
  7.2 1.6 copy-start.33
  7.2 1.6 copy-start.38
  7.2 244.9 %all-gather.5.cloned.1.call-start = ((), (), s32[]{:S(2)}) async-start(), calls=%async_computation.3 | async-start | bytes 6635520 | tf_op jit(solution)/shard_map/all_gather | solution.py:1440
  7.9 0.9 copy-start.40
  7.9 263.1 %all-gather.3.cloned.1.call-start = ((), (), s32[]{:S(2)}) async-start(), calls=%async_computation.2 | async-start | bytes 13271040 | tf_op jit(solution)/shard_map/all_gather | solution.py:1439
  8.7 821.0 %reduce-scatter.5.cloned.1.call-start = ((), (), s32[]{:S(2)}) async-start(), calls=%async_computation.5 | async-start | bytes 6635520 | tf_op jit(solution)/shard_map/reduce_scatter | solution.py:1517
  113.1 3.8 copy-start.21
  116.9 4.7 copy-start.23
  118.0 8.9 %copy-start.24 = (bf16[1024,2304]{1,0:T(8,128)(2,1)}, bf16[1024,2304]{1,0:T(8,128)(2,1)S(1)}, u32[]{:S(2)}) copy-start(bf16[1024,2304]{1,0:T(8,128)(2,1)S(1)} %fusion.3) | copy-start | bytes 14155780
  127.2 1.5 copy-start.41
  127.2 1.5 copy-start.42
  129.1 17.6 %copy-start.2 = (bf16[1024,256]{1,0:T(8,128)(2,1)}, bf16[1024,256]{1,0:T(8,128)(2,1)S(1)}, u32[]{:S(2)}) copy-start(bf16[1024,256]{1,0:T(8,128)(2,1)S(1)} %copy.51.values) | copy-start | bytes 1572868
  140.1 3.9 copy-start.26
  140.1 3.9 copy-start.28
  142.8 1.4 copy-start.30
  144.2 6.2 copy-start
  146.7 10.6 %copy-start.4 = (bf16[1024,256]{1,0:T(8,128)(2,1)}, bf16[1024,256]{1,0:T(8,128)(2,1)S(1)}, u32[]{:S(2)}) copy-start(bf16[1024,256]{1,0:T(8,128)(2,1)S(1)} %pad_maximum_fusion.8.keys) | copy-start | bytes 1572868
  150.4 6.8 copy-start.10
  246.7 2.8 copy-start.12
  246.7 2.1 copy-start.19
  249.4 1.4 copy-start.14
  402.7 2.4 copy-start.17
  404.8 2.6 copy-start.15
  404.8 2.6 copy-start.22
  573.3 269.3 %reduce-scatter.3.cloned.1.call-start = ((), (), s32[]{:S(2)}) async-start(), calls=%async_computation.4 | async-start | bytes 13271040 | tf_op jit(solution)/shard_map/reduce_scatter | solution.py:1514
  574.0 3.1 copy-start.13
  574.0 4.4 copy-start.16
  659.2 5.9 copy-start.1
  659.2 5.9 copy-start.3
  659.3 5.9 copy-start.5
  672.6 1.0 copy-start.6
  673.6 1.0 copy-start.8
  674.5 2.7 copy-start.27
  674.6 2.7 copy-start.29
  677.3 7.4 copy-start.25
  679.8 1.4 copy-start.7
  680.9 1.3 copy-start.9
  681.2 7.5 copy-start.31
  681.2 3.5 copy-start.11
  681.3 7.4 copy-start.34
  682.3 6.4 slice-start.2
  684.7 3.9 copy-start.36
  684.7 4.0 slice-start.3
  699.2 10.6 %copy-start.32 = (bf16[128,8,2,256]{3,1,2,0:T(8,128)(2,1)S(1)}, bf16[128,8,2,256]{3,1,2,0:T(8,128)(2,1)}, u32[]{:S(2)}) copy-start(bf16[128,8,2,256]{3,1,2,0:T(8,128)(2,1)} %copy-done.31) | copy-start | bytes 3145732
  699.2 10.6 %copy-start.35 = (bf16[1024,256]{1,0:T(8,128)(2,1)S(1)}, bf16[1024,256]{1,0:T(8,128)(2,1)}, u32[]{:S(2)}) copy-start(bf16[1024,256]{1,0:T(8,128)(2,1)} %copy-done.34) | copy-start | bytes 1572868
  699.2 10.6 %copy-start.37 = (bf16[1024,256]{1,0:T(8,128)(2,1)S(1)}, bf16[1024,256]{1,0:T(8,128)(2,1)}, u32[]{:S(2)}) copy-start(bf16[1024,256]{1,0:T(8,128)(2,1)} %copy-done.36) | copy-start | bytes 1572868
  720.3 5.2 slice-start
  720.4 5.2 slice-start.1
  823.1 1.3 copy-start.20
  825.3 2.3 copy-start.18
  825.5 4.2 copy-start.39
Sparse Core Ops, SparseCore 0:
  9.9 109.9 all-gather.4
  121.7 149.3 all-gather.2
  573.4 109.5 reduce-scatter.4
  685.9 156.6 reduce-scatter.2

commit v5 on v4

--- a/solution.py
+++ b/solution.py
@@ -153,14 +153,13 @@
     pl.semaphore_wait(barrier, count)
 
 
-def start_exchange(n_plane, by_core, source, target, send_sems, recv_sems, local_sem):
+def start_exchange(n_plane, source, target, send_sems, recv_sems, local_sem):
     me = lax.axis_index("chip") * 2 + lax.axis_index("core")
     copies = []
     for step in (4, 2, 6, 3, 5, 1, 7):
         to = lax.rem(me + step, n_plane)
-        block = lax.rem(to, 2) if by_core else to
         copy = remote(
-            source.at[block],
+            source.at[to],
             target.at[me],
             send_sems.at[step],
             recv_sems.at[step],
@@ -168,25 +167,93 @@
         )
         copy.start()
         copies.append(copy)
-    block = lax.rem(me, 2) if by_core else me
-    own = pltpu.make_async_copy(source.at[block], target.at[me], local_sem.at[0])
+    own = pltpu.make_async_copy(source.at[me], target.at[me], local_sem.at[0])
     own.start()
     copies.append(own)
     return copies
 
 
-def exchange_kernel(n_plane, by_core, source, target, send_sems, recv_sems, local_sem):
+class Spread:
+    def __init__(self, source, target, send_sems, recv_sems, local_sem):
+        self.source, self.target = source, target
+        self.send_sems, self.recv_sems = send_sems, recv_sems
+        self.local_sem = local_sem
+        self.q = lax.axis_index("chip")
+        self.k = lax.axis_index("core")
+        self.half = source.shape[1] // 2
+
+    def chip(self, flip):
+        x, y = lax.rem(self.q, 2), self.q // 2
+        x = 1 - x if flip in (1, 3) else x
+        y = 1 - y if flip in (2, 3) else y
+        return y * 2 + x
+
+    def direct(self, flip, twin):
+        core = 1 - self.k if twin else self.k
+        slot = 2 * flip + twin
+        return remote(
+            self.source.at[core],
+            self.target.at[2 * self.q + self.k],
+            self.send_sems.at[slot],
+            self.recv_sems.at[slot],
+            {"chip": self.chip(flip), "core": core},
+        )
+
+    def passed(self, flip, twin):
+        core = 1 - self.k if twin else self.k
+        slot = 8 + 2 * (flip - 1) + twin
+        rows = pl.ds(0 if flip == 1 else self.half, self.half)
+        block = self.target.at[2 * self.chip(flip) + core, rows]
+        return remote(
+            block,
+            block,
+            self.send_sems.at[slot],
+            self.recv_sems.at[slot],
+            {"chip": self.chip(3 - flip)},
+        )
+
+    def own(self):
+        return pltpu.make_async_copy(
+            self.source.at[self.k],
+            self.target.at[2 * self.q + self.k],
+            self.local_sem.at[0],
+        )
+
+    def start(self):
+        for twin in (0, 1):
+            for flip in (1, 2):
+                self.direct(flip, twin).start()
+        self.direct(0, 1).start()
+        self.own().start()
+
+    def pass_on(self):
+        for twin in (0, 1):
+            for flip in (1, 2):
+                self.direct(flip, twin).wait_recv()
+                self.passed(flip, twin).start()
+
+    def finish(self):
+        for twin in (0, 1):
+            for flip in (1, 2):
+                self.passed(flip, twin).wait()
+                self.direct(flip, twin).wait_send()
+        self.direct(0, 1).wait()
+        self.own().wait()
+
+
+SPREAD_SLOTS = 12
+
+
+def exchange_kernel(n_plane, source, target, send_sems, recv_sems, local_sem):
     greet(n_plane, 1)
-    for copy in start_exchange(
-        n_plane, by_core, source, target, send_sems, recv_sems, local_sem
-    ):
+    for copy in start_exchange(n_plane, source, target, send_sems, recv_sems, local_sem):
         copy.wait()
 
 
-def plane_exchange(blocks, by_core, collective_id):
+def plane_exchange(blocks, collective_id):
     n_plane = 2 * KV_HEADS
     return pl.pallas_call(
-        partial(exchange_kernel, n_plane, by_core),
+        partial(exchange_kernel, n_plane),
         out_shape=jax.ShapeDtypeStruct((n_plane,) + blocks.shape[1:], blocks.dtype),
         in_specs=[ANY],
         out_specs=ANY,
@@ -195,6 +262,107 @@
             collective_id=collective_id, has_side_effects=True
         ),
     )(blocks)
+
+
+def spread_kernel(
+    n_plane,
+    blocks,
+    low_gate,
+    low_up,
+    tokens,
+    target,
+    grads,
+    left,
+    right,
+    tile,
+    send_sems,
+    recv_sems,
+    local_sem,
+    load_sem,
+    row_sem,
+    tile_sem,
+):
+    greet(n_plane, 1)
+    spread = Spread(blocks, target, send_sems, recv_sems, local_sem)
+    spread.start()
+    n_units, unit_rows, units = low_gate.shape
+    width = right.shape[1]
+    piece_len = tokens.shape[3]
+    loads = []
+    for i, source in enumerate((low_gate, low_up)):
+        for u in range(n_units):
+            place = left.at[i, pl.ds(u * unit_rows, unit_rows)]
+            loads.append(pltpu.make_async_copy(source.at[u], place, load_sem.at[i, u]))
+    for u in range(n_units):
+        for half in range(2):
+            place = right.at[pl.ds(u * unit_rows + half * piece_len, piece_len)]
+            source = tokens.at[u // 2, u % 2, half]
+            loads.append(pltpu.make_async_copy(source, place, row_sem.at[u, half]))
+    for load in loads:
+        load.start()
+    for load in loads:
+        load.wait()
+    row_tile, col_tile = units // 3, width // 3
+
+    def tile_store(i, r, c, slot):
+        rows = pl.ds(pl.multiple_of(r * row_tile, 16), row_tile)
+        cols = pl.ds(pl.multiple_of(i * width + c * col_tile, 128), col_tile)
+        return pltpu.make_async_copy(tile.at[slot], grads.at[rows, cols], tile_sem.at[slot])
+
+    def one_tile(j, carry):
+        i, slot = lax.div(j, 9), lax.rem(j, 2)
+        r, c = lax.div(lax.rem(j, 9), 3), lax.rem(j, 3)
+        rows = pl.ds(pl.multiple_of(r * row_tile, 128), row_tile)
+        cols = pl.ds(pl.multiple_of(c * col_tile, 128), col_tile)
+        total = outer_rows(left[i, :, rows], right[:, cols])
+
+        @pl.when(j >= 2)
+        def _():
+            tile_store(i, r, c, slot).wait()
+
+        tile[slot] = total.astype(tile.dtype)
+        tile_store(i, r, c, slot).start()
+        return carry
+
+    lax.fori_loop(0, PASS_TURN, one_tile, 0)
+    spread.pass_on()
+    lax.fori_loop(PASS_TURN, 18, one_tile, 0)
+    for slot in range(2):
+        tile_store(0, 0, 0, slot).wait()
+    spread.finish()
+
+
+PASS_TURN = 14
+
+
+def spread_plane(blocks, low_gate, low_up, tokens):
+    n_plane = 2 * KV_HEADS
+    low = blocks.dtype
+    n_units, unit_rows, units = low_gate.shape
+    width = blocks.shape[2]
+    return pl.pallas_call(
+        partial(spread_kernel, n_plane),
+        out_shape=[
+            jax.ShapeDtypeStruct((n_plane,) + blocks.shape[1:], low),
+            jax.ShapeDtypeStruct((units, 2 * width), low),
+        ],
+        in_specs=[ANY] * 4,
+        out_specs=[ANY, ANY],
+        scratch_shapes=[
+            pltpu.VMEM((2, n_units * unit_rows, units), low),
+            pltpu.VMEM((n_units * unit_rows, width), low),
+            pltpu.VMEM((2, units // 3, width // 3), low),
+            DMA((SPREAD_SLOTS,)),
+            DMA((SPREAD_SLOTS,)),
+            DMA((1,)),
+            DMA((2, n_units)),
+            DMA((n_units, 2)),
+            DMA((2,)),
+        ],
+        compiler_params=pltpu.CompilerParams(
+            collective_id=3, has_side_effects=True, vmem_limit_bytes=48 * 1024 * 1024
+        ),
+    )(blocks, low_gate, low_up, tokens)
 
 
 def gather_kernel(
@@ -235,12 +403,11 @@
         swaps.append(copy)
     own = pltpu.make_async_copy(blocks.at[q], blocks_all.at[s, k, q], chip_local.at[0])
     own.start()
-    hidden_copies = start_exchange(
-        n_plane, True, hidden, hidden_all, hid_send, hid_recv, hid_local
-    )
+    spread = Spread(hidden, hidden_all, hid_send, hid_recv, hid_local)
     for copy in swaps:
         copy.wait_recv()
     own.wait()
+    spread.start()
 
     def to_left(d):
         return remote(
@@ -276,6 +443,8 @@
 
     to_twin(s).start()
     for hop in range(1, n_seq):
+        if hop == 2:
+            spread.pass_on()
         from_left = s - hop
         from_right = s + hop
 
@@ -313,8 +482,7 @@
         from_twin(d).wait_recv()
     for copy in swaps:
         copy.wait_send()
-    for copy in hidden_copies:
-        copy.wait()
+    spread.finish()
 
 
 def gather_first(n_seq, hidden, blocks):
@@ -329,8 +497,8 @@
         in_specs=[ANY, ANY],
         out_specs=[ANY, ANY],
         scratch_shapes=[
-            DMA((n_plane,)),
-            DMA((n_plane,)),
+            DMA((SPREAD_SLOTS,)),
+            DMA((SPREAD_SLOTS,)),
             DMA((1,)),
             DMA((n_chip,)),
             DMA((n_chip,)),
@@ -442,9 +610,7 @@
     for d in range(n_seq):
         to_twin(d).start()
         load(d).start()
-    part_copies = start_exchange(
-        n_plane, False, parts, parts_all, part_send, part_recv, part_local
-    )
+    part_copies = start_exchange(n_plane, parts, parts_all, part_send, part_recv, part_local)
     never = s < 0
     for hop in range(1, n_seq):
         left = hop - n_seq + s
@@ -644,7 +810,7 @@
 
 
 SUBS = 1
-SUM_TURNS = (0, 1, 5, 6, 11, 12)
+SUM_TURNS = (0, 1, 4, 5, 8, 8)
 GELU_SCALE = math.sqrt(2.0 / math.pi)
 
 
@@ -659,10 +825,10 @@
 
 def units_kernel(n_seq, backward, *refs):
     if backward:
-        tokens, units, downs, kept_gate, kept_up, kept_hidden, inputs = refs[:7]
-        out, first_out, second_out, unit_grads, down_grads = refs[7:12]
+        tokens, units, downs, kept_gate, kept_up, kept_hidden = refs[:6]
+        out, first_out, second_out, down_grads = refs[6:10]
         stage_outs = (first_out, second_out)
-        scratch = refs[12:]
+        scratch = refs[10:]
     else:
         tokens, units, downs = refs[:3]
         out, tokens_all, first_out, second_out, third_out = refs[3:8]
@@ -671,8 +837,8 @@
     units_v, downs_v, held, own_sum, twin_sum, twin_out, line, stage = scratch[:8]
     scratch = scratch[8:]
     if backward:
-        kept, kept_sem, tile, tile_sem, load_sem, rows_sem = scratch[:6]
-        scratch = scratch[6:]
+        kept, kept_sem, tile, tile_sem, load_sem = scratch[:5]
+        scratch = scratch[5:]
     (
         weight_sem,
         own_sem,
@@ -886,108 +1052,61 @@
 
     row_tile, col_tile = n_units // 3, width // 3
 
-    def weight_gradients(between):
+    def down_gradient(between):
         unit_rows = 2 * piece_len
-
-        def left_load(i, u):
-            source = (kept_hidden, first_out, second_out)[i].at[u]
-            if i == 1:
-                place = kept.at[u // 2, u % 2] if u < n else stage.at[(u - n) // 2, u % 2]
-            else:
-                place = downs_v.at[
-                    pl.ds((u % n) * unit_rows, unit_rows), pl.ds((u // n) * n_units, n_units)
-                ]
-            return pltpu.make_async_copy(source, place, load_sem.at[i, u])
-
-        def input_load(u):
-            place = units_v.at[
-                pl.ds((u % n) * unit_rows, unit_rows), pl.ds((u // n) * width, width)
+        group_rows = n * unit_rows
+
+        def left_load(u):
+            place = downs_v.at[
+                pl.ds((u % n) * unit_rows, unit_rows), pl.ds((u // n) * n_units, n_units)
             ]
-            source = inputs.at[u // 2, u % 2]
-            return [
-                pltpu.make_async_copy(
-                    source.at[half],
-                    place.at[pl.ds(half * piece_len, piece_len)],
-                    rows_sem.at[u, half],
-                )
-                for half in range(2)
+            return pltpu.make_async_copy(kept_hidden.at[u], place, load_sem.at[u])
+
+        def left_rows(g, first):
+            return downs_v[
+                :group_rows, pl.ds(pl.multiple_of(g * n_units + first, 128), row_tile)
             ]
 
-        def left_rows(i, u, cols):
-            if i == 1:
-                return kept[u // 2, u % 2, :, cols] if u < n else stage[(u - n) // 2, u % 2, :, cols]
-            return downs_v[
-                (u % n) * unit_rows : (u % n + 1) * unit_rows,
-                pl.ds(pl.multiple_of((u // n) * n_units + cols.start, 128), row_tile),
-            ]
-
-        def right_rows(i, u, cols):
-            if i == 0:
-                return held[u // 2, u % 2, :, :, cols].reshape(unit_rows, col_tile)
-            return units_v[
-                (u % n) * unit_rows : (u % n + 1) * unit_rows,
-                pl.ds(pl.multiple_of((u // n) * width + cols.start, 128), col_tile),
-            ]
-
-        def tile_store(i, r, c, slot):
+        def right_rows(g, first):
+            cols = pl.ds(pl.multiple_of(first, 128), col_tile)
+            part = held[g * n // 2 : (g + 1) * n // 2, :, :, :, cols]
+            return part.reshape(group_rows, col_tile)
+
+        def tile_store(r, c, slot):
             rows = pl.ds(pl.multiple_of(r * row_tile, 16), row_tile)
-            if i == 0:
-                cols = pl.ds(pl.multiple_of(c * col_tile, 128), col_tile)
-                place = down_grads.at[rows, cols]
-            else:
-                cols = pl.ds(pl.multiple_of((i - 1) * width + c * col_tile, 128), col_tile)
-                place = unit_grads.at[rows, cols]
-            return pltpu.make_async_copy(tile.at[slot], place, tile_sem.at[slot])
+            cols = pl.ds(pl.multiple_of(c * col_tile, 128), col_tile)
+            return pltpu.make_async_copy(tile.at[slot], down_grads.at[rows, cols], tile_sem.at[slot])
 
         for u in range(2 * n):
-            left_load(0, u).start()
-        for h in range(2):
-            for i in range(2):
-                stage_store(i, 0, h, h).wait()
+            left_load(u).start()
         for u in range(2 * n):
-            for load in input_load(u):
-                load.start()
-            left_load(1, u).start()
-        for i in range(3):
-            for u in range(2 * n):
-                left_load(i, u).wait()
-            if i == 1:
-                for u in range(2 * n):
-                    for load in input_load(u):
-                        load.wait()
-                for u in range(2 * n):
-                    left_load(2, u).start()
-
-            def one_tile(j, carry, i=i):
-                count = 9 * i + j
-                slot = lax.rem(count, 2)
-                r, c = lax.div(j, 3), lax.rem(j, 3)
-                row_cols = pl.ds(pl.multiple_of(r * row_tile, 128), row_tile)
-                col_cols = pl.ds(pl.multiple_of(c * col_tile, 128), col_tile)
-                total = jnp.zeros((row_tile, col_tile), jnp.float32)
-                for u in range(2 * n):
-                    total = total + outer_rows(
-                        left_rows(i, u, row_cols), right_rows(i, u, col_cols)
-                    )
-
-                @pl.when(count >= 2)
+            left_load(u).wait()
+
+        def one_tile(j, carry):
+            slot = lax.rem(j, 2)
+            r, c = lax.div(j, 3), lax.rem(j, 3)
+            total = sum(
+                outer_rows(left_rows(g, r * row_tile), right_rows(g, c * col_tile))
+                for g in range(2)
+            )
+
+            @pl.when(j >= 2)
+            def _():
+                tile_store(r, c, slot).wait()
+
+            tile[slot] = total.astype(tile.dtype)
+            tile_store(r, c, slot).start()
+            for step, turn in enumerate(SUM_TURNS):
+
+                @pl.when(j == turn)
                 def _():
-                    tile_store(i, r, c, slot).wait()
-
-                tile[slot] = total.astype(tile.dtype)
-                tile_store(i, r, c, slot).start()
-
-                for step, turn in enumerate(SUM_TURNS):
-
-                    @pl.when(count == turn)
-                    def _():
-                        between(step)
-
-                return carry
-
-            lax.fori_loop(0, 9, one_tile, 0)
+                    between(step)
+
+            return carry
+
+        lax.fori_loop(0, 9, one_tile, 0)
         for slot in range(2):
-            tile_store(0, 0, 0, slot).wait()
+            tile_store(0, 0, slot).wait()
 
     def unit(t, carry):
         d, h = source(t)
@@ -1058,7 +1177,7 @@
             combine(lax.div(unit, 2), lax.rem(unit, 2))
 
     if backward:
-        weight_gradients(middle)
+        down_gradient(middle)
     else:
 
         def one(i, carry):
@@ -1126,9 +1245,8 @@
 
     lax.fori_loop(0, 2 * n, drain, 0)
     for h in range(2):
-        if not backward:
-            for i in range(len(stage_outs)):
-                stage_store(i, 0, h, h).wait()
+        for i in range(len(stage_outs)):
+            stage_store(i, 0, h, h).wait()
         pltpu.make_async_copy(own_sum.at[s, h], out.at[h], out_sem.at[h]).wait()
 
 
@@ -1158,14 +1276,13 @@
             DMA((2, 2)),
             pltpu.VMEM((2, n_units // 3, width // 3), low),
             DMA((2,)),
-            DMA((3, 2 * n_seq)),
-            DMA((2 * n_seq, 2)),
+            DMA((2 * n_seq,)),
         ]
     else:
         outs += [jax.ShapeDtypeStruct(held, low)]
     outs += [jax.ShapeDtypeStruct(unit_rows, low)] * n_stage
     if backward:
-        outs += [jax.ShapeDtypeStruct(units.shape, low), jax.ShapeDtypeStruct(downs.shape, low)]
+        outs += [jax.ShapeDtypeStruct(downs.shape, low)]
     pairs = DMA((n_seq, halves))
     scratch += [DMA((2,)), DMA((halves,))] + [pairs] * 7
     scratch += [DMA((n_seq, halves, SUBS)), DMA((n_seq + 1, halves, SUBS))]
@@ -1480,7 +1597,7 @@
     attn_out = attend(queries, keys, values, segment_col, segment_row)
     proj_parts = times_rows(attn_out, own_out).astype(jnp.bfloat16)
     proj_parts = plane_exchange(
-        proj_parts.reshape(n_plane, piece_len, model_width), False, 2
+        proj_parts.reshape(n_plane, piece_len, model_width), 2
     )
 
     def sum_parts(parts):
@@ -1503,17 +1620,14 @@
     cotangent = output_cotangent.reshape(row_count, model_width).astype(jnp.float32)
     unused_last, pull_last = jax.vjp(rms_norm, down_out, gain_cols[:, 3])
     grad_down, grad_gain_last = pull_last(cotangent)
-    grad_ffn_in, unused_gate, unused_up, gate_up_rows, down_rows = run_units(
+    grad_ffn_in, gate_low, up_low, down_rows = run_units(
         n_seq,
         grad_down.astype(jnp.bfloat16).reshape(pieces),
         unit_weights,
         down_units,
-        (gate_part, up_part, hidden_part, ffn_all),
+        (gate_part, up_part, hidden_part),
     )
     grad_ffn_in = grad_ffn_in.reshape(row_count, model_width)
-    gate_up_grad = lax.psum_scatter(
-        gate_up_rows, "chip", scatter_dimension=0, tiled=True
-    ).astype(jnp.float32)
     down_grad = lax.psum_scatter(down_rows, "chip", scatter_dimension=0, tiled=True).astype(
         jnp.float32
     )
@@ -1525,9 +1639,13 @@
     grad_proj, grad_gain_post = pull_post(grad_after)
     grad_proj_low = grad_proj.astype(jnp.bfloat16)
 
-    grad_proj_all = plane_exchange(
-        grad_proj_low.reshape(groups, piece_len, model_width), True, 3
-    ).reshape(seq_len, model_width)
+    grad_proj_all, gate_up_rows = spread_plane(
+        grad_proj_low.reshape(groups, piece_len, model_width), gate_low, up_low, ffn_all
+    )
+    gate_up_grad = lax.psum_scatter(
+        gate_up_rows, "chip", scatter_dimension=0, tiled=True
+    ).astype(jnp.float32)
+    grad_proj_all = grad_proj_all.reshape(seq_len, model_width)
     grad_attn = add_slice(grad_proj_all, own_out).astype(jnp.bfloat16)
     grad_query_rot, grad_key_rot, grad_values = attend_back(
         queries, keys, values, segment_col, segment_row, grad_attn

time: 863 us -> 834 us (0.966)
  waiting for transfers between devices: 30.6 us -> 1.42 us
    pallas_call x2, Pallas kernels: 294 us -> 271 us  [run_units(): pl.pallas_call(partial(units_kernel, n_seq, backward), out_shape=outs, in...]
    all_gather x1, waiting for transfers between devices: 18.9 us -> 0.01 us  [per_device_by_heads(): unit_weights = lax.all_gather(gate_up_weight, 'chip', axis=0, tiled=True)]
    pallas_call x2, Pallas kernels: 159 us -> 176 us  [the longest x1 106 us: plane_exchange(): pl.pallas_call(partial(exchange_kernel, n_plane), out_shape=jax.ShapeDtyp...]
    reduce_scatter x1, waiting for transfers between devices: 9.96 us -> 0.01 us  [per_device_by_heads(): lax.psum_scatter(gate_up_rows, 'chip', scatter_dimension=0, tiled=True)]
    pallas_call x1, Pallas kernels: 96.9 us -> 106 us  [sum_last(): pl.pallas_call(partial(last_kernel, n_seq, n_plane), out_shape=[jax.Shape...]
    unnamed x111 -> x115, local copies, waits for them, and re-layouts: 19.4 us -> 23.2 us
  transfers between devices with their start and end apart: 4 -> 4, of which waited for: 2 -> 0; matrix products, arithmetic and copies ran while one was open for 15% -> 15% of each run, Pallas kernels for 42% -> 47%
where the time goes in v5:
time: 834 us; the launch traced here: 825 us
  Pallas kernels  655 us (79%)
  other arithmetic  64 us (8%)
  local copies, waits for them, and re-layouts  48.7 us (6%)
  matrix products  41.2 us (5%)
  between operations  15 us (2%)
    pallas_call x2, Pallas kernels, run_units(): pl.pallas_call(partial(units_kernel, n_seq, backward), out_shape=outs, in...  271 us
    pallas_call x1, Pallas kernels, sum_last(): pl.pallas_call(partial(last_kernel, n_seq, n_plane), out_shape=[jax.Shape...  106 us
    pallas_call x1, Pallas kernels, plane_exchange(): pl.pallas_call(partial(exchange_kernel, n_plane), out_shape=jax.ShapeDtyp...  106 us
    pallas_call x1, Pallas kernels, gather_first(): pl.pallas_call(partial(gather_kernel, n_seq, n_plane), out_shape=[jax.Sha...  90.8 us
    pallas_call x1, Pallas kernels, spread_plane(): pl.pallas_call(partial(spread_kernel, n_plane), out_shape=[jax.ShapeDtype...  69.9 us
    unnamed x115, local copies, waits for them, and re-layouts  23.2 us
    dot_general x2, matrix products, times_rows(): lax.dot_general(left, weight_piece, (((1,), (1,)), ((), ())), preferred_e...  17.2 us
  transfers between devices with their start and end apart: 4, of which 0 were waited for; matrix products, arithmetic and copies ran while one was open for 15% of the time, Pallas kernels for 47%

profile of v5, /device:TPU:0, one launch (start us, length us, event | category | flops | bytes accessed | tf_op | source)
XLA Modules:
  0.0 825.2 jit_solution(17002855744046587277)
XLA Ops:
  7.2 0.7 all-gather.5.cloned.1.call-update
  8.0 0.7 all-gather.3.cloned.1.call-update
  8.9 1.1 pad_maximum_fusion.4.blocks
  10.0 90.8 %shard_map.144 = (bf16[8,128,2304]{2,1,0:T(8,128)(2,1)}, bf16[4,2,4,80,1536]{4,3,2,1,0:T(8,128)(2,1)}) custom-call(bf16[2,128,2304]{2,1,0:T(8,128)(2,1)} %hidden.1, bf16[4,80,1536]{2,1,0:T(8,128)(2,1)} %pad_maximum_fusion.4.blocks), custom_call_target="tpu_custom_call" | custom-call | tf_op jit(solution)/shard_map/pallas_call | solution.py:491
  100.8 3.7 slice.219
  104.6 3.8 copy.35
  108.3 0.8 convert_bitcast_fusion
  109.5 3.5 fusion.1
  113.2 1.1 fusion.3
  114.4 3.7 copy-done.26
  118.1 5.4 fusion.10
  123.7 1.5 slice.221
  125.6 1.3 copy.50
  126.9 2.7 fusion.72
  129.6 2.5 copy.49
  132.2 1.3 copy.48
  133.5 0.8 select_reduce_fusion
  134.3 1.9 multiply_cosine_fusion.1
  136.2 2.7 subtract_convert_fusion.1
  138.9 1.1 pad_maximum_fusion.2
  140.3 2.4 fusion.45
  142.8 3.7 shard_map.145
  146.5 6.8 convolution_convert_fusion
  153.3 105.7 %shard_map.146 = bf16[8,128,2304]{2,1,0:T(8,128)(2,1)} custom-call(bf16[8,128,2304]{2,1,0:T(8,128)(2,1)} %bitcast.138), custom_call_target="tpu_custom_call" | custom-call | tf_op jit(solution)/shard_map/pallas_call | solution.py:255
  259.0 3.4 convert_reduce_fusion.1
  262.7 1.9 copy-done.21
  264.5 0.6 multiply_reduce_fusion.5
  265.2 1.4 copy-done.15
  266.6 1.3 multiply_convert_fusion.refs_0_
  267.9 130.3 %shard_map.147 = (f32[2,128,2304]{2,1,0:T(8,128)}, bf16[4,2,2,128,2304]{4,3,2,1,0:T(8,128)(2,1)}, bf16[8,256,1152]{2,1,0:T(8,128)(2,1)}, bf16[8,256,1152]{2,1,0:T(8,128)(2,1)}, bf16[8,256,1152]{2,1,0:T(8,128)(2,1)}) custom-call(bf16[2,128,2304]{2,1,0:T(8,128)(2,1)} %multiply_convert_fusion.refs_0_, bf16[1152,4608]{1,0:T(8,128)(2,1)} %all-gather.3.cloned.1.call-done.refs_1_, ...), custom_call_target="tpu_custom_call" | custom-call | tf_op jit(solution)/shard_map/pallas_call | solution.py:1291
  398.2 2.1 multiply_reduce_fusion.4
  400.6 2.3 fusion.15
  402.9 3.3 fusion.16
  406.2 140.4 %shard_map.148 = (f32[2,128,2304]{2,1,0:T(8,128)}, bf16[8,256,1152]{2,1,0:T(8,128)(2,1)}, bf16[8,256,1152]{2,1,0:T(8,128)(2,1)}, bf16[1152,2304]{1,0:T(8,128)(2,1)}) custom-call(bf16[2,128,2304]{2,1,0:T(8,128)(2,1)} %get-tuple-element.66.refs_0_, bf16[1152,4608]{1,0:T(8,128)(2,1)} %all-gather.3.cloned.1.call-done.refs_1_, ...), custom_call_target="tpu_custom_call" | custom-call | tf_op jit(solution)/shard_map/pallas_call | solution.py:1291
  546.6 1.6 copy-done.17
  548.2 2.4 multiply_reduce_fusion
  550.9 3.1 multiply_reduce_fusion.1
  554.5 0.9 copy-done.19
  555.4 69.9 %shard_map.149 = (bf16[8,128,2304]{2,1,0:T(8,128)(2,1)S(1)}, bf16[1152,4608]{1,0:T(8,128)(2,1)}) custom-call(bf16[2,128,2304]{2,1,0:T(8,128)(2,1)S(1)} %fusion.17.blocks, bf16[8,256,1152]{2,1,0:T(8,128)(2,1)} %get-tuple-element.32.low_gate, bf16[8,256,1152]{2,1,0:T(8,128)(2,1)} %get-tuple-element.33.low_up, ...), custom_call_target="tpu_custom_call" | custom-call | tf_op jit(solution)/shard_map/pallas_call | solution.py:343
  625.3 2.2 copy-done.12
  627.9 5.8 fusion.24.grads
  633.8 7.5 shard_map.150
  641.3 1.0 copy-done.6
  642.2 1.0 copy-done.8
  643.2 2.3 reshape.562
  645.5 2.7 add_convert_fusion.1
  648.3 1.1 pad_maximum_fusion.3
  649.8 1.0 copy-done.9
  650.7 2.3 fusion.40
  653.2 7.3 convolution_convert_fusion.2
  660.6 5.6 convolution_convert_fusion.1
  666.1 5.1 pad_maximum_fusion
  671.2 10.3 %copy.42 = bf16[2304,1536]{1,0:T(8,128)(2,1)} copy(bf16[2304,1536]{0,1:T(8,128)(2,1)} %pad_maximum_fusion) | data formatting | bytes 14155776 | tf_op jit(solution)/shard_map/concatenate | solution.py:1664
  681.5 10.3 %fusion.5 = (bf16[2304]{0:T(1024)(128)(2,1)S(1)}, bf16[1024,2304]{1,0:T(8,128)(2,1)}) fusion(bf16[8,128,2304]{2,1,0:T(8,128)(2,1)} %get-tuple-element.25, f32[1024]{0:T(1024)S(1)} %rsqrt_bitcast_fusion, bf16[2304,1536]{1,0:T(8,128)(2,1)} %bitcast.132, bf16[1024,256]{1,0:T(8,128)(2,1)S(1)} %copy-done.37, bf16[1024,256]{1,0:T(8,128)(2,1)S(1)} %copy-done.39, ...), kind=kOutput, calls=%fused_computation.11 | convolution fusion | flops 4849924096 | bytes 16261632 | tf_op jit(solution)/shard_map/dot_general | solution.py:99
  692.1 4.9 fusion.7.blocks
  697.1 106.5 %shard_map.151 = (bf16[8,128,2304]{2,1,0:T(8,128)(2,1)S(1)}, bf16[4,80,1536]{2,1,0:T(8,128)(2,1)S(1)}) custom-call(bf16[8,128,2304]{2,1,0:T(8,128)(2,1)S(1)} %bitcast.122, bf16[4,2,4,80,1536]{4,3,2,1,0:T(8,128)(2,1)S(1)} %fusion.7.blocks), custom_call_target="tpu_custom_call" | custom-call | tf_op jit(solution)/shard_map/pallas_call | solution.py:662
  803.5 0.6 convert_reduce_fusion.2
  804.1 0.8 convert_reduce_fusion
  805.5 0.6 fusion.19
  806.6 0.9 pad_maximum_fusion.7
  807.5 1.2 copy-done.20
  808.6 2.1 fusion.18
  810.7 3.0 convert_element_type.151
  813.7 4.8 convert_element_type.150
  (152 shorter events, 5.2 us)
Async XLA Ops:
  7.2 1.6 copy-start.35
  7.2 1.6 copy-start.40
  7.2 260.7 %all-gather.5.cloned.1.call-start = ((), (), s32[]{:S(2)}) async-start(), calls=%async_computation.3 | async-start | bytes 6635520 | tf_op jit(solution)/shard_map/all_gather | solution.py:1557
  7.9 0.9 copy-start.42
  7.9 259.9 %all-gather.3.cloned.1.call-start = ((), (), s32[]{:S(2)}) async-start(), calls=%async_computation.2 | async-start | bytes 13271040 | tf_op jit(solution)/shard_map/all_gather | solution.py:1556
  8.7 802.1 %reduce-scatter.5.cloned.1.call-start = ((), (), s32[]{:S(2)}) async-start(), calls=%async_computation.5 | async-start | bytes 6635520 | tf_op jit(solution)/shard_map/reduce_scatter | solution.py:1631
  109.5 3.8 copy-start.23
  113.2 4.9 copy-start.26
  114.4 9.1 %copy-start.27 = (bf16[1024,2304]{1,0:T(8,128)(2,1)}, bf16[1024,2304]{1,0:T(8,128)(2,1)S(1)}, u32[]{:S(2)}) copy-start(bf16[1024,2304]{1,0:T(8,128)(2,1)S(1)} %fusion.3) | copy-start | bytes 14155780
  123.7 1.5 copy-start.43
  123.7 1.5 copy-start.44
  125.6 17.1 %copy-start.2 = (bf16[1024,256]{1,0:T(8,128)(2,1)}, bf16[1024,256]{1,0:T(8,128)(2,1)S(1)}, u32[]{:S(2)}) copy-start(bf16[1024,256]{1,0:T(8,128)(2,1)S(1)} %copy.51.values) | copy-start | bytes 1572868
  136.1 3.9 copy-start.28
  136.2 3.9 copy-start.30
  138.9 1.4 copy-start.32
  140.3 6.2 copy-start
  142.7 10.6 %copy-start.4 = (bf16[1024,256]{1,0:T(8,128)(2,1)}, bf16[1024,256]{1,0:T(8,128)(2,1)S(1)}, u32[]{:S(2)}) copy-start(bf16[1024,256]{1,0:T(8,128)(2,1)S(1)} %pad_maximum_fusion.8.keys) | copy-start | bytes 1572868
  146.5 6.9 copy-start.10
  262.4 2.8 copy-start.13
  262.4 2.1 copy-start.21
  265.2 1.4 copy-start.15
  398.2 2.4 copy-start.18
  400.2 2.6 copy-start.16
  400.3 2.6 copy-start.24
  546.5 1.7 copy-start.17
  546.6 267.2 %reduce-scatter.3.cloned.1.call-start = ((), (), s32[]{:S(2)}) async-start(), calls=%async_computation.4 | async-start | bytes 13271040 | tf_op jit(solution)/shard_map/reduce_scatter | solution.py:1645
  548.2 2.4 copy-start.14
  548.2 2.7 copy-start.25
  554.0 1.4 copy-start.19
  625.3 2.2 copy-start.12
  627.9 5.9 copy-start.1
  627.9 5.9 copy-start.3
  627.9 5.9 copy-start.5
  641.2 1.0 copy-start.6
  642.2 1.0 copy-start.8
  643.2 2.3 copy-start.29
  643.2 2.3 copy-start.31
  648.3 1.4 copy-start.7
  649.4 1.3 copy-start.9
  649.7 10.9 %copy-start.33 = (bf16[128,8,2,256]{3,1,2,0:T(8,128)(2,1)}, bf16[128,8,2,256]{3,1,2,0:T(8,128)(2,1)S(1)}, u32[]{:S(2)}) copy-start(bf16[128,8,2,256]{3,1,2,0:T(8,128)(2,1)S(1)} %copy.53) | copy-start | bytes 3145732
  649.7 3.5 copy-start.11
  649.8 10.8 %copy-start.36 = (bf16[1024,256]{1,0:T(8,128)(2,1)}, bf16[1024,256]{1,0:T(8,128)(2,1)S(1)}, u32[]{:S(2)}) copy-start(bf16[1024,256]{1,0:T(8,128)(2,1)S(1)} %convert.66) | copy-start | bytes 1572868
  650.7 9.8 %slice-start.2 = ((s8[4718592]{0:T(1024)(128)(4,1)}), s8[4194304]{0:T(1024)(128)(4,1)S(1)}, s32[]{:S(2)}) async-start(s8[4718592]{0:T(1024)(128)(4,1)} %bitcast.136), calls=%async_computation.8 | async-start | bytes 8388608
  653.2 7.4 copy-start.38
  653.2 7.4 slice-start.3
  671.2 10.3 %copy-start.34 = (bf16[128,8,2,256]{3,1,2,0:T(8,128)(2,1)S(1)}, bf16[128,8,2,256]{3,1,2,0:T(8,128)(2,1)}, u32[]{:S(2)}) copy-start(bf16[128,8,2,256]{3,1,2,0:T(8,128)(2,1)} %copy-done.33) | copy-start | bytes 3145732
  671.2 10.3 %copy-start.37 = (bf16[1024,256]{1,0:T(8,128)(2,1)S(1)}, bf16[1024,256]{1,0:T(8,128)(2,1)}, u32[]{:S(2)}) copy-start(bf16[1024,256]{1,0:T(8,128)(2,1)} %copy-done.36) | copy-start | bytes 1572868
  671.2 10.3 %copy-start.39 = (bf16[1024,256]{1,0:T(8,128)(2,1)S(1)}, bf16[1024,256]{1,0:T(8,128)(2,1)}, u32[]{:S(2)}) copy-start(bf16[1024,256]{1,0:T(8,128)(2,1)} %copy-done.38) | copy-start | bytes 1572868
  692.1 4.9 slice-start
  692.1 4.9 slice-start.1
  804.1 1.3 copy-start.22
  806.3 2.3 copy-start.20
  806.5 4.2 copy-start.41
Sparse Core Ops, SparseCore 0:
  9.9 97.2 all-gather.4
  109.0 157.4 all-gather.2
  546.7 96.0 reduce-scatter.4
  645.8 158.9 reduce-scatter.2

commit v6 on v5

--- a/solution.py
+++ b/solution.py
@@ -777,6 +777,21 @@
     )(queries, keys, values, segment_col, segment_row, grads)
 
 
+def chip_beside(c, flip):
+    return c ^ flip
+
+
+def chip_places(rows):
+    q = lax.axis_index("chip")
+    x, y = lax.rem(q, 2), lax.div(q, 2)
+    across = (2 * (1 - y) + 1 - x) * rows
+    return (q * rows, (2 * y + 1 - x) * rows, (2 * (1 - y) + x) * rows, across, across + rows // 2)
+
+
+def send_beside(part, flip):
+    return lax.ppermute(part, "chip", [(c, chip_beside(c, flip)) for c in range(KV_HEADS)])
+
+
 def unit_orders(n):
     units, sums = [], []
     for s in range(n):
@@ -825,15 +840,18 @@
 
 def units_kernel(n_seq, backward, *refs):
     if backward:
-        tokens, units, downs, kept_gate, kept_up, kept_hidden = refs[:6]
-        out, first_out, second_out, down_grads = refs[6:10]
+        tokens, units = refs[:2]
+        downs = refs[2:7]
+        kept_gate, kept_up, kept_hidden = refs[7:10]
+        out, first_out, second_out, down_grads = refs[10:14]
         stage_outs = (first_out, second_out)
-        scratch = refs[10:]
+        scratch = refs[14:]
     else:
-        tokens, units, downs = refs[:3]
-        out, tokens_all, first_out, second_out, third_out = refs[3:8]
+        tokens, units = refs[:2]
+        downs = refs[2:7]
+        out, tokens_all, first_out, second_out, third_out = refs[7:12]
         stage_outs = (first_out, second_out, third_out)
-        scratch = refs[8:]
+        scratch = refs[12:]
     units_v, downs_v, held, own_sum, twin_sum, twin_out, line, stage = scratch[:8]
     scratch = scratch[8:]
     if backward:
@@ -970,14 +988,19 @@
         token_twin(s, h, tokens.at[h]).start()
         own_load(h).start()
     load_units = pltpu.make_async_copy(units, units_v, weight_sem.at[0])
-    load_downs = pltpu.make_async_copy(downs, downs_v, weight_sem.at[1])
+    load_downs = []
+    for i, (first, part) in enumerate(zip(chip_places(downs[0].shape[0]), downs)):
+        rows = pl.ds(pl.multiple_of(first, 16), part.shape[0])
+        load_downs.append(pltpu.make_async_copy(part, downs_v.at[rows], weight_sem.at[1 + i]))
     load_units.start()
-    load_downs.start()
+    for load in load_downs:
+        load.start()
     if backward:
         for i in range(2):
             kept_load(i, s, 0, 0).start()
     load_units.wait()
-    load_downs.wait()
+    for load in load_downs:
+        load.wait()
 
     def add_rows(d, h, sub, into_own, use_line):
         step = 16
@@ -1253,7 +1276,7 @@
 def run_units(n_seq, tokens, units, downs, kept=None):
     backward = kept is not None
     low = tokens.dtype
-    n_units = downs.shape[0]
+    n_units = units.shape[0]
     halves, piece_len, width = tokens.shape
     n_stage = 2 if backward else 3
     held = (n_seq, halves, 2, piece_len, width)
@@ -1261,7 +1284,7 @@
     sums = (n_seq, halves, piece_len, width)
     scratch = [
         pltpu.VMEM(units.shape, low),
-        pltpu.VMEM(downs.shape, low),
+        pltpu.VMEM((n_units, width), low),
         pltpu.VMEM(held, low),
         pltpu.VMEM(sums, jnp.float32),
         pltpu.VMEM(sums, low),
@@ -1282,12 +1305,12 @@
         outs += [jax.ShapeDtypeStruct(held, low)]
     outs += [jax.ShapeDtypeStruct(unit_rows, low)] * n_stage
     if backward:
-        outs += [jax.ShapeDtypeStruct(downs.shape, low)]
+        outs += [jax.ShapeDtypeStruct((n_units, width), low)]
     pairs = DMA((n_seq, halves))
-    scratch += [DMA((2,)), DMA((halves,))] + [pairs] * 7
+    scratch += [DMA((1 + len(downs),)), DMA((halves,))] + [pairs] * 7
     scratch += [DMA((n_seq, halves, SUBS)), DMA((n_seq + 1, halves, SUBS))]
     scratch += [DMA((n_stage, 2)), pairs, DMA((halves,))]
-    operands = (tokens, units, downs) + (tuple(kept) if backward else ())
+    operands = (tokens, units) + tuple(downs) + (tuple(kept) if backward else ())
     return pl.pallas_call(
         partial(units_kernel, n_seq, backward),
         out_shape=outs,
@@ -1554,7 +1577,8 @@
     )
     hidden_all, blocks_all = gather_first(n_seq, hidden_in, blocks)
     unit_weights = lax.all_gather(gate_up_weight, "chip", axis=0, tiled=True)
-    down_units = lax.all_gather(down_weight, "chip", axis=0, tiled=True)
+    blocks_all, down_weight = lax.optimization_barrier((blocks_all, down_weight))
+    down_x, down_y = send_beside(down_weight, 1), send_beside(down_weight, 2)
     blocks_all = blocks_all.transpose(0, 2, 1, 3, 4)
     own_weights = blocks_all[:, :, :, :weight_rows].reshape(model_width, block_width)
     own_qkv = own_weights[:, :part_width]
@@ -1596,6 +1620,15 @@
     segment_row = jnp.where(valid == 1, segment, -1)[None, :]
     attn_out = attend(queries, keys, values, segment_col, segment_row)
     proj_parts = times_rows(attn_out, own_out).astype(jnp.bfloat16)
+    proj_parts, down_x, down_y = lax.optimization_barrier((proj_parts, down_x, down_y))
+    half = down_weight.shape[0] // 2
+    down_units = (
+        down_weight,
+        down_x,
+        down_y,
+        send_beside(down_x[:half], 2),
+        send_beside(down_y[half:], 1),
+    )
     proj_parts = plane_exchange(
         proj_parts.reshape(n_plane, piece_len, model_width), 2
     )

time: 834 us -> 818 us (0.981)
  Pallas kernels: 655 us -> 619 us
  waiting for transfers between devices: 1.42 us -> 13.5 us
    pallas_call x1, Pallas kernels: 106 us -> 60.7 us  [plane_exchange(): pl.pallas_call(partial(exchange_kernel, n_plane), out_shape=jax.ShapeDtyp...]
    ppermute x0 -> x4, waiting for transfers between devices: none -> 12.8 us  [send_beside(): lax.ppermute(part, 'chip', [(c, chip_beside(c, flip)) for c in range(KV_H...]
  transfers between devices with their start and end apart: 4 -> 7, of which waited for: 0 -> 4; matrix products, arithmetic and copies ran while one was open for 15% -> 16% of each run, Pallas kernels for 47% -> 43%
where the time goes in v6:
time: 818 us; the launch traced here: 809 us
  Pallas kernels  619 us (76%)
  other arithmetic  64 us (8%)
  local copies, waits for them, and re-layouts  51 us (6%)
  matrix products  41.2 us (5%)
  between operations  15 us (2%)
  waiting for transfers between devices  13.5 us (2%)
    pallas_call x2, Pallas kernels, run_units(): pl.pallas_call(partial(units_kernel, n_seq, backward), out_shape=outs, in...  273 us
    pallas_call x1, Pallas kernels, sum_last(): pl.pallas_call(partial(last_kernel, n_seq, n_plane), out_shape=[jax.Shape...  106 us
    pallas_call x1, Pallas kernels, gather_first(): pl.pallas_call(partial(gather_kernel, n_seq, n_plane), out_shape=[jax.Sha...  97.2 us
    pallas_call x1, Pallas kernels, spread_plane(): pl.pallas_call(partial(spread_kernel, n_plane), out_shape=[jax.ShapeDtype...  70.8 us
    pallas_call x1, Pallas kernels, plane_exchange(): pl.pallas_call(partial(exchange_kernel, n_plane), out_shape=jax.ShapeDtyp...  60.7 us
    unnamed x115, local copies, waits for them, and re-layouts  23.3 us
    dot_general x2, matrix products, times_rows(): lax.dot_general(left, weight_piece, (((1,), (1,)), ((), ())), preferred_e...  17.2 us
  transfers between devices with their start and end apart: 7, of which 4 were waited for; matrix products, arithmetic and copies ran while one was open for 16% of the time, Pallas kernels for 43%

profile of v6, /device:TPU:0, one launch (start us, length us, event | category | flops | bytes accessed | tf_op | source)
XLA Modules:
  0.0 809.2 jit_solution(11428652924619752125)
XLA Ops:
  8.5 1.1 pad_maximum_fusion.4.blocks
  9.5 97.2 %shard_map.144 = (bf16[8,128,2304]{2,1,0:T(8,128)(2,1)}, bf16[4,2,4,80,1536]{4,3,2,1,0:T(8,128)(2,1)}) custom-call(bf16[2,128,2304]{2,1,0:T(8,128)(2,1)} %hidden.1, bf16[4,80,1536]{2,1,0:T(8,128)(2,1)} %pad_maximum_fusion.4.blocks), custom_call_target="tpu_custom_call" | custom-call | tf_op jit(solution)/shard_map/pallas_call | solution.py:491
  107.5 1.4 collective-permute-start
  108.9 3.7 slice.227
  112.6 3.8 copy.35
  117.6 3.5 fusion.1
  121.3 1.1 fusion.3
  122.5 3.6 copy-done.26
  126.0 5.4 fusion.10
  131.6 1.5 slice.229
  133.6 1.3 copy.50
  134.9 2.7 fusion.72
  137.6 2.5 copy.49
  140.1 1.3 copy.48
  142.2 1.9 multiply_cosine_fusion.1
  144.1 2.7 subtract_convert_fusion.1
  146.8 1.1 pad_maximum_fusion.2
  148.2 2.4 fusion.45
  150.7 3.7 shard_map.145
  154.4 6.8 convolution_convert_fusion
  161.2 6.1 collective-permute-done.1.refs_4_
  167.8 60.7 %shard_map.146 = bf16[8,128,2304]{2,1,0:T(8,128)(2,1)} custom-call(bf16[8,128,2304]{2,1,0:T(8,128)(2,1)} %bitcast.138), custom_call_target="tpu_custom_call" | custom-call | tf_op jit(solution)/shard_map/pallas_call | solution.py:255
  228.5 1.1 slice.200
  229.7 1.1 slice.201
  230.8 1.1 collective-permute-start.3
  231.9 1.7 collective-permute-start.2
  233.6 3.4 convert_reduce_fusion.1
  237.3 1.9 copy-done.21
  239.8 1.4 copy-done.15
  241.2 1.3 multiply_convert_fusion.refs_0_
  242.5 5.2 collective-permute-done.3.refs_6_
  247.7 1.1 collective-permute-done.2.refs_5_
  248.7 129.1 %shard_map.147 = (f32[2,128,2304]{2,1,0:T(8,128)}, bf16[4,2,2,128,2304]{4,3,2,1,0:T(8,128)(2,1)}, bf16[8,256,1152]{2,1,0:T(8,128)(2,1)}, bf16[8,256,1152]{2,1,0:T(8,128)(2,1)}, bf16[8,256,1152]{2,1,0:T(8,128)(2,1)}) custom-call(bf16[2,128,2304]{2,1,0:T(8,128)(2,1)} %multiply_convert_fusion.refs_0_, bf16[1152,4608]{1,0:T(8,128)(2,1)} %all-gather.2.cloned.1.call-done.refs_1_, ...), custom_call_target="tpu_custom_call" | custom-call | tf_op jit(solution)/shard_map/pallas_call | solution.py:1314
  377.9 2.1 multiply_reduce_fusion.4
  380.2 2.3 fusion.15
  382.6 3.3 fusion.16
  385.9 143.9 %shard_map.148 = (f32[2,128,2304]{2,1,0:T(8,128)}, bf16[8,256,1152]{2,1,0:T(8,128)(2,1)}, bf16[8,256,1152]{2,1,0:T(8,128)(2,1)}, bf16[1152,2304]{1,0:T(8,128)(2,1)}) custom-call(bf16[2,128,2304]{2,1,0:T(8,128)(2,1)} %get-tuple-element.76.refs_0_, bf16[1152,4608]{1,0:T(8,128)(2,1)} %all-gather.2.cloned.1.call-done.refs_1_, bf16[288,2304]{1,0:T(8,128)(2,1)} %refs_2_.1, ...), custom_call_target="tpu_custom_call" | custom-call | tf_op jit(solution)/shard_map/pallas_call | solution.py:1314
  529.9 1.6 copy-done.17
  531.5 2.4 multiply_reduce_fusion
  534.1 3.1 multiply_reduce_fusion.1
  537.7 0.9 copy-done.19
  538.6 70.8 %shard_map.149 = (bf16[8,128,2304]{2,1,0:T(8,128)(2,1)S(1)}, bf16[1152,4608]{1,0:T(8,128)(2,1)}) custom-call(bf16[2,128,2304]{2,1,0:T(8,128)(2,1)S(1)} %fusion.17.blocks, bf16[8,256,1152]{2,1,0:T(8,128)(2,1)} %get-tuple-element.42.low_gate, bf16[8,256,1152]{2,1,0:T(8,128)(2,1)} %get-tuple-element.43.low_up, ...), custom_call_target="tpu_custom_call" | custom-call | tf_op jit(solution)/shard_map/pallas_call | solution.py:343
  609.4 2.2 copy-done.12
  612.0 5.8 fusion.24.grads
  617.9 7.5 shard_map.150
  625.4 1.0 copy-done.6
  626.4 1.0 copy-done.8
  627.3 2.3 reshape.562
  629.7 2.7 add_convert_fusion.1
  632.4 1.1 pad_maximum_fusion.3
  633.9 1.0 copy-done.9
  634.9 2.3 fusion.40
  637.3 7.3 convolution_convert_fusion.2
  644.7 5.6 convolution_convert_fusion.1
  650.3 5.0 pad_maximum_fusion
  655.3 10.2 %copy.42 = bf16[2304,1536]{1,0:T(8,128)(2,1)} copy(bf16[2304,1536]{0,1:T(8,128)(2,1)} %pad_maximum_fusion) | data formatting | bytes 14155776 | tf_op jit(solution)/shard_map/concatenate | solution.py:1697
  665.5 10.3 %fusion.5 = (bf16[2304]{0:T(1024)(128)(2,1)S(1)}, bf16[1024,2304]{1,0:T(8,128)(2,1)}) fusion(bf16[8,128,2304]{2,1,0:T(8,128)(2,1)} %get-tuple-element.30, f32[1024]{0:T(1024)S(1)} %rsqrt_bitcast_fusion, bf16[2304,1536]{1,0:T(8,128)(2,1)} %bitcast.132, bf16[1024,256]{1,0:T(8,128)(2,1)S(1)} %copy-done.37, bf16[1024,256]{1,0:T(8,128)(2,1)S(1)} %copy-done.39, ...), kind=kOutput, calls=%fused_computation.11 | convolution fusion | flops 4849924096 | bytes 16261632 | tf_op jit(solution)/shard_map/dot_general | solution.py:99
  676.1 4.9 fusion.7.blocks
  681.0 106.5 %shard_map.151 = (bf16[8,128,2304]{2,1,0:T(8,128)(2,1)S(1)}, bf16[4,80,1536]{2,1,0:T(8,128)(2,1)S(1)}) custom-call(bf16[8,128,2304]{2,1,0:T(8,128)(2,1)S(1)} %bitcast.122, bf16[4,2,4,80,1536]{4,3,2,1,0:T(8,128)(2,1)S(1)} %fusion.7.blocks), custom_call_target="tpu_custom_call" | custom-call | tf_op jit(solution)/shard_map/pallas_call | solution.py:662
  790.6 0.9 pad_maximum_fusion.7
  791.5 1.2 copy-done.20
  792.6 2.1 fusion.18
  794.7 3.0 convert_element_type.151
  797.7 4.8 convert_element_type.150
  (159 shorter events, 11.6 us)
Async XLA Ops:
  7.2 1.1 copy-start.35
  7.2 1.1 copy-start.40
  7.2 1.2 copy-start.42
  7.2 241.5 %all-gather.2.cloned.1.call-start = ((), (), s32[]{:S(2)}) async-start(), calls=%async_computation.2 | async-start | bytes 13271040 | tf_op jit(solution)/shard_map/all_gather | solution.py:1579
  7.9 786.8 %reduce-scatter.5.cloned.1.call-start = ((), (), s32[]{:S(2)}) async-start(), calls=%async_computation.4 | async-start | bytes 6635520 | tf_op jit(solution)/shard_map/reduce_scatter | solution.py:1664
  106.8 60.5 %collective-permute-start.1 = (bf16[288,2304]{1,0:T(8,128)(2,1)}, bf16[288,2304]{1,0:T(8,128)(2,1)}, u32[]{:S(2)}, u32[]{:S(2)}) collective-permute-start(bf16[288,2304]{1,0:T(8,128)(2,1)} %refs_2_.1), channel_id=1, source_target_pairs={{0,4},{2,6},{4,0},{6,2},{1,5},{3,7},{5,1},{7,3},{8,12},{10,14},{12... | collective-permute-start | bytes 3981320 | tf_op jit(solution)/shard_map/ppermute | solution.py:792
  107.5 60.3 %collective-permute-start = (bf16[288,2304]{1,0:T(8,128)(2,1)}, bf16[288,2304]{1,0:T(8,128)(2,1)}, u32[]{:S(2)}, u32[]{:S(2)}) collective-permute-start(bf16[288,2304]{1,0:T(8,128)(2,1)} %refs_2_.1), channel_id=1, source_target_pairs={{0,2},{2,0},{4,6},{6,4},{1,3},{3,1},{5,7},{7,5},{8,10},{10,8},{12,... | collective-permute-start | bytes 3981320 | tf_op jit(solution)/shard_map/ppermute | solution.py:792
  117.6 3.8 copy-start.23
  121.3 4.7 copy-start.26
  122.5 8.9 %copy-start.27 = (bf16[1024,2304]{1,0:T(8,128)(2,1)}, bf16[1024,2304]{1,0:T(8,128)(2,1)S(1)}, u32[]{:S(2)}) copy-start(bf16[1024,2304]{1,0:T(8,128)(2,1)S(1)} %fusion.3) | copy-start | bytes 14155780
  131.6 1.5 copy-start.43
  131.6 1.5 copy-start.44
  133.5 17.1 %copy-start.2 = (bf16[1024,256]{1,0:T(8,128)(2,1)}, bf16[1024,256]{1,0:T(8,128)(2,1)S(1)}, u32[]{:S(2)}) copy-start(bf16[1024,256]{1,0:T(8,128)(2,1)S(1)} %copy.51.values) | copy-start | bytes 1572868
  144.1 3.9 copy-start.28
  144.1 3.9 copy-start.30
  146.8 1.4 copy-start.32
  148.2 6.2 copy-start
  150.7 10.6 %copy-start.4 = (bf16[1024,256]{1,0:T(8,128)(2,1)}, bf16[1024,256]{1,0:T(8,128)(2,1)S(1)}, u32[]{:S(2)}) copy-start(bf16[1024,256]{1,0:T(8,128)(2,1)S(1)} %pad_maximum_fusion.8.keys) | copy-start | bytes 1572868
  154.4 6.9 copy-start.10
  230.8 16.9 %collective-permute-start.3 = (bf16[144,2304]{1,0:T(8,128)(2,1)S(1)}, bf16[144,2304]{1,0:T(8,128)(2,1)}, u32[]{:S(2)}, u32[]{:S(2)}) collective-permute-start(bf16[144,2304]{1,0:T(8,128)(2,1)S(1)} %slice.201), channel_id=1, source_target_pairs={{0,2},{2,0},{4,6},{6,4},{1,3},{3,1},{5,7},{7,5},{8,10},{10,8},{12,... | collective-permute-start | bytes 1990664 | tf_op jit(solution)/shard_map/ppermute | solution.py:792
  231.9 16.8 %collective-permute-start.2 = (bf16[144,2304]{1,0:T(8,128)(2,1)S(1)}, bf16[144,2304]{1,0:T(8,128)(2,1)}, u32[]{:S(2)}, u32[]{:S(2)}) collective-permute-start(bf16[144,2304]{1,0:T(8,128)(2,1)S(1)} %slice.200), channel_id=1, source_target_pairs={{0,4},{2,6},{4,0},{6,2},{1,5},{3,7},{5,1},{7,3},{8,12},{10,14},{12... | collective-permute-start | bytes 1990664 | tf_op jit(solution)/shard_map/ppermute | solution.py:792
  237.0 2.8 copy-start.13
  237.0 2.1 copy-start.21
  239.8 1.4 copy-start.15
  377.9 2.4 copy-start.18
  379.9 2.6 copy-start.16
  379.9 2.6 copy-start.24
  529.8 1.7 copy-start.17
  529.8 267.9 %reduce-scatter.3.cloned.1.call-start = ((), (), s32[]{:S(2)}) async-start(), calls=%async_computation.3 | async-start | bytes 13271040 | tf_op jit(solution)/shard_map/reduce_scatter | solution.py:1678
  531.5 2.4 copy-start.14
  531.5 2.7 copy-start.25
  537.2 1.4 copy-start.19
  609.4 2.2 copy-start.12
  612.0 5.9 copy-start.1
  612.0 5.9 copy-start.3
  612.0 5.9 copy-start.5
  625.4 1.0 copy-start.6
  626.4 1.0 copy-start.8
  627.3 2.3 copy-start.29
  627.3 2.3 copy-start.31
  632.4 1.4 copy-start.7
  633.5 1.3 copy-start.9
  633.8 10.9 %copy-start.33 = (bf16[128,8,2,256]{3,1,2,0:T(8,128)(2,1)}, bf16[128,8,2,256]{3,1,2,0:T(8,128)(2,1)S(1)}, u32[]{:S(2)}) copy-start(bf16[128,8,2,256]{3,1,2,0:T(8,128)(2,1)S(1)} %copy.53) | copy-start | bytes 3145732
  633.8 3.5 copy-start.11
  633.9 10.8 %copy-start.36 = (bf16[1024,256]{1,0:T(8,128)(2,1)}, bf16[1024,256]{1,0:T(8,128)(2,1)S(1)}, u32[]{:S(2)}) copy-start(bf16[1024,256]{1,0:T(8,128)(2,1)S(1)} %convert.66) | copy-start | bytes 1572868
  634.9 9.8 %slice-start.2 = ((s8[4718592]{0:T(1024)(128)(4,1)}), s8[4194304]{0:T(1024)(128)(4,1)S(1)}, s32[]{:S(2)}) async-start(s8[4718592]{0:T(1024)(128)(4,1)} %bitcast.136), calls=%async_computation.7 | async-start | bytes 8388608
  637.3 7.4 copy-start.38
  637.3 7.4 slice-start.3
  655.3 10.2 %copy-start.34 = (bf16[128,8,2,256]{3,1,2,0:T(8,128)(2,1)S(1)}, bf16[128,8,2,256]{3,1,2,0:T(8,128)(2,1)}, u32[]{:S(2)}) copy-start(bf16[128,8,2,256]{3,1,2,0:T(8,128)(2,1)} %copy-done.33) | copy-start | bytes 3145732
  655.3 10.2 %copy-start.37 = (bf16[1024,256]{1,0:T(8,128)(2,1)S(1)}, bf16[1024,256]{1,0:T(8,128)(2,1)}, u32[]{:S(2)}) copy-start(bf16[1024,256]{1,0:T(8,128)(2,1)} %copy-done.36) | copy-start | bytes 1572868
  655.3 10.2 %copy-start.39 = (bf16[1024,256]{1,0:T(8,128)(2,1)S(1)}, bf16[1024,256]{1,0:T(8,128)(2,1)}, u32[]{:S(2)}) copy-start(bf16[1024,256]{1,0:T(8,128)(2,1)} %copy-done.38) | copy-start | bytes 1572868
  676.0 5.0 slice-start
  676.1 5.0 slice-start.1
  788.1 1.3 copy-start.22
  790.3 2.3 copy-start.20
  790.5 4.2 copy-start.41
Sparse Core Ops, SparseCore 0:
  9.9 185.8 all-gather.1
  529.9 96.7 reduce-scatter.4
  629.9 158.8 reduce-scatter.2

commit v7 on v6

--- a/solution.py
+++ b/solution.py
@@ -153,24 +153,158 @@
     pl.semaphore_wait(barrier, count)
 
 
-def start_exchange(n_plane, source, target, send_sems, recv_sems, local_sem):
-    me = lax.axis_index("chip") * 2 + lax.axis_index("core")
-    copies = []
-    for step in (4, 2, 6, 3, 5, 1, 7):
-        to = lax.rem(me + step, n_plane)
-        copy = remote(
-            source.at[to],
-            target.at[me],
-            send_sems.at[step],
-            recv_sems.at[step],
-            plane_device(to),
-        )
-        copy.start()
-        copies.append(copy)
-    own = pltpu.make_async_copy(source.at[me], target.at[me], local_sem.at[0])
-    own.start()
-    copies.append(own)
-    return copies
+def chip_at(q, flip):
+    x, y = lax.rem(q, 2), q // 2
+    x = 1 - x if flip in (1, 3) else x
+    y = 1 - y if flip in (2, 3) else y
+    return y * 2 + x
+
+
+class Merge:
+    def __init__(self, source, target, added, own_part, sems):
+        self.source, self.target, self.added, self.own_part = source, target, added, own_part
+        self.send_sems, self.recv_sems, self.load_sems, self.local_sems = sems
+        self.q = lax.axis_index("chip")
+        self.k = lax.axis_index("core")
+        self.half = source.shape[1] // 2
+
+    def rows(self, flip):
+        return pl.ds(0 if flip == 1 else self.half, self.half)
+
+    def direct(self, flip, core):
+        chip = chip_at(self.q, flip)
+        slot = 6 * (flip - 1) + core
+        return remote(
+            self.source.at[2 * chip + core, self.rows(flip)],
+            self.target.at[1, self.k, self.rows(flip)],
+            self.send_sems.at[slot],
+            self.recv_sems.at[6 * (flip - 1) + self.k],
+            {"chip": chip, "core": core},
+        )
+
+    def arrival(self, flip, core):
+        return remote(
+            self.source.at[0, self.rows(flip)],
+            self.target.at[1, core, self.rows(flip)],
+            self.send_sems.at[0],
+            self.recv_sems.at[6 * (flip - 1) + core],
+            {"chip": chip_at(self.q, flip)},
+        )
+
+    def across(self, flip, core):
+        slot = 6 * (flip - 1) + 2 + core
+        return remote(
+            self.source.at[2 * chip_at(self.q, 3) + core, self.rows(flip)],
+            self.added.at[flip - 1, core],
+            self.send_sems.at[slot],
+            self.recv_sems.at[slot],
+            {"chip": chip_at(self.q, flip)},
+        )
+
+    def load(self, flip, core):
+        return pltpu.make_async_copy(
+            self.source.at[2 * chip_at(self.q, 3 - flip) + core, self.rows(flip)],
+            self.own_part.at[flip - 1, core],
+            self.load_sems.at[flip - 1, core],
+        )
+
+    def summed(self, flip, core):
+        slot = 6 * (flip - 1) + 4 + core
+        return remote(
+            self.own_part.at[flip - 1, core],
+            self.target.at[2, self.k, self.rows(flip)],
+            self.send_sems.at[slot],
+            self.recv_sems.at[6 * (flip - 1) + 4 + self.k],
+            {"chip": chip_at(self.q, 3 - flip), "core": core},
+        )
+
+    def summed_arrival(self, flip, core):
+        return remote(
+            self.own_part.at[flip - 1, 0],
+            self.target.at[2, core, self.rows(flip)],
+            self.send_sems.at[0],
+            self.recv_sems.at[6 * (flip - 1) + 4 + core],
+            {"chip": chip_at(self.q, 3 - flip)},
+        )
+
+    def twin(self):
+        return remote(
+            self.source.at[2 * self.q + 1 - self.k],
+            self.target.at[0, self.k],
+            self.send_sems.at[12],
+            self.recv_sems.at[12],
+            {"core": 1 - self.k},
+        )
+
+    def twin_arrival(self):
+        return remote(
+            self.source.at[0],
+            self.target.at[0, 1 - self.k],
+            self.send_sems.at[12],
+            self.recv_sems.at[12],
+            {"core": 1 - self.k},
+        )
+
+    def own(self):
+        return pltpu.make_async_copy(
+            self.source.at[2 * self.q + self.k], self.target.at[0, self.k], self.local_sems.at[0]
+        )
+
+    def start(self):
+        pairs = [(flip, core) for core in (0, 1) for flip in (1, 2)]
+        for flip, core in pairs:
+            self.across(flip, core).start()
+        for flip, core in pairs:
+            self.load(flip, core).start()
+        for flip, core in pairs:
+            self.direct(flip, core).start()
+        self.twin().start()
+        self.own().start()
+
+    def pass_on(self):
+        step = 16
+        for core in (0, 1):
+            for flip in (1, 2):
+                self.load(flip, core).wait()
+                self.across(flip, core).wait_recv()
+
+                def body(i, carry, flip=flip, core=core):
+                    rows = pl.ds(pl.multiple_of(i * step, step), step)
+                    total = self.own_part[flip - 1, core, rows, :].astype(jnp.float32)
+                    total = total + self.added[flip - 1, core, rows, :].astype(jnp.float32)
+                    self.own_part[flip - 1, core, rows, :] = total.astype(self.own_part.dtype)
+                    return carry
+
+                lax.fori_loop(0, self.half // step, body, 0)
+                self.summed(flip, core).start()
+
+    def finish(self):
+        for core in (0, 1):
+            for flip in (1, 2):
+                self.across(flip, core).wait_send()
+                self.direct(flip, core).wait_send()
+                self.arrival(flip, core).wait_recv()
+                self.summed(flip, core).wait_send()
+                self.summed_arrival(flip, core).wait_recv()
+        self.twin().wait_send()
+        self.twin_arrival().wait_recv()
+        self.own().wait()
+
+
+def merge_scratch(blocks):
+    part = (2, 2, blocks.shape[1] // 2, blocks.shape[2])
+    return [
+        pltpu.VMEM(part, blocks.dtype),
+        pltpu.VMEM(part, blocks.dtype),
+        DMA((13,)),
+        DMA((13,)),
+        DMA((2, 2)),
+        DMA((1,)),
+    ]
+
+
+def merged_shape(blocks):
+    return jax.ShapeDtypeStruct((3, 2) + blocks.shape[1:], blocks.dtype)
 
 
 class Spread:
@@ -183,10 +317,7 @@
         self.half = source.shape[1] // 2
 
     def chip(self, flip):
-        x, y = lax.rem(self.q, 2), self.q // 2
-        x = 1 - x if flip in (1, 3) else x
-        y = 1 - y if flip in (2, 3) else y
-        return y * 2 + x
+        return chip_at(self.q, flip)
 
     def direct(self, flip, twin):
         core = 1 - self.k if twin else self.k
@@ -244,24 +375,42 @@
 SPREAD_SLOTS = 12
 
 
-def exchange_kernel(n_plane, source, target, send_sems, recv_sems, local_sem):
+def merge_kernel(n_plane, source, rows_x, rows_y, target, across, added, own_part, *sems):
     greet(n_plane, 1)
-    for copy in start_exchange(n_plane, source, target, send_sems, recv_sems, local_sem):
+    merge = Merge(source, target, added, own_part, sems[:4])
+    pass_send, pass_recv = sems[4:]
+    merge.start()
+    half = rows_x.shape[0] // 2
+    passed = [
+        remote(
+            rows.at[pl.ds(i * half, half)],
+            across.at[i],
+            pass_send.at[i],
+            pass_recv.at[i],
+            {"chip": chip_at(merge.q, 2 - i)},
+        )
+        for i, rows in enumerate((rows_x, rows_y))
+    ]
+    for copy in passed:
+        copy.start()
+    merge.pass_on()
+    merge.finish()
+    for copy in passed:
         copy.wait()
 
 
-def plane_exchange(blocks, collective_id):
-    n_plane = 2 * KV_HEADS
+def merge_plane(blocks, rows_x, rows_y, collective_id):
+    half = (2, rows_x.shape[0] // 2, rows_x.shape[1])
     return pl.pallas_call(
-        partial(exchange_kernel, n_plane),
-        out_shape=jax.ShapeDtypeStruct((n_plane,) + blocks.shape[1:], blocks.dtype),
-        in_specs=[ANY],
-        out_specs=ANY,
-        scratch_shapes=[DMA((n_plane,)), DMA((n_plane,)), DMA((1,))],
+        partial(merge_kernel, 2 * KV_HEADS),
+        out_shape=[merged_shape(blocks), jax.ShapeDtypeStruct(half, rows_x.dtype)],
+        in_specs=[ANY] * 3,
+        out_specs=[ANY] * 2,
+        scratch_shapes=merge_scratch(blocks) + [DMA((2,)), DMA((2,))],
         compiler_params=pltpu.CompilerParams(
             collective_id=collective_id, has_side_effects=True
         ),
-    )(blocks)
+    )(blocks, rows_x, rows_y)
 
 
 def spread_kernel(
@@ -523,8 +672,11 @@
     held,
     twin,
     line,
+    part_added,
+    part_own,
     part_send,
     part_recv,
+    part_load,
     part_local,
     held_sem,
     twin_send,
@@ -610,9 +762,13 @@
     for d in range(n_seq):
         to_twin(d).start()
         load(d).start()
-    part_copies = start_exchange(n_plane, parts, parts_all, part_send, part_recv, part_local)
+    part_sems = (part_send, part_recv, part_load, part_local)
+    merge = Merge(parts, parts_all, part_added, part_own, part_sems)
+    merge.start()
     never = s < 0
     for hop in range(1, n_seq):
+        if hop == 2:
+            merge.pass_on()
         left = hop - n_seq + s
         right = n_seq - hop + s
 
@@ -648,8 +804,7 @@
         def _():
             to_right(d).wait_send()
 
-    for copy in part_copies:
-        copy.wait()
+    merge.finish()
     for copy in swaps:
         copy.wait()
     own.wait()
@@ -662,7 +817,7 @@
     return pl.pallas_call(
         partial(last_kernel, n_seq, n_plane),
         out_shape=[
-            jax.ShapeDtypeStruct(parts.shape, parts.dtype),
+            merged_shape(parts),
             jax.ShapeDtypeStruct(block, blocks.dtype),
         ],
         in_specs=[ANY, ANY],
@@ -671,9 +826,7 @@
             pltpu.VMEM((n_seq,) + block, blocks.dtype),
             pltpu.VMEM((n_seq,) + block, blocks.dtype),
             pltpu.VMEM((n_seq + 1,) + block, blocks.dtype),
-            DMA((n_plane,)),
-            DMA((n_plane,)),
-            DMA((1,)),
+            *merge_scratch(parts),
             DMA((n_seq,)),
             DMA((n_seq,)),
             DMA((n_seq,)),
@@ -781,11 +934,15 @@
     return c ^ flip
 
 
-def chip_places(rows):
+LATE = 3
+
+
+def chip_places(rows, late_rows):
     q = lax.axis_index("chip")
     x, y = lax.rem(q, 2), lax.div(q, 2)
     across = (2 * (1 - y) + 1 - x) * rows
-    return (q * rows, (2 * y + 1 - x) * rows, (2 * (1 - y) + x) * rows, across, across + rows // 2)
+    half = (rows - late_rows) // 2
+    return (q * rows, (2 * y + 1 - x) * rows, (2 * (1 - y) + x) * rows, across, across + half)
 
 
 def send_beside(part, flip):
@@ -841,24 +998,28 @@
 def units_kernel(n_seq, backward, *refs):
     if backward:
         tokens, units = refs[:2]
-        downs = refs[2:7]
-        kept_gate, kept_up, kept_hidden = refs[7:10]
-        out, first_out, second_out, down_grads = refs[10:14]
+        downs, late = refs[2:7], refs[7]
+        kept_gate, kept_up, kept_hidden = refs[8:11]
+        out, first_out, second_out, down_grads = refs[11:15]
         stage_outs = (first_out, second_out)
-        scratch = refs[14:]
+        scratch = refs[15:]
     else:
         tokens, units = refs[:2]
         downs = refs[2:7]
-        out, tokens_all, first_out, second_out, third_out = refs[7:12]
+        out, tokens_all, late, first_out, second_out, third_out = refs[7:13]
         stage_outs = (first_out, second_out, third_out)
-        scratch = refs[12:]
+        scratch = refs[13:]
     units_v, downs_v, held, own_sum, twin_sum, twin_out, line, stage = scratch[:8]
     scratch = scratch[8:]
     if backward:
         kept, kept_sem, tile, tile_sem, load_sem = scratch[:5]
         scratch = scratch[5:]
+    else:
+        own_hidden, late_send, late_recv = scratch[:3]
+        scratch = scratch[3:]
     (
         weight_sem,
+        late_sem,
         own_sem,
         left_send,
         right_send,
@@ -961,7 +1122,39 @@
     def _():
         pl.semaphore_signal(barrier, inc=1, device_id={"seq": s + 1}, device_id_type=MESH)
 
-    pl.semaphore_wait(barrier, 1 + jnp.where(s > 0, 1, 0) + jnp.where(s < n - 1, 1, 0))
+    greeted = 1 + jnp.where(s > 0, 1, 0) + jnp.where(s < n - 1, 1, 0)
+    n_chip, late_rows = late.shape[:2]
+    chip_rows = n_units // n_chip
+    q = lax.axis_index("chip")
+    if not backward:
+        for step in range(1, n_chip):
+            pl.semaphore_signal(
+                barrier,
+                inc=1,
+                device_id={"chip": lax.rem(q + step, n_chip)},
+                device_id_type=MESH,
+            )
+        greeted = greeted + n_chip - 1
+    pl.semaphore_wait(barrier, greeted)
+
+    def late_place(chip):
+        first = chip * chip_rows + chip_rows - late_rows
+        return downs_v.at[pl.ds(pl.multiple_of(first, 16), late_rows)]
+
+    def late_copy(step):
+        return remote(
+            downs[0].at[pl.ds(chip_rows - late_rows, late_rows)],
+            late_place(q),
+            late_send.at[step],
+            late_recv.at[step],
+            {"chip": lax.rem(q + step, n_chip)},
+        )
+
+    def late_store(chip):
+        return pltpu.make_async_copy(late_place(chip), late.at[chip], late_sem.at[chip])
+
+    def late_load(chip):
+        return pltpu.make_async_copy(late.at[chip], late_place(chip), late_sem.at[chip])
 
     def second_half(t):
         @pl.when((s < n - 1) & (t == pick(right_table, 0, s)))
@@ -989,9 +1182,20 @@
         own_load(h).start()
     load_units = pltpu.make_async_copy(units, units_v, weight_sem.at[0])
     load_downs = []
-    for i, (first, part) in enumerate(zip(chip_places(downs[0].shape[0]), downs)):
-        rows = pl.ds(pl.multiple_of(first, 16), part.shape[0])
-        load_downs.append(pltpu.make_async_copy(part, downs_v.at[rows], weight_sem.at[1 + i]))
+    for i, (first, part) in enumerate(zip(chip_places(chip_rows, late_rows), downs)):
+        count = chip_rows - late_rows if i == 0 and backward else part.shape[0]
+        load_downs.append(
+            pltpu.make_async_copy(
+                part.at[pl.ds(0, count)],
+                downs_v.at[pl.ds(pl.multiple_of(first, 16), count)],
+                weight_sem.at[1 + i],
+            )
+        )
+    if backward:
+        load_downs += [late_load(chip) for chip in range(n_chip)]
+    else:
+        for step in (2, 1, 3):
+            late_copy(step).start()
     load_units.start()
     for load in load_downs:
         load.start()
@@ -1040,7 +1244,7 @@
     columns = width // 3
     chunk = n_units // 3
 
-    def compute_forward(d, h, slot):
+    def hidden_forward(d, h, slot):
         rows = held[d, h].reshape(2 * piece_len, width)
         for c in range(3):
             cols = slice(c * chunk, (c + 1) * chunk)
@@ -1050,11 +1254,17 @@
             stage[0, slot, :, cols] = gate.astype(stage.dtype)
             stage[1, slot, :, cols] = up.astype(stage.dtype)
             stage[2, slot, :, cols] = (value * up).astype(stage.dtype)
+
+    def down_forward(d, h, hidden):
         for c in range(3):
             cols = slice(c * columns, (c + 1) * columns)
-            part = add_slice(stage[2, slot], downs_v[:, cols])
+            part = add_slice(hidden[...], downs_v[:, cols])
             own_sum[d, h, :, cols] = part[:piece_len]
             twin_out[d, h, :, cols] = part[piece_len:].astype(twin_out.dtype)
+        part_twin(d, h).start()
+
+    def own_forward(h):
+        down_forward(s, h, own_hidden.at[h])
 
     def compute_backward(d, h, slot):
         rows = held[d, h].reshape(2 * piece_len, width)
@@ -1173,9 +1383,23 @@
         token_twin(d, h, held.at[d, h, 0]).wait_recv()
         if backward:
             compute_backward(d, h, slot)
+            part_twin(d, h).start()
         else:
-            compute_forward(d, h, slot)
-        part_twin(d, h).start()
+            hidden_forward(d, h, slot)
+
+            @pl.when(t < 2)
+            def _():
+                own_hidden[slot] = stage[2, slot]
+
+            @pl.when(t == 2)
+            def _():
+                for step in range(1, n_chip):
+                    late_copy(step).wait_recv()
+
+            @pl.when(t >= 2)
+            def _():
+                down_forward(d, h, stage.at[2, slot])
+
         if not backward:
             all_store(d, h).start()
         for i in range(len(stage_outs)):
@@ -1203,8 +1427,16 @@
         down_gradient(middle)
     else:
 
+        for chip in range(n_chip):
+            late_store(chip).start()
+
         def one(i, carry):
             middle(i)
+
+            @pl.when((i == 1) | (i == 2))
+            def _():
+                own_forward(i - 1)
+
             return carry
 
         lax.fori_loop(0, n_sums, one, 0)
@@ -1267,6 +1499,11 @@
         return carry
 
     lax.fori_loop(0, 2 * n, drain, 0)
+    if not backward:
+        for step in range(1, n_chip):
+            late_copy(step).wait_send()
+        for chip in range(n_chip):
+            late_store(chip).wait()
     for h in range(2):
         for i in range(len(stage_outs)):
             stage_store(i, 0, h, h).wait()
@@ -1293,6 +1530,7 @@
         pltpu.VMEM((n_stage, 2) + unit_rows[1:], low),
     ]
     outs = [jax.ShapeDtypeStruct(tokens.shape, jnp.float32)]
+    late_shape = (KV_HEADS, downs[0].shape[0] // LATE, width)
     if backward:
         scratch += [
             pltpu.VMEM((2, 2) + unit_rows[1:], low),
@@ -1302,12 +1540,13 @@
             DMA((2 * n_seq,)),
         ]
     else:
-        outs += [jax.ShapeDtypeStruct(held, low)]
+        scratch += [pltpu.VMEM((2,) + unit_rows[1:], low), DMA((KV_HEADS,)), DMA((KV_HEADS,))]
+        outs += [jax.ShapeDtypeStruct(held, low), jax.ShapeDtypeStruct(late_shape, low)]
     outs += [jax.ShapeDtypeStruct(unit_rows, low)] * n_stage
     if backward:
         outs += [jax.ShapeDtypeStruct((n_units, width), low)]
     pairs = DMA((n_seq, halves))
-    scratch += [DMA((1 + len(downs),)), DMA((halves,))] + [pairs] * 7
+    scratch += [DMA((6,)), DMA((KV_HEADS,)), DMA((halves,))] + [pairs] * 7
     scratch += [DMA((n_seq, halves, SUBS)), DMA((n_seq + 1, halves, SUBS))]
     scratch += [DMA((n_stage, 2)), pairs, DMA((halves,))]
     operands = (tokens, units) + tuple(downs) + (tuple(kept) if backward else ())
@@ -1578,7 +1817,8 @@
     hidden_all, blocks_all = gather_first(n_seq, hidden_in, blocks)
     unit_weights = lax.all_gather(gate_up_weight, "chip", axis=0, tiled=True)
     blocks_all, down_weight = lax.optimization_barrier((blocks_all, down_weight))
-    down_x, down_y = send_beside(down_weight, 1), send_beside(down_weight, 2)
+    early = down_weight.shape[0] - down_weight.shape[0] // LATE
+    down_x, down_y = send_beside(down_weight[:early], 1), send_beside(down_weight[:early], 2)
     blocks_all = blocks_all.transpose(0, 2, 1, 3, 4)
     own_weights = blocks_all[:, :, :, :weight_rows].reshape(model_width, block_width)
     own_qkv = own_weights[:, :part_width]
@@ -1620,22 +1860,13 @@
     segment_row = jnp.where(valid == 1, segment, -1)[None, :]
     attn_out = attend(queries, keys, values, segment_col, segment_row)
     proj_parts = times_rows(attn_out, own_out).astype(jnp.bfloat16)
-    proj_parts, down_x, down_y = lax.optimization_barrier((proj_parts, down_x, down_y))
-    half = down_weight.shape[0] // 2
-    down_units = (
-        down_weight,
-        down_x,
-        down_y,
-        send_beside(down_x[:half], 2),
-        send_beside(down_y[half:], 1),
-    )
-    proj_parts = plane_exchange(
-        proj_parts.reshape(n_plane, piece_len, model_width), 2
-    )
+    proj_parts, down_across = merge_plane(
+        proj_parts.reshape(n_plane, piece_len, model_width), down_x, down_y, 2
+    )
+    down_units = (down_weight, down_x, down_y, down_across[0], down_across[1])
 
     def sum_parts(parts):
-        parts = parts.reshape(n_chip, groups, piece_len, model_width).astype(jnp.float32)
-        return jnp.sum(parts, axis=0).reshape(row_count, model_width)
+        return jnp.sum(parts.astype(jnp.float32), axis=0).reshape(row_count, model_width)
 
     attn_proj = sum_parts(proj_parts)
     residual = hidden_in.reshape(row_count, model_width).astype(jnp.float32)
@@ -1643,7 +1874,7 @@
     ffn_input = rms_norm(after_attn, gain_cols[:, 2]).astype(jnp.bfloat16)
 
     pieces = (groups, piece_len, model_width)
-    down_out, ffn_all, gate_part, up_part, hidden_part = run_units(
+    down_out, ffn_all, down_late, gate_part, up_part, hidden_part = run_units(
         n_seq, ffn_input.reshape(pieces), unit_weights, down_units
     )
     down_out = down_out.reshape(row_count, model_width)
@@ -1658,7 +1889,7 @@
         grad_down.astype(jnp.bfloat16).reshape(pieces),
         unit_weights,
         down_units,
-        (gate_part, up_part, hidden_part),
+        (down_late, gate_part, up_part, hidden_part),
     )
     grad_ffn_in = grad_ffn_in.reshape(row_count, model_width)
     down_grad = lax.psum_scatter(down_rows, "chip", scatter_dimension=0, tiled=True).astype(

time: 818 us -> 781 us (0.955)
  Pallas kernels: 619 us -> 598 us
  waiting for transfers between devices: 13.5 us -> 0.72 us
    pallas_call x2, Pallas kernels: 167 us -> 146 us  [the longest x1 92.3 us: sum_last(): pl.pallas_call(partial(last_kernel, n_seq, n_plane), out_shape=[merged_sh...]
    ppermute x4 -> x2, waiting for transfers between devices: 12.8 us -> 0.01 us  [send_beside(): lax.ppermute(part, 'chip', [(c, chip_beside(c, flip)) for c in range(KV_H...]
    unnamed x115 -> x107, local copies, waits for them, and re-layouts: 23.3 us -> 21.7 us
  transfers between devices with their start and end apart: 7 -> 5, of which waited for: 4 -> 0; matrix products, arithmetic and copies ran while one was open for 16% -> 17% of each run, Pallas kernels for 43% -> 42%
where the time goes in v7:
time: 781 us; the launch traced here: 771 us
  Pallas kernels  598 us (77%)
  other arithmetic  65.1 us (8%)
  local copies, waits for them, and re-layouts  48.6 us (6%)
  matrix products  40.9 us (5%)
  between operations  15.2 us (2%)
    pallas_call x2, Pallas kernels, run_units(): pl.pallas_call(partial(units_kernel, n_seq, backward), out_shape=outs, in...  272 us
    pallas_call x1, Pallas kernels, gather_first(): pl.pallas_call(partial(gather_kernel, n_seq, n_plane), out_shape=[jax.Sha...  97.2 us
    pallas_call x1, Pallas kernels, sum_last(): pl.pallas_call(partial(last_kernel, n_seq, n_plane), out_shape=[merged_sh...  92.3 us
    pallas_call x1, Pallas kernels, spread_plane(): pl.pallas_call(partial(spread_kernel, n_plane), out_shape=[jax.ShapeDtype...  72 us
    pallas_call x1, Pallas kernels, merge_plane(): pl.pallas_call(partial(merge_kernel, 2 * KV_HEADS), out_shape=[merged_sha...  53.3 us
    unnamed x107, local copies, waits for them, and re-layouts  21.7 us
    dot_general x2, matrix products, times_rows(): lax.dot_general(left, weight_piece, (((1,), (1,)), ((), ())), preferred_e...  16.4 us
  transfers between devices with their start and end apart: 5, of which 0 were waited for; matrix products, arithmetic and copies ran while one was open for 17% of the time, Pallas kernels for 42%

profile of v7, /device:TPU:0, one launch (start us, length us, event | category | flops | bytes accessed | tf_op | source)
XLA Modules:
  0.0 771.0 jit_solution(7187936242161590040)
XLA Ops:
  7.2 0.7 all-gather.2.cloned.1.call-update
  8.5 1.1 pad_maximum_fusion.4.blocks
  9.5 97.2 %shard_map.144 = (bf16[8,128,2304]{2,1,0:T(8,128)(2,1)}, bf16[4,2,4,80,1536]{4,3,2,1,0:T(8,128)(2,1)}) custom-call(bf16[2,128,2304]{2,1,0:T(8,128)(2,1)} %hidden.1, bf16[4,80,1536]{2,1,0:T(8,128)(2,1)} %pad_maximum_fusion.4.blocks), custom_call_target="tpu_custom_call" | custom-call | tf_op jit(solution)/shard_map/pallas_call | solution.py:640
  106.8 1.0 slice.202
  108.4 1.4 collective-permute-start
  109.8 3.7 slice.232
  113.5 3.8 copy.35
  117.3 0.8 convert_bitcast_fusion
  118.5 3.5 fusion.1
  122.0 3.6 fusion.3
  125.7 5.3 fusion.10
  130.9 0.9 slice.240
  131.8 1.1 slice.237
  133.9 1.2 copy.51.values
  135.1 2.7 copy.50
  137.8 1.4 fusion.72
  139.3 1.7 copy.49
  141.0 1.5 copy.48
  142.5 0.8 select_reduce_fusion
  143.3 1.9 multiply_cosine_fusion.1
  145.2 0.8 copy-done.27
  146.0 1.2 subtract_convert_fusion.1
  147.2 1.1 pad_maximum_fusion.2
  148.6 2.4 fusion.45
  151.1 3.9 shard_map.145
  155.0 6.3 convolution_convert_fusion
  161.3 53.3 %shard_map.146 = (bf16[3,2,128,2304]{3,2,1,0:T(8,128)(2,1)}, bf16[2,96,2304]{2,1,0:T(8,128)(2,1)}) custom-call(bf16[8,128,2304]{2,1,0:T(8,128)(2,1)} %bitcast.138, bf16[192,2304]{1,0:T(8,128)(2,1)} %collective-permute-done.rows_x.refs_3_, bf16[192,2304]{1,0:T(8,128)(2,1)} %collective-permute-done.1.rows_y.refs_4_), custom_call_target="tpu_custom_call" | custom-call | tf_op jit(solution)/shard_map/pallas_call | solution.py:404
  214.7 2.8 convert_reduce_fusion.1
  217.8 1.9 copy-done.21
  220.8 1.2 slice_bitcast_fusion
  222.0 1.3 multiply_convert_fusion.refs_0_
  223.3 133.4 %shard_map.147 = (f32[2,128,2304]{2,1,0:T(8,128)}, bf16[4,2,2,128,2304]{4,3,2,1,0:T(8,128)(2,1)}, bf16[4,96,2304]{2,1,0:T(8,128)(2,1)}, bf16[8,256,1152]{2,1,0:T...) custom-call(bf16[2,128,2304]{2,1,0:T(8,128)(2,1)} %multiply_convert_fusion.refs_0_, ...), custom_call_target="tpu_custom_call" | custom-call | tf_op jit(solution)/shard_map/pallas_call | solution.py:1553
  356.7 2.1 multiply_reduce_fusion.4
  359.1 2.2 fusion.15
  361.3 3.2 fusion.16
  364.5 138.5 %shard_map.148 = (f32[2,128,2304]{2,1,0:T(8,128)}, bf16[8,256,1152]{2,1,0:T(8,128)(2,1)}, bf16[8,256,1152]{2,1,0:T(8,128)(2,1)}, bf16[1152,2304]{1,0:T(8,128)(2,1)}) custom-call(bf16[2,128,2304]{2,1,0:T(8,128)(2,1)} %get-tuple-element.76.refs_0_, bf16[1152,4608]{1,0:T(8,128)(2,1)} %all-gather.2.cloned.1.call-done.refs_1_, bf16[288,2304]{1,0:T(8,128)(2,1)} %refs_2_.1, ...), custom_call_target="tpu_custom_call" | custom-call | tf_op jit(solution)/shard_map/pallas_call | solution.py:1553
  503.1 1.6 copy-done.17
  504.6 2.6 multiply_reduce_fusion
  507.3 3.1 multiply_reduce_fusion.1
  510.9 0.9 copy-done.19
  511.8 72.0 %shard_map.149 = (bf16[8,128,2304]{2,1,0:T(8,128)(2,1)S(1)}, bf16[1152,4608]{1,0:T(8,128)(2,1)}) custom-call(bf16[2,128,2304]{2,1,0:T(8,128)(2,1)S(1)} %fusion.17.blocks, bf16[8,256,1152]{2,1,0:T(8,128)(2,1)} %get-tuple-element.42.low_gate, bf16[8,256,1152]{2,1,0:T(8,128)(2,1)} %get-tuple-element.43.low_up, ...), custom_call_target="tpu_custom_call" | custom-call | tf_op jit(solution)/shard_map/pallas_call | solution.py:492
  583.8 2.2 copy-done.12
  586.4 5.8 fusion.24.grads
  592.3 7.7 shard_map.150
  600.0 1.0 copy-done.6
  601.0 1.0 copy-done.8
  602.0 2.3 reshape.556
  604.3 2.6 add_convert_fusion.1
  606.9 1.1 pad_maximum_fusion.3
  608.3 0.9 copy-done.9
  609.3 2.3 fusion.40
  611.7 6.2 convolution_convert_fusion.2
  617.9 7.3 convolution_convert_fusion.1
  625.1 5.8 pad_maximum_fusion
  630.9 10.2 %copy.42 = bf16[2304,1536]{1,0:T(8,128)(2,1)} copy(bf16[2304,1536]{0,1:T(8,128)(2,1)} %pad_maximum_fusion) | data formatting | bytes 14155776 | tf_op jit(solution)/shard_map/concatenate | solution.py:1928
  641.1 10.1 %fusion.5 = (bf16[2304]{0:T(1024)(128)(2,1)S(1)}, bf16[1024,2304]{1,0:T(8,128)(2,1)}) fusion(bf16[8,128,2304]{2,1,0:T(8,128)(2,1)} %get-tuple-element.30, f32[1024]{0:T(1024)S(1)} %rsqrt_bitcast_fusion, bf16[2304,1536]{1,0:T(8,128)(2,1)} %bitcast.130, bf16[1024,256]{1,0:T(8,128)(2,1)S(1)} %convert.64, bf16[1024,256]{1,0:T(8,128)(2,1)S(1)} %maximum_bitcast_fusion, ...), kind=kOutput, calls=%fused_computation.9 | convolution fusion | flops 4849924096 | bytes 16261632 | tf_op jit(solution)/shard_map/dot_general | solution.py:99
  651.5 5.2 fusion.7.blocks
  656.7 92.3 %shard_map.151 = (bf16[3,2,128,2304]{3,2,1,0:T(8,128)(2,1)S(1)}, bf16[4,80,1536]{2,1,0:T(8,128)(2,1)S(1)}) custom-call(bf16[8,128,2304]{2,1,0:T(8,128)(2,1)S(1)} %bitcast.122, bf16[4,2,4,80,1536]{4,3,2,1,0:T(8,128)(2,1)S(1)} %fusion.7.blocks), custom_call_target="tpu_custom_call" | custom-call | tf_op jit(solution)/shard_map/pallas_call | solution.py:817
  750.2 0.7 copy-done.22
  752.1 0.9 pad_maximum_fusion.7
  752.9 1.2 copy-done.20
  754.1 2.1 fusion.18
  756.2 3.0 convert_element_type.143
  759.2 4.8 convert_element_type.142
  (148 shorter events, 8.3 us)
Async XLA Ops:
  7.2 1.1 copy-start.33
  7.2 1.1 copy-start.34
  7.2 1.2 copy-start.36
  7.2 216.1 %all-gather.2.cloned.1.call-start = ((), (), s32[]{:S(2)}) async-start(), calls=%async_computation.2 | async-start | bytes 13271040 | tf_op jit(solution)/shard_map/all_gather | solution.py:1818
  7.9 748.3 %reduce-scatter.5.cloned.1.call-start = ((), (), s32[]{:S(2)}) async-start(), calls=%async_computation.4 | async-start | bytes 6635520 | tf_op jit(solution)/shard_map/reduce_scatter | solution.py:1895
  8.5 98.3 %copy-start.25 = (bf16[288,2304]{1,0:T(8,128)(2,1)S(1)}, bf16[288,2304]{1,0:T(8,128)(2,1)}, u32[]{:S(2)}) copy-start(bf16[288,2304]{1,0:T(8,128)(2,1)} %refs_2_.1) | copy-start | bytes 3981316
  107.8 53.5 %collective-permute-start.1 = (bf16[192,2304]{1,0:T(8,128)(2,1)}, bf16[192,2304]{1,0:T(8,128)(2,1)}, u32[]{:S(2)}, u32[]{:S(2)}) collective-permute-start(bf16[192,2304]{1,0:T(8,128)(2,1)} %slice.202), channel_id=1, source_target_pairs={{0,4},{2,6},{4,0},{6,2},{1,5},{3,7},{5,1},{7,3},{8,12},{10,14},{12... | collective-permute-start | bytes 2654216 | tf_op jit(solution)/shard_map/ppermute | solution.py:949
  108.4 52.9 %collective-permute-start = (bf16[192,2304]{1,0:T(8,128)(2,1)}, bf16[192,2304]{1,0:T(8,128)(2,1)}, u32[]{:S(2)}, u32[]{:S(2)}) collective-permute-start(bf16[192,2304]{1,0:T(8,128)(2,1)} %slice.202), channel_id=1, source_target_pairs={{0,2},{2,0},{4,6},{6,4},{1,3},{3,1},{5,7},{7,5},{8,10},{10,8},{12,... | collective-permute-start | bytes 2654216 | tf_op jit(solution)/shard_map/ppermute | solution.py:949
  118.5 7.2 slice-start.2
  122.0 3.7 slice-start.3
  125.6 5.3 copy-start.26
  132.9 0.7 copy-start.37
  132.9 0.7 copy-start.38
  135.1 16.0 %copy-start.2 = (bf16[1024,256]{1,0:T(8,128)(2,1)}, bf16[1024,256]{1,0:T(8,128)(2,1)S(1)}, u32[]{:S(2)}) copy-start(bf16[1024,256]{1,0:T(8,128)(2,1)S(1)} %copy.51.values) | copy-start | bytes 1572868
  145.2 0.8 copy-start.27
  145.2 2.0 copy-start.29
  147.2 1.4 copy-start.31
  148.6 6.3 copy-start
  151.1 10.2 %copy-start.4 = (bf16[1024,256]{1,0:T(8,128)(2,1)}, bf16[1024,256]{1,0:T(8,128)(2,1)S(1)}, u32[]{:S(2)}) copy-start(bf16[1024,256]{1,0:T(8,128)(2,1)S(1)} %pad_maximum_fusion.8.keys) | copy-start | bytes 1572868
  155.0 6.3 copy-start.10
  217.5 2.8 copy-start.13
  217.5 2.1 copy-start.21
  219.6 1.2 copy-start.32
  220.3 1.7 copy-start.15
  356.7 2.4 copy-start.18
  358.7 2.5 copy-start.16
  358.8 2.5 copy-start.23
  503.0 1.7 copy-start.17
  503.0 256.2 %reduce-scatter.3.cloned.1.call-start = ((), (), s32[]{:S(2)}) async-start(), calls=%async_computation.3 | async-start | bytes 13271040 | tf_op jit(solution)/shard_map/reduce_scatter | solution.py:1909
  504.6 2.6 copy-start.14
  504.6 2.7 copy-start.24
  510.4 1.4 copy-start.19
  583.8 2.2 copy-start.12
  586.4 5.9 copy-start.1
  586.4 5.9 copy-start.3
  586.4 5.9 copy-start.5
  600.0 1.0 copy-start.6
  601.0 1.0 copy-start.8
  602.0 2.3 copy-start.28
  602.0 2.3 copy-start.30
  606.9 1.4 copy-start.7
  608.0 1.2 copy-start.9
  608.3 3.4 copy-start.11
  609.3 8.6 %slice-start.4 = ((s8[4718592]{0:T(1024)(128)(4,1)}), s8[4194304]{0:T(1024)(128)(4,1)S(1)}, s32[]{:S(2)}) async-start(s8[4718592]{0:T(1024)(128)(4,1)} %bitcast.136), calls=%async_computation.9 | async-start | bytes 8388608
  611.7 6.2 slice-start.5
  651.5 5.2 slice-start
  651.5 5.2 slice-start.1
  749.7 1.3 copy-start.22
  751.8 2.3 copy-start.20
  752.0 4.2 copy-start.35
Sparse Core Ops, SparseCore 0:
  9.9 161.5 all-gather.1
  503.1 97.4 reduce-scatter.4
  603.8 136.2 reduce-scatter.2

commit v8 on v7

--- a/solution.py
+++ b/solution.py
@@ -884,6 +884,14 @@
     )(queries, keys, values, segment_col, segment_row)
 
 
+def turn_back(grads, cosine, sine_part):
+    half = grads.shape[1] // 2
+    first, second = grads[:, :half], grads[:, half:]
+    return jnp.concatenate(
+        [first * cosine + second * sine_part, second * cosine - first * sine_part], axis=1
+    )
+
+
 def attend_back_kernel(
     group_size,
     queries,
@@ -892,12 +900,16 @@
     segment_col,
     segment_row,
     grads,
-    grad_queries,
+    cosine,
+    sine_part,
+    out,
     grad_keys,
     grad_values,
 ):
     seq_len = keys.shape[0]
     inverse_root = 1.0 / math.sqrt(HEAD_DIM)
+    key_cols = slice(group_size * HEAD_DIM, (group_size + 1) * HEAD_DIM)
+    value_cols = slice((group_size + 1) * HEAD_DIM, (group_size + 2) * HEAD_DIM)
     grad_keys[...] = jnp.zeros_like(grad_keys)
     grad_values[...] = jnp.zeros_like(grad_values)
     for first in range(0, seq_len, QUERY_BLOCK):
@@ -913,21 +925,73 @@
             grad_probs = times_rows(grad, values[:width])
             mean = jnp.sum(probs * grad_probs, axis=-1, keepdims=True)
             grad_scaled = (probs * (grad_probs - mean) * (1.0 - bent * bent)).astype(jnp.bfloat16)
-            grad_queries[rows, cols] = add_slice(grad_scaled, keys[:width]) * inverse_root
+            grad_query = add_slice(grad_scaled, keys[:width]) * inverse_root
+            out[rows, cols] = turn_back(grad_query, cosine[rows, :], sine_part[rows, :]).astype(
+                out.dtype
+            )
             grad_keys[:width, :] += outer_rows(grad_scaled, query) * inverse_root
             grad_values[:width, :] += outer_rows(probs.astype(jnp.bfloat16), grad)
-
-
-def attend_back(queries, keys, values, segment_col, segment_row, grads):
+    for first in range(0, seq_len, QUERY_BLOCK):
+        rows = slice(first, first + QUERY_BLOCK)
+        out[rows, key_cols] = turn_back(
+            grad_keys[rows, :], cosine[rows, :], sine_part[rows, :]
+        ).astype(out.dtype)
+        out[rows, value_cols] = grad_values[rows, :].astype(out.dtype)
+
+
+def attend_back(queries, keys, values, segment_col, segment_row, grads, cosine, sine_part):
+    seq_len, own_width = queries.shape
     return pl.pallas_call(
-        partial(attend_back_kernel, queries.shape[1] // HEAD_DIM),
-        out_shape=[
-            jax.ShapeDtypeStruct(queries.shape, jnp.float32),
-            jax.ShapeDtypeStruct(keys.shape, jnp.float32),
-            jax.ShapeDtypeStruct(values.shape, jnp.float32),
+        partial(attend_back_kernel, own_width // HEAD_DIM),
+        out_shape=jax.ShapeDtypeStruct((seq_len, own_width + 2 * HEAD_DIM), jnp.bfloat16),
+        scratch_shapes=[
+            pltpu.VMEM((seq_len, HEAD_DIM), jnp.float32),
+            pltpu.VMEM((seq_len, HEAD_DIM), jnp.float32),
         ],
         compiler_params=pltpu.CompilerParams(vmem_limit_bytes=40 * 1024 * 1024),
-    )(queries, keys, values, segment_col, segment_row, grads)
+    )(queries, keys, values, segment_col, segment_row, grads, cosine, sine_part)
+
+
+def weight_blocks_kernel(weight_rows, inputs, grads, grad_outs, outs, gains, blocks):
+    n_first, n_core, n_chip, block_rows = blocks.shape[:4]
+    columns = outs.shape[1]
+    for c in range(blocks.shape[4] // columns):
+        cols = slice(c * columns, (c + 1) * columns)
+        if c * columns < grads.shape[1]:
+            total = outer_rows(inputs[...], grads[:, cols])
+        else:
+            total = outer_rows(grad_outs[...], outs[...])
+        for d in range(n_first):
+            for q in range(n_chip):
+                for core in range(n_core):
+                    b = (d * n_chip + q) * n_core + core
+                    part = total[b * weight_rows : (b + 1) * weight_rows]
+                    part = jnp.concatenate([part, gains[b, :, cols]], axis=0)
+                    blocks[d, core, q, :, cols] = part.astype(blocks.dtype)
+
+
+def weight_blocks(n_seq, inputs, grads, grad_outs, outs, gains):
+    seq_len, model_width = inputs.shape
+    n_blocks, extra_rows, block_width = gains.shape
+    weight_rows = model_width // n_blocks
+    steps = 2
+    part = model_width // steps
+    block = (n_seq // steps, 2, KV_HEADS, weight_rows + extra_rows, block_width)
+    whole = lambda i: (0, 0)
+    return pl.pallas_call(
+        partial(weight_blocks_kernel, weight_rows),
+        grid=(steps,),
+        out_shape=jax.ShapeDtypeStruct((n_seq,) + block[1:], jnp.bfloat16),
+        in_specs=[
+            pl.BlockSpec((seq_len, part), lambda i: (0, i)),
+            pl.BlockSpec(grads.shape, whole),
+            pl.BlockSpec((seq_len, part), lambda i: (0, i)),
+            pl.BlockSpec(outs.shape, whole),
+            pl.BlockSpec((n_blocks // steps, extra_rows, block_width), lambda i: (i, 0, 0)),
+        ],
+        out_specs=pl.BlockSpec(block, lambda i: (i, 0, 0, 0, 0)),
+        compiler_params=pltpu.CompilerParams(vmem_limit_bytes=56 * 1024 * 1024),
+    )(inputs, grads, grad_outs, outs, gains)
 
 
 def chip_beside(c, flip):
@@ -935,6 +999,7 @@
 
 
 LATE = 3
+LATE_COLUMNS = 2
 
 
 def chip_places(rows, late_rows):
@@ -1000,9 +1065,11 @@
         tokens, units = refs[:2]
         downs, late = refs[2:7], refs[7]
         kept_gate, kept_up, kept_hidden = refs[8:11]
-        out, first_out, second_out, down_grads = refs[11:15]
+        out, first_out, second_out, early_grads = refs[11:15]
+        late_grads = refs[15 : 15 + LATE_COLUMNS]
+        late_parts = refs[15 + LATE_COLUMNS : 15 + 2 * LATE_COLUMNS]
         stage_outs = (first_out, second_out)
-        scratch = refs[15:]
+        scratch = refs[15 + 2 * LATE_COLUMNS :]
     else:
         tokens, units = refs[:2]
         downs = refs[2:7]
@@ -1015,8 +1082,10 @@
         kept, kept_sem, tile, tile_sem, load_sem = scratch[:5]
         scratch = scratch[5:]
     else:
-        own_hidden, late_send, late_recv = scratch[:3]
-        scratch = scratch[3:]
+        own_hidden = scratch[0]
+        scratch = scratch[1:]
+    late_send, late_recv = scratch[:2]
+    scratch = scratch[2:]
     (
         weight_sem,
         late_sem,
@@ -1126,16 +1195,14 @@
     n_chip, late_rows = late.shape[:2]
     chip_rows = n_units // n_chip
     q = lax.axis_index("chip")
-    if not backward:
-        for step in range(1, n_chip):
-            pl.semaphore_signal(
-                barrier,
-                inc=1,
-                device_id={"chip": lax.rem(q + step, n_chip)},
-                device_id_type=MESH,
-            )
-        greeted = greeted + n_chip - 1
-    pl.semaphore_wait(barrier, greeted)
+    for step in range(1, n_chip):
+        pl.semaphore_signal(
+            barrier,
+            inc=1,
+            device_id={"chip": lax.rem(q + step, n_chip)},
+            device_id_type=MESH,
+        )
+    pl.semaphore_wait(barrier, greeted + n_chip - 1)
 
     def late_place(chip):
         first = chip * chip_rows + chip_rows - late_rows
@@ -1148,6 +1215,16 @@
             late_send.at[step],
             late_recv.at[step],
             {"chip": lax.rem(q + step, n_chip)},
+        )
+
+    def late_grad(i, step):
+        chip = lax.rem(q + step, n_chip)
+        return remote(
+            late_grads[i].at[pl.ds(pl.multiple_of(chip * chip_rows, 16), chip_rows)],
+            late_parts[i].at[q],
+            late_send.at[n_chip * i + step],
+            late_recv.at[n_chip * i + step],
+            {"chip": chip},
         )
 
     def late_store(chip):
@@ -1307,23 +1384,25 @@
 
         def tile_store(r, c, slot):
             rows = pl.ds(pl.multiple_of(r * row_tile, 16), row_tile)
-            cols = pl.ds(pl.multiple_of(c * col_tile, 128), col_tile)
-            return pltpu.make_async_copy(tile.at[slot], down_grads.at[rows, cols], tile_sem.at[slot])
+            if c < LATE_COLUMNS:
+                place = late_grads[c].at[rows]
+            else:
+                place = early_grads.at[rows, pl.ds((c - LATE_COLUMNS) * col_tile, col_tile)]
+            return pltpu.make_async_copy(tile.at[slot], place, tile_sem.at[slot])
 
         for u in range(2 * n):
             left_load(u).start()
         for u in range(2 * n):
             left_load(u).wait()
 
-        def one_tile(j, carry):
-            slot = lax.rem(j, 2)
-            r, c = lax.div(j, 3), lax.rem(j, 3)
+        def one_tile(c, r, carry):
+            slot = lax.rem(r, 2)
             total = sum(
                 outer_rows(left_rows(g, r * row_tile), right_rows(g, c * col_tile))
                 for g in range(2)
             )
 
-            @pl.when(j >= 2)
+            @pl.when(r >= 2)
             def _():
                 tile_store(r, c, slot).wait()
 
@@ -1331,15 +1410,19 @@
             tile_store(r, c, slot).start()
             for step, turn in enumerate(SUM_TURNS):
 
-                @pl.when(j == turn)
+                @pl.when(3 * c + r == turn)
                 def _():
                     between(step)
 
             return carry
 
-        lax.fori_loop(0, 9, one_tile, 0)
-        for slot in range(2):
-            tile_store(0, 0, slot).wait()
+        for c in range(3):
+            lax.fori_loop(0, 3, partial(one_tile, c), 0)
+            for slot in range(2):
+                tile_store(0, c, slot).wait()
+            if c < LATE_COLUMNS:
+                for step in (2, 1, 3):
+                    late_grad(c, step).start()
 
     def unit(t, carry):
         d, h = source(t)
@@ -1499,7 +1582,11 @@
         return carry
 
     lax.fori_loop(0, 2 * n, drain, 0)
-    if not backward:
+    if backward:
+        for i in range(LATE_COLUMNS):
+            for step in range(1, n_chip):
+                late_grad(i, step).wait()
+    else:
         for step in range(1, n_chip):
             late_copy(step).wait_send()
         for chip in range(n_chip):
@@ -1540,11 +1627,16 @@
             DMA((2 * n_seq,)),
         ]
     else:
-        scratch += [pltpu.VMEM((2,) + unit_rows[1:], low), DMA((KV_HEADS,)), DMA((KV_HEADS,))]
+        scratch += [pltpu.VMEM((2,) + unit_rows[1:], low)]
         outs += [jax.ShapeDtypeStruct(held, low), jax.ShapeDtypeStruct(late_shape, low)]
     outs += [jax.ShapeDtypeStruct(unit_rows, low)] * n_stage
     if backward:
-        outs += [jax.ShapeDtypeStruct((n_units, width), low)]
+        column = width // 3
+        outs += [jax.ShapeDtypeStruct((n_units, (3 - LATE_COLUMNS) * column), low)]
+        outs += [jax.ShapeDtypeStruct((n_units, column), low)] * LATE_COLUMNS
+        parts = (KV_HEADS, n_units // KV_HEADS, column)
+        outs += [jax.ShapeDtypeStruct(parts, low)] * LATE_COLUMNS
+    scratch += [DMA((KV_HEADS * LATE_COLUMNS,)), DMA((KV_HEADS * LATE_COLUMNS,))]
     pairs = DMA((n_seq, halves))
     scratch += [DMA((6,)), DMA((KV_HEADS,)), DMA((halves,))] + [pairs] * 7
     scratch += [DMA((n_seq, halves, SUBS)), DMA((n_seq + 1, halves, SUBS))]
@@ -1884,7 +1976,7 @@
     cotangent = output_cotangent.reshape(row_count, model_width).astype(jnp.float32)
     unused_last, pull_last = jax.vjp(rms_norm, down_out, gain_cols[:, 3])
     grad_down, grad_gain_last = pull_last(cotangent)
-    grad_ffn_in, gate_low, up_low, down_rows = run_units(
+    grad_ffn_in, gate_low, up_low, early_rows, *late = run_units(
         n_seq,
         grad_down.astype(jnp.bfloat16).reshape(pieces),
         unit_weights,
@@ -1892,9 +1984,17 @@
         (down_late, gate_part, up_part, hidden_part),
     )
     grad_ffn_in = grad_ffn_in.reshape(row_count, model_width)
-    down_grad = lax.psum_scatter(down_rows, "chip", scatter_dimension=0, tiled=True).astype(
-        jnp.float32
-    )
+    chip = lax.axis_index("chip")
+    chips = jnp.arange(n_chip, dtype=jnp.int32)[:, None, None]
+    down_columns = []
+    for grads, parts in zip(late[:LATE_COLUMNS], late[LATE_COLUMNS:]):
+        own = lax.dynamic_slice_in_dim(grads, chip * parts.shape[1], parts.shape[1], 0)
+        parts = jnp.where(chips == chip, own[None], parts)
+        down_columns.append(jnp.sum(parts.astype(jnp.float32), axis=0))
+    if LATE_COLUMNS < 3:
+        early_grad = lax.psum_scatter(early_rows, "chip", scatter_dimension=0, tiled=True)
+        down_columns.append(early_grad.astype(jnp.float32))
+    down_grad = jnp.concatenate(down_columns, axis=1)
 
     unused_mid, pull_mid = jax.vjp(rms_norm, after_attn, gain_cols[:, 2])
     grad_after_ffn, grad_gain_mid = pull_mid(grad_ffn_in)
@@ -1911,39 +2011,30 @@
     ).astype(jnp.float32)
     grad_proj_all = grad_proj_all.reshape(seq_len, model_width)
     grad_attn = add_slice(grad_proj_all, own_out).astype(jnp.bfloat16)
-    grad_query_rot, grad_key_rot, grad_values = attend_back(
-        queries, keys, values, segment_col, segment_row, grad_attn
-    )
-    grad_queries = rotate_back(
-        grad_query_rot.reshape(seq_len, group_size, HEAD_DIM), cosine, sine_part
-    ).reshape(seq_len, own_width)
-    grad_keys = rotate_back(
-        grad_key_rot.reshape(seq_len, 1, HEAD_DIM), cosine, sine_part
-    ).reshape(seq_len, HEAD_DIM)
-    grad_projected = jnp.concatenate([grad_queries, grad_keys, grad_values], axis=1).astype(
-        jnp.bfloat16
+    grad_projected = attend_back(
+        queries,
+        keys,
+        values,
+        segment_col,
+        segment_row,
+        grad_attn,
+        cosine[:, 0],
+        sine_part[:, 0],
     )
     grad_in_part = times_rows(grad_projected, own_qkv)
     grad_gain_first = jnp.sum(grad_in_part * seq_rows * seq_factor, axis=0)
-    weight_part = jnp.concatenate(
-        [
-            outer_rows(attn_input, grad_projected).astype(jnp.bfloat16),
-            outer_rows(grad_proj_all, attn_out).astype(jnp.bfloat16),
-        ],
-        axis=1,
-    ).reshape(n_seq, n_chip, 2, weight_rows, block_width)
     gain_terms = (
         jnp.stack([grad_gain_first, grad_gain_post, grad_gain_mid, grad_gain_last])
-        .astype(jnp.bfloat16)
-        .reshape(-1, n_seq, n_chip, 2, weight_rows)
-        .transpose(1, 2, 3, 0, 4)
+        .reshape(-1, n_seq * n_plane, weight_rows)
+        .transpose(1, 0, 2)
     )
     gain_terms = jnp.pad(
         gain_terms,
-        ((0, 0),) * 3
-        + ((0, extra_rows - gain_terms.shape[3]), (0, block_width - weight_rows)),
-    )
-    grad_blocks = jnp.concatenate([weight_part, gain_terms], axis=3).transpose(0, 2, 1, 3, 4)
+        ((0, 0), (0, extra_rows - gain_terms.shape[1]), (0, block_width - weight_rows)),
+    )
+    grad_blocks = weight_blocks(
+        n_seq, attn_input, grad_projected, grad_proj_all, attn_out, gain_terms
+    )
     grad_in_parts, grad_sums = sum_last(
         n_seq,
         grad_in_part.astype(jnp.bfloat16).reshape(n_plane, piece_len, model_width),

time: 781 us -> 759 us (0.972)
  other arithmetic: 65.1 us -> 45.7 us
  Pallas kernels: 598 us -> 616 us
  matrix products: 40.9 us -> 27.8 us
    pallas_call x1, Pallas kernels: 72 us -> 50 us  [spread_plane(): pl.pallas_call(partial(spread_kernel, n_plane), out_shape=[jax.ShapeDtype...]
    pallas_call x2, Pallas kernels: 272 us -> 294 us  [run_units(): pl.pallas_call(partial(units_kernel, n_seq, backward), out_shape=outs, in...]
    pallas_call x1 -> x2, Pallas kernels: 7.71 us -> 22.4 us  [the longest x1 14.8 us: weight_blocks(): pl.pallas_call(partial(weight_blocks_kernel, weight_rows), grid=(steps,),...]
    dot_general x2 -> x0, matrix products: 13.4 us -> none  [outer_rows(): lax.dot_general(left, right, (((0,), (0,)), ((), ())), preferred_element_...]
    concatenate x1 -> x0, local copies, waits for them, and re-layouts: 10.2 us -> none  [per_device_by_heads(): jnp.concatenate([outer_rows(attn_input, grad_projected).astype(jnp.bfloat...]
    unnamed x107 -> x104, local copies, waits for them, and re-layouts: 21.7 us -> 22.1 us
  transfers between devices with their start and end apart: 5 -> 5, of which waited for: 0 -> 0; matrix products, arithmetic and copies ran while one was open for 17% -> 12% of each run, Pallas kernels for 42% -> 43%
where the time goes in v8:
time: 759 us; the launch traced here: 751 us
  Pallas kernels  616 us (81%)
  other arithmetic  45.7 us (6%)
  local copies, waits for them, and re-layouts  43.3 us (6%)
  matrix products  27.8 us (4%)
  between operations  14.9 us (2%)
    pallas_call x2, Pallas kernels, run_units(): pl.pallas_call(partial(units_kernel, n_seq, backward), out_shape=outs, in...  294 us
    pallas_call x1, Pallas kernels, gather_first(): pl.pallas_call(partial(gather_kernel, n_seq, n_plane), out_shape=[jax.Sha...  97.2 us
    pallas_call x1, Pallas kernels, sum_last(): pl.pallas_call(partial(last_kernel, n_seq, n_plane), out_shape=[merged_sh...  95 us
    pallas_call x1, Pallas kernels, merge_plane(): pl.pallas_call(partial(merge_kernel, 2 * KV_HEADS), out_shape=[merged_sha...  53.9 us
    pallas_call x1, Pallas kernels, spread_plane(): pl.pallas_call(partial(spread_kernel, n_plane), out_shape=[jax.ShapeDtype...  50 us
    unnamed x104, local copies, waits for them, and re-layouts  22.1 us
    dot_general x2, matrix products, times_rows(): lax.dot_general(left, weight_piece, (((1,), (1,)), ((), ())), preferred_e...  16.9 us
  transfers between devices with their start and end apart: 5, of which 0 were waited for; matrix products, arithmetic and copies ran while one was open for 12% of the time, Pallas kernels for 43%

profile of v8, /device:TPU:0, one launch (start us, length us, event | category | flops | bytes accessed | tf_op | source)
XLA Modules:
  0.0 750.5 jit_solution(10925030024152113278)
XLA Ops:
  7.2 0.7 all-gather.2.cloned.1.call-update
  8.5 1.1 pad_maximum_fusion.2.blocks
  9.5 97.2 %shard_map.144 = (bf16[8,128,2304]{2,1,0:T(8,128)(2,1)}, bf16[4,2,4,80,1536]{4,3,2,1,0:T(8,128)(2,1)}) custom-call(bf16[2,128,2304]{2,1,0:T(8,128)(2,1)} %hidden.1, bf16[4,80,1536]{2,1,0:T(8,128)(2,1)} %pad_maximum_fusion.2.blocks), custom_call_target="tpu_custom_call" | custom-call | tf_op jit(solution)/shard_map/pallas_call | solution.py:640
  106.8 1.0 slice.190
  107.8 1.2 collective-permute-start
  109.0 0.8 collective-permute-start.1
  109.8 6.5 slice.216
  116.3 0.8 convert_bitcast_fusion
  117.4 6.9 copy.29
  124.4 1.0 fusion
  125.4 1.1 fusion.2.inputs
  126.6 1.1 slice-done.5
  127.8 5.1 fusion.7
  133.0 1.9 copy-done.28
  134.9 0.9 slice.224
  136.0 1.1 copy.37
  137.1 0.6 copy.36
  137.8 0.8 select_reduce_fusion
  138.6 1.9 multiply_cosine_fusion.1
  140.5 1.2 subtract_convert_fusion
  141.7 0.8 copy-done.9
  142.5 1.1 pad_maximum_fusion.1
  143.9 1.3 copy.38
  145.2 1.2 copy.39.values
  146.7 3.9 fusion.34
  150.7 3.7 shard_map.145.outs
  154.4 6.3 convolution_convert_fusion
  160.8 53.9 %shard_map.146 = (bf16[3,2,128,2304]{3,2,1,0:T(8,128)(2,1)}, bf16[2,96,2304]{2,1,0:T(8,128)(2,1)}) custom-call(bf16[8,128,2304]{2,1,0:T(8,128)(2,1)} %bitcast.126, bf16[192,2304]{1,0:T(8,128)(2,1)} %collective-permute-done.rows_x.refs_3_, bf16[192,2304]{1,0:T(8,128)(2,1)} %collective-permute-done.1.rows_y.refs_4_), custom_call_target="tpu_custom_call" | custom-call | tf_op jit(solution)/shard_map/pallas_call | solution.py:404
  214.7 2.8 convert_reduce_fusion.1
  217.7 1.9 copy-done.22
  219.6 0.6 multiply_reduce_fusion.5
  220.7 1.2 slice_bitcast_fusion
  221.9 1.3 multiply_convert_fusion.refs_0_
  223.2 133.3 %shard_map.147 = (f32[2,128,2304]{2,1,0:T(8,128)}, bf16[4,2,2,128,2304]{4,3,2,1,0:T(8,128)(2,1)}, bf16[4,96,2304]{2,1,0:T(8,128)(2,1)}, bf16[8,256,1152]{2,1,0:T...) custom-call(bf16[2,128,2304]{2,1,0:T(8,128)(2,1)} %multiply_convert_fusion.refs_0_, ...), custom_call_target="tpu_custom_call" | custom-call | tf_op jit(solution)/shard_map/pallas_call | solution.py:1645
  356.5 2.1 multiply_reduce_fusion.4
  358.9 2.3 fusion.12
  361.2 3.3 fusion.13
  364.5 160.2 %shard_map.148 = (f32[2,128,2304]{2,1,0:T(8,128)}, bf16[8,256,1152]{2,1,0:T(8,128)(2,1)}, bf16[8,256,1152]{2,1,0:T(8,128)(2,1)}, bf16[1152,768]{1,0:T(8,128)(2,1...) custom-call(bf16[2,128,2304]{2,1,0:T(8,128)(2,1)} %get-tuple-element, ...), custom_call_target="tpu_custom_call" | custom-call | tf_op jit(solution)/shard_map/pallas_call | solution.py:1645
  524.8 3.1 multiply_reduce_fusion
  528.2 0.8 copy-done.18
  528.9 3.1 multiply_reduce_fusion.1
  532.6 0.9 copy-done.20
  533.4 50.0 %shard_map.149 = (bf16[8,128,2304]{2,1,0:T(8,128)(2,1)S(1)}, bf16[1152,4608]{1,0:T(8,128)(2,1)}) custom-call(bf16[2,128,2304]{2,1,0:T(8,128)(2,1)S(1)} %fusion.14.blocks, bf16[8,256,1152]{2,1,0:T(8,128)(2,1)} %get-tuple-element.43.low_gate, bf16[8,256,1152]{2,1,0:T(8,128)(2,1)} %get-tuple-element.44.low_up, ...), custom_call_target="tpu_custom_call" | custom-call | tf_op jit(solution)/shard_map/pallas_call | solution.py:492
  583.5 2.2 copy-done.8
  585.7 5.8 fusion.21.grads
  591.6 7.6 %shard_map.150.grads = bf16[1024,1024]{1,0:T(8,128)(2,1)S(1)} custom-call(bf16[1024,512]{1,0:T(8,128)(2,1)S(1)} %bitcast.109, bf16[1024,256]{1,0:T(8,128)(2,1)S(1)} %copy-done.7, bf16[1024,256]{1,0:T(8,128)(2,1)S(1)} %copy.39.values, s32[1024,1]{1,0:T(8,128)S(1)} %copy-done.5, s32[1,1024]{1,0:T(1,128)S(1)} %get-tuple-element.72.segment_row, ...), custom_call_target="tpu_custom_call" | custom-call | tf_op jit(solution)/shard_map/pallas_call | solution.py:944
  599.6 10.6 %fusion.4 = (f32[2304]{0:T(1024)S(1)}, bf16[1024,2304]{1,0:T(8,128)(2,1)}) fusion(bf16[8,128,2304]{2,1,0:T(8,128)(2,1)} %get-tuple-element.31, f32[1024]{0:T(1024)S(1)} %rsqrt_bitcast_fusion, bf16[1024,1024]{1,0:T(8,128)(2,1)S(1)} %shard_map.150.grads, bf16[2304,1536]{1,0:T(8,128)(2,1)} %bitcast.120), kind=kOutput, calls=%fused_computation.7 | convolution fusion | flops 4843632640 | bytes 16266240 | tf_op jit(solution)/shard_map/dot_general | solution.py:99
  610.4 1.3 pad.9.gains
  611.7 14.8 %shard_map.151.blocks = bf16[4,2,4,80,1536]{4,3,2,1,0:T(8,128)(2,1)} custom-call(bf16[1024,2304]{1,0:T(8,128)(2,1)} %copy-done.24, bf16[1024,1024]{1,0:T(8,128)(2,1)} %copy-done.3, bf16[1024,2304]{1,0:T(8,128)(2,1)} %bitcast.114, bf16[1024,512]{1,0:T(8,128)(2,1)} %copy-done.13, f32[32,8,1536]{2,1,0:T(8,128)} %pad.9.gains), custom_call_target="tpu_custom_call" | custom-call | tf_op jit(solution)/shard_map/pallas_call | solution.py:981
  626.5 3.5 copy-done
  630.1 95.0 %shard_map.152 = (bf16[3,2,128,2304]{3,2,1,0:T(8,128)(2,1)S(1)}, bf16[4,80,1536]{2,1,0:T(8,128)(2,1)S(1)}) custom-call(bf16[8,128,2304]{2,1,0:T(8,128)(2,1)S(1)} %bitcast.112, bf16[4,2,4,80,1536]{4,3,2,1,0:T(8,128)(2,1)S(1)} %copy-done), custom_call_target="tpu_custom_call" | custom-call | tf_op jit(solution)/shard_map/pallas_call | solution.py:817
  725.1 0.6 convert_reduce_fusion.4
  725.7 1.0 constant_dynamic-slice_fusion.1
  726.7 1.1 constant_dynamic-slice_fusion
  728.3 0.7 copy-done.23
  729.0 0.6 fusion.16
  730.1 0.9 pad_maximum_fusion.3
  731.0 1.0 copy-done.29
  732.5 0.8 convert_reduce_fusion.3
  733.3 0.8 copy-done.21
  734.2 2.1 fusion.15
  736.2 1.1 convert_element_type.140
  737.3 1.7 pad_maximum_fusion
  739.0 4.8 convert_element_type.137
  (138 shorter events, 5.7 us)
Async XLA Ops:
  7.2 1.1 copy-start.32
  7.2 1.1 copy-start.33
  7.2 1.2 copy-start.35
  7.2 216.0 %all-gather.2.cloned.1.call-start = ((), (), s32[]{:S(2)}) async-start(), calls=%async_computation.2 | async-start | bytes 13271040 | tf_op jit(solution)/shard_map/all_gather | solution.py:1910
  7.9 728.3 %reduce-scatter.5.cloned.1.call-start = ((), (), s32[]{:S(2)}) async-start(), calls=%async_computation.4 | async-start | bytes 2211840 | tf_op jit(solution)/shard_map/reduce_scatter | solution.py:1995
  8.5 98.3 %copy-start.27 = (bf16[288,2304]{1,0:T(8,128)(2,1)S(1)}, bf16[288,2304]{1,0:T(8,128)(2,1)}, u32[]{:S(2)}) copy-start(bf16[288,2304]{1,0:T(8,128)(2,1)} %refs_2_.1) | copy-start | bytes 3981316
  107.8 53.0 %collective-permute-start = (bf16[192,2304]{1,0:T(8,128)(2,1)}, bf16[192,2304]{1,0:T(8,128)(2,1)}, u32[]{:S(2)}, u32[]{:S(2)}) collective-permute-start(bf16[192,2304]{1,0:T(8,128)(2,1)} %slice.190), channel_id=1, source_target_pairs={{0,2},{2,0},{4,6},{6,4},{1,3},{3,1},{5,7},{7,5},{8,10},{10,8},{12,... | collective-permute-start | bytes 2654216 | tf_op jit(solution)/shard_map/ppermute | solution.py:1014
  109.0 51.8 %collective-permute-start.1 = (bf16[192,2304]{1,0:T(8,128)(2,1)}, bf16[192,2304]{1,0:T(8,128)(2,1)}, u32[]{:S(2)}, u32[]{:S(2)}) collective-permute-start(bf16[192,2304]{1,0:T(8,128)(2,1)} %slice.190), channel_id=1, source_target_pairs={{0,4},{2,6},{4,0},{6,2},{1,5},{3,7},{5,1},{7,3},{8,12},{10,14},{12... | collective-permute-start | bytes 2654216 | tf_op jit(solution)/shard_map/ppermute | solution.py:1014
  117.2 7.2 slice-start.2
  117.4 7.0 slice-start.3
  124.4 2.2 slice-start.4
  125.4 2.3 slice-start.5
  126.6 6.2 copy-start.24
  132.9 2.0 copy-start.28
  136.0 1.7 copy-start.36
  136.0 1.7 copy-start.37
  140.5 1.2 copy-start.11
  141.7 0.8 copy-start.9
  142.5 1.4 slice-start.6
  143.9 6.8 copy-start.1
  146.7 7.8 %copy-start.4 = (s32[1024,1]{1,0:T(8,128)}, s32[1024,1]{1,0:T(8,128)S(1)}, u32[]{:S(2)}) copy-start(s32[1024,1]{1,0:T(8,128)S(1)} %copy.34.segment_col) | copy-start | bytes 12292
  150.7 10.1 %copy-start.6 = (bf16[1024,256]{1,0:T(8,128)(2,1)}, bf16[1024,256]{1,0:T(8,128)(2,1)S(1)}, u32[]{:S(2)}) copy-start(bf16[1024,256]{1,0:T(8,128)(2,1)S(1)} %pad_maximum_fusion.4.keys) | copy-start | bytes 1572868
  154.4 6.3 copy-start.13
  217.4 2.8 copy-start.14
  217.4 2.1 copy-start.22
  219.6 1.2 copy-start.31
  220.2 1.7 copy-start.16
  356.5 2.4 copy-start.19
  358.6 2.6 copy-start.17
  358.6 2.6 copy-start.25
  524.7 3.2 copy-start.26
  524.7 214.2 %reduce-scatter.3.cloned.1.call-start = ((), (), s32[]{:S(2)}) async-start(), calls=%async_computation.3 | async-start | bytes 13271040 | tf_op jit(solution)/shard_map/reduce_scatter | solution.py:2009
  524.8 3.4 copy-start.15
  524.8 4.1 copy-start.18
  532.0 1.4 copy-start.20
  583.5 2.2 copy-start.8
  585.7 5.9 copy-start.2
  585.7 5.9 copy-start.5
  585.7 5.9 copy-start.7
  585.7 5.9 copy-start.10
  585.7 5.9 copy-start.12
  599.2 11.0 %copy-start.3 = (bf16[1024,1024]{1,0:T(8,128)(2,1)}, bf16[1024,1024]{1,0:T(8,128)(2,1)S(1)}, u32[]{:S(2)}) copy-start(bf16[1024,1024]{1,0:T(8,128)(2,1)S(1)} %shard_map.150.grads) | copy-start | bytes 6291460
  610.4 16.1 %slice-start = ((s8[4718592]{0:T(1024)(128)(4,1)}), s8[4194304]{0:T(1024)(128)(4,1)S(1)}, s32[]{:S(2)}) async-start(s8[4718592]{0:T(1024)(128)(4,1)} %bitcast.110), calls=%async_computation.5 | async-start | bytes 8388608
  611.7 14.8 %slice-start.1 = ((s8[4718592]{0:T(1024)(128)(4,1)}), s8[524288]{0:T(1024)(128)(4,1)S(1)}, s32[]{:S(2)}) async-start(s8[4718592]{0:T(1024)(128)(4,1)} %bitcast.110), calls=%async_computation.6 | async-start | bytes 1048576
  626.5 3.5 copy-start
  727.8 1.3 copy-start.23
  729.8 2.1 copy-start.29
  729.8 2.6 copy-start.30
  730.1 3.3 copy-start.34
  732.5 1.7 copy-start.21
Sparse Core Ops, SparseCore 0:
  9.9 162.0 all-gather.1
  524.9 44.2 reduce-scatter.4
  585.8 141.2 reduce-scatter.2

commit v9 on v8

--- a/solution.py
+++ b/solution.py
@@ -999,7 +999,8 @@
 
 
 LATE = 3
-LATE_COLUMNS = 2
+PAIRS = 2
+LATE_COLUMNS = 1
 
 
 def chip_places(rows, late_rows):
@@ -1424,6 +1425,21 @@
                 for step in (2, 1, 3):
                     late_grad(c, step).start()
 
+    def arrive(t):
+        d, h = source(t)
+        piece = held.at[d, h, 0]
+        token_left(d, h, piece).wait_recv()
+
+        @pl.when((d < s) & (s < n - 1))
+        def _():
+            token_right(d, h, piece).start()
+
+        @pl.when((d > s) & (s > 0))
+        def _():
+            token_left(d, h, piece).start()
+
+        token_twin(d, h, piece).start()
+
     def unit(t, carry):
         d, h = source(t)
         slot = lax.rem(t, 2)
@@ -1436,20 +1452,19 @@
         def _():
             own_load(h).wait()
 
+        inner = jnp.logical_not(at_end)
+        pair = inner & (t >= 2) & (t < 2 + 2 * PAIRS)
+
+        @pl.when((t >= 2) & (jnp.logical_not(pair) | (lax.rem(t, 2) == 0)))
+        def _():
+            arrive(t)
+
+        @pl.when(pair & (lax.rem(t, 2) == 0))
+        def _():
+            arrive(t + 1)
+
         @pl.when(t >= 2)
         def _():
-            piece = held.at[d, h, 0]
-            token_left(d, h, piece).wait_recv()
-
-            @pl.when((d < s) & (s < n - 1))
-            def _():
-                token_right(d, h, piece).start()
-
-            @pl.when((d > s) & (s > 0))
-            def _():
-                token_left(d, h, piece).start()
-
-            token_twin(d, h, piece).start()
             for i in range(len(stage_outs)):
                 stage_store(i, d, h, slot).wait()
 

time: 759 us -> 748 us (0.986)
  Pallas kernels: 616 us -> 607 us
    pallas_call x2, Pallas kernels: 294 us -> 263 us  [run_units(): pl.pallas_call(partial(units_kernel, n_seq, backward), out_shape=outs, in...]
    pallas_call x1, Pallas kernels: 50 us -> 68.2 us  [spread_plane(): pl.pallas_call(partial(spread_kernel, n_plane), out_shape=[jax.ShapeDtype...]
    unnamed x104 -> x102, local copies, waits for them, and re-layouts: 22.1 us -> 21.7 us
  transfers between devices with their start and end apart: 5 -> 5, of which waited for: 0 -> 0; matrix products, arithmetic and copies ran while one was open for 12% -> 11% of each run, Pallas kernels for 43% -> 47%
where the time goes in v9:
time: 748 us; the launch traced here: 740 us
  Pallas kernels  607 us (81%)
  other arithmetic  45 us (6%)
  local copies, waits for them, and re-layouts  41.8 us (6%)
  matrix products  27.8 us (4%)
  between operations  14.9 us (2%)
    pallas_call x2, Pallas kernels, run_units(): pl.pallas_call(partial(units_kernel, n_seq, backward), out_shape=outs, in...  263 us
    pallas_call x1, Pallas kernels, sum_last(): pl.pallas_call(partial(last_kernel, n_seq, n_plane), out_shape=[merged_sh...  98.7 us
    pallas_call x1, Pallas kernels, gather_first(): pl.pallas_call(partial(gather_kernel, n_seq, n_plane), out_shape=[jax.Sha...  97.2 us
    pallas_call x1, Pallas kernels, spread_plane(): pl.pallas_call(partial(spread_kernel, n_plane), out_shape=[jax.ShapeDtype...  68.2 us
    pallas_call x1, Pallas kernels, merge_plane(): pl.pallas_call(partial(merge_kernel, 2 * KV_HEADS), out_shape=[merged_sha...  54.1 us
    unnamed x102, local copies, waits for them, and re-layouts  21.7 us
    dot_general x2, matrix products, times_rows(): lax.dot_general(left, weight_piece, (((1,), (1,)), ((), ())), preferred_e...  16.9 us
  transfers between devices with their start and end apart: 5, of which 0 were waited for; matrix products, arithmetic and copies ran while one was open for 11% of the time, Pallas kernels for 47%

profile of v9, /device:TPU:0, one launch (start us, length us, event | category | flops | bytes accessed | tf_op | source)
XLA Modules:
  0.0 739.8 jit_solution(761777060219539513)
XLA Ops:
  7.2 0.7 all-gather.2.cloned.1.call-update
  8.5 1.1 pad_maximum_fusion.2.blocks
  9.5 97.2 %shard_map.144 = (bf16[8,128,2304]{2,1,0:T(8,128)(2,1)}, bf16[4,2,4,80,1536]{4,3,2,1,0:T(8,128)(2,1)}) custom-call(bf16[2,128,2304]{2,1,0:T(8,128)(2,1)} %hidden.1, bf16[4,80,1536]{2,1,0:T(8,128)(2,1)} %pad_maximum_fusion.2.blocks), custom_call_target="tpu_custom_call" | custom-call | tf_op jit(solution)/shard_map/pallas_call | solution.py:640
  106.8 1.0 slice.190
  107.8 1.2 collective-permute-start
  109.0 0.8 collective-permute-start.1
  109.8 6.5 slice.216
  116.3 0.8 convert_bitcast_fusion
  117.4 6.9 copy.29
  124.4 1.0 fusion
  125.4 1.1 fusion.2.inputs
  126.6 1.1 slice-done.5
  127.7 5.1 fusion.7
  133.0 1.9 copy-done.28
  134.8 0.9 slice.224
  136.0 0.9 copy.37
  136.9 0.6 copy.36
  137.5 0.8 select_reduce_fusion
  138.3 1.9 multiply_cosine_fusion.1
  140.2 1.2 subtract_convert_fusion
  141.4 0.8 copy-done.9
  142.3 1.1 pad_maximum_fusion.1
  143.7 1.3 copy.38
  145.0 1.2 copy.39.values
  146.4 3.9 fusion.34
  150.5 3.7 shard_map.145.outs
  154.2 6.3 convolution_convert_fusion
  160.6 54.1 %shard_map.146 = (bf16[3,2,128,2304]{3,2,1,0:T(8,128)(2,1)}, bf16[2,96,2304]{2,1,0:T(8,128)(2,1)}) custom-call(bf16[8,128,2304]{2,1,0:T(8,128)(2,1)} %bitcast.126, bf16[192,2304]{1,0:T(8,128)(2,1)} %collective-permute-done.rows_x.refs_3_, bf16[192,2304]{1,0:T(8,128)(2,1)} %collective-permute-done.1.rows_y.refs_4_), custom_call_target="tpu_custom_call" | custom-call | tf_op jit(solution)/shard_map/pallas_call | solution.py:404
  214.7 2.8 convert_reduce_fusion.1
  217.7 1.9 copy-done.22
  219.6 0.6 multiply_reduce_fusion.5
  220.2 0.5 copy-done.30
  220.7 1.1 slice_bitcast_fusion
  221.9 1.3 multiply_convert_fusion.refs_0_
  223.2 127.1 %shard_map.147 = (f32[2,128,2304]{2,1,0:T(8,128)}, bf16[4,2,2,128,2304]{4,3,2,1,0:T(8,128)(2,1)}, bf16[4,96,2304]{2,1,0:T(8,128)(2,1)}, bf16[8,256,1152]{2,1,0:T...) custom-call(bf16[2,128,2304]{2,1,0:T(8,128)(2,1)} %multiply_convert_fusion.refs_0_, ...), custom_call_target="tpu_custom_call" | custom-call | tf_op jit(solution)/shard_map/pallas_call | solution.py:1660
  350.2 2.1 multiply_reduce_fusion.4
  352.6 2.3 fusion.12
  354.9 3.3 fusion.13
  358.2 136.0 %shard_map.148 = (f32[2,128,2304]{2,1,0:T(8,128)}, bf16[8,256,1152]{2,1,0:T(8,128)(2,1)}, bf16[8,256,1152]{2,1,0:T(8,128)(2,1)}, bf16[1152,1536]{1,0:T(8,128)(2,...) custom-call(bf16[2,128,2304]{2,1,0:T(8,128)(2,1)} %get-tuple-element.72.refs_0_, ...), custom_call_target="tpu_custom_call" | custom-call | tf_op jit(solution)/shard_map/pallas_call | solution.py:1660
  494.4 1.6 copy-done.18
  496.0 2.4 multiply_reduce_fusion
  498.7 3.1 multiply_reduce_fusion.1
  501.8 0.5 fusion.14.blocks
  502.3 0.9 copy-done.20
  503.1 68.2 %shard_map.149 = (bf16[8,128,2304]{2,1,0:T(8,128)(2,1)S(1)}, bf16[1152,4608]{1,0:T(8,128)(2,1)}) custom-call(bf16[2,128,2304]{2,1,0:T(8,128)(2,1)S(1)} %fusion.14.blocks, bf16[8,256,1152]{2,1,0:T(8,128)(2,1)} %get-tuple-element.41.low_gate, bf16[8,256,1152]{2,1,0:T(8,128)(2,1)} %get-tuple-element.42.low_up, ...), custom_call_target="tpu_custom_call" | custom-call | tf_op jit(solution)/shard_map/pallas_call | solution.py:492
  571.4 2.2 copy-done.8
  573.6 5.8 fusion.21.grads
  579.5 7.6 %shard_map.150.grads = bf16[1024,1024]{1,0:T(8,128)(2,1)S(1)} custom-call(bf16[1024,512]{1,0:T(8,128)(2,1)S(1)} %bitcast.109, bf16[1024,256]{1,0:T(8,128)(2,1)S(1)} %copy-done.7, bf16[1024,256]{1,0:T(8,128)(2,1)S(1)} %copy.39.values, s32[1024,1]{1,0:T(8,128)S(1)} %copy-done.5, s32[1,1024]{1,0:T(1,128)S(1)} %get-tuple-element.66.segment_row, ...), custom_call_target="tpu_custom_call" | custom-call | tf_op jit(solution)/shard_map/pallas_call | solution.py:944
  587.4 10.6 %fusion.4 = (f32[2304]{0:T(1024)S(1)}, bf16[1024,2304]{1,0:T(8,128)(2,1)}) fusion(bf16[8,128,2304]{2,1,0:T(8,128)(2,1)} %get-tuple-element.29, f32[1024]{0:T(1024)S(1)} %rsqrt_bitcast_fusion, bf16[1024,1024]{1,0:T(8,128)(2,1)S(1)} %shard_map.150.grads, bf16[2304,1536]{1,0:T(8,128)(2,1)} %bitcast.120), kind=kOutput, calls=%fused_computation.7 | convolution fusion | flops 4843632640 | bytes 16266240 | tf_op jit(solution)/shard_map/dot_general | solution.py:99
  598.2 1.3 pad.9.gains
  599.6 14.7 %shard_map.151.blocks = bf16[4,2,4,80,1536]{4,3,2,1,0:T(8,128)(2,1)} custom-call(bf16[1024,2304]{1,0:T(8,128)(2,1)} %copy-done.24, bf16[1024,1024]{1,0:T(8,128)(2,1)} %copy-done.3, bf16[1024,2304]{1,0:T(8,128)(2,1)} %bitcast.114, bf16[1024,512]{1,0:T(8,128)(2,1)} %copy-done.13, f32[32,8,1536]{2,1,0:T(8,128)} %pad.9.gains), custom_call_target="tpu_custom_call" | custom-call | tf_op jit(solution)/shard_map/pallas_call | solution.py:981
  614.3 3.6 copy-done
  617.8 98.7 %shard_map.152 = (bf16[3,2,128,2304]{3,2,1,0:T(8,128)(2,1)S(1)}, bf16[4,80,1536]{2,1,0:T(8,128)(2,1)S(1)}) custom-call(bf16[8,128,2304]{2,1,0:T(8,128)(2,1)S(1)} %bitcast.112, bf16[4,2,4,80,1536]{4,3,2,1,0:T(8,128)(2,1)S(1)} %copy-done), custom_call_target="tpu_custom_call" | custom-call | tf_op jit(solution)/shard_map/pallas_call | solution.py:817
  716.6 0.6 convert_reduce_fusion.3
  717.2 1.1 constant_dynamic-slice_fusion
  718.2 0.5 convert_reduce_fusion
  718.8 0.7 copy-done.23
  719.5 0.6 fusion.16
  720.6 0.9 pad_maximum_fusion.3
  721.4 1.0 copy-done.29
  723.1 2.1 fusion.15
  725.2 1.4 convert_element_type.136
  726.6 1.7 pad_maximum_fusion
  728.3 4.8 convert_element_type.134
  (135 shorter events, 4.4 us)
Async XLA Ops:
  7.2 1.1 copy-start.31
  7.2 1.1 copy-start.32
  7.2 1.2 copy-start.34
  7.2 216.0 %all-gather.2.cloned.1.call-start = ((), (), s32[]{:S(2)}) async-start(), calls=%async_computation.2 | async-start | bytes 13271040 | tf_op jit(solution)/shard_map/all_gather | solution.py:1925
  7.9 717.3 %reduce-scatter.5.cloned.1.call-start = ((), (), s32[]{:S(2)}) async-start(), calls=%async_computation.4 | async-start | bytes 4423680 | tf_op jit(solution)/shard_map/reduce_scatter | solution.py:2010
  8.5 98.3 %copy-start.27 = (bf16[288,2304]{1,0:T(8,128)(2,1)S(1)}, bf16[288,2304]{1,0:T(8,128)(2,1)}, u32[]{:S(2)}) copy-start(bf16[288,2304]{1,0:T(8,128)(2,1)} %refs_2_.1) | copy-start | bytes 3981316
  107.8 52.8 %collective-permute-start = (bf16[192,2304]{1,0:T(8,128)(2,1)}, bf16[192,2304]{1,0:T(8,128)(2,1)}, u32[]{:S(2)}, u32[]{:S(2)}) collective-permute-start(bf16[192,2304]{1,0:T(8,128)(2,1)} %slice.190), channel_id=1, source_target_pairs={{0,2},{2,0},{4,6},{6,4},{1,3},{3,1},{5,7},{7,5},{8,10},{10,8},{12,... | collective-permute-start | bytes 2654216 | tf_op jit(solution)/shard_map/ppermute | solution.py:1015
  109.0 51.6 %collective-permute-start.1 = (bf16[192,2304]{1,0:T(8,128)(2,1)}, bf16[192,2304]{1,0:T(8,128)(2,1)}, u32[]{:S(2)}, u32[]{:S(2)}) collective-permute-start(bf16[192,2304]{1,0:T(8,128)(2,1)} %slice.190), channel_id=1, source_target_pairs={{0,4},{2,6},{4,0},{6,2},{1,5},{3,7},{5,1},{7,3},{8,12},{10,14},{12... | collective-permute-start | bytes 2654216 | tf_op jit(solution)/shard_map/ppermute | solution.py:1015
  117.2 7.2 slice-start.2
  117.4 7.0 slice-start.3
  124.4 2.2 slice-start.4
  125.4 2.3 slice-start.5
  126.6 6.2 copy-start.24
  132.8 2.0 copy-start.28
  136.0 1.5 copy-start.35
  136.0 1.5 copy-start.36
  140.2 1.2 copy-start.11
  141.4 0.8 copy-start.9
  142.3 1.4 slice-start.6
  143.6 6.8 copy-start.1
  146.4 7.8 %copy-start.4 = (s32[1024,1]{1,0:T(8,128)}, s32[1024,1]{1,0:T(8,128)S(1)}, u32[]{:S(2)}) copy-start(s32[1024,1]{1,0:T(8,128)S(1)} %copy.34.segment_col) | copy-start | bytes 12292
  150.5 10.1 %copy-start.6 = (bf16[1024,256]{1,0:T(8,128)(2,1)}, bf16[1024,256]{1,0:T(8,128)(2,1)S(1)}, u32[]{:S(2)}) copy-start(bf16[1024,256]{1,0:T(8,128)(2,1)S(1)} %pad_maximum_fusion.4.keys) | copy-start | bytes 1572868
  154.2 6.3 copy-start.13
  217.4 2.8 copy-start.14
  217.4 2.1 copy-start.22
  219.6 1.2 copy-start.30
  220.2 1.7 copy-start.16
  350.2 2.4 copy-start.19
  352.3 2.6 copy-start.17
  352.3 2.6 copy-start.25
  494.3 1.7 copy-start.18
  494.3 233.9 %reduce-scatter.3.cloned.1.call-start = ((), (), s32[]{:S(2)}) async-start(), calls=%async_computation.3 | async-start | bytes 13271040 | tf_op jit(solution)/shard_map/reduce_scatter | solution.py:2024
  496.0 2.4 copy-start.15
  496.0 2.7 copy-start.26
  501.7 1.4 copy-start.20
  571.3 2.2 copy-start.8
  573.6 5.9 copy-start.2
  573.6 5.9 copy-start.5
  573.6 5.9 copy-start.7
  573.6 5.9 copy-start.10
  573.6 5.9 copy-start.12
  587.1 10.9 %copy-start.3 = (bf16[1024,1024]{1,0:T(8,128)(2,1)}, bf16[1024,1024]{1,0:T(8,128)(2,1)S(1)}, u32[]{:S(2)}) copy-start(bf16[1024,1024]{1,0:T(8,128)(2,1)S(1)} %shard_map.150.grads) | copy-start | bytes 6291460
  598.2 16.0 %slice-start = ((s8[4718592]{0:T(1024)(128)(4,1)}), s8[4194304]{0:T(1024)(128)(4,1)S(1)}, s32[]{:S(2)}) async-start(s8[4718592]{0:T(1024)(128)(4,1)} %bitcast.110), calls=%async_computation.5 | async-start | bytes 8388608
  599.6 14.7 %slice-start.1 = ((s8[4718592]{0:T(1024)(128)(4,1)}), s8[524288]{0:T(1024)(128)(4,1)S(1)}, s32[]{:S(2)}) async-start(s8[4718592]{0:T(1024)(128)(4,1)} %bitcast.110), calls=%async_computation.6 | async-start | bytes 1048576
  614.3 3.6 copy-start
  718.2 1.3 copy-start.23
  720.3 2.1 copy-start.29
  720.5 2.4 copy-start.33
  720.6 2.6 copy-start.21
Sparse Core Ops, SparseCore 0:
  9.9 162.2 all-gather.1
  494.5 75.0 reduce-scatter.4
  573.7 143.9 reduce-scatter.2

commit v10 on v9

--- a/solution.py
+++ b/solution.py
@@ -121,6 +121,10 @@
         device_id=device,
         device_id_type=MESH,
     )
+
+
+def line_neighbours(s, n_seq):
+    return {"seq": jnp.maximum(s - 1, 0)}, {"seq": jnp.minimum(s + 1, n_seq - 1)}
 
 
 def plane_device(index):
@@ -537,6 +541,7 @@
     s = lax.axis_index("seq")
     q = lax.axis_index("chip")
     k = lax.axis_index("core")
+    before, after = line_neighbours(s, n_seq)
     greet(n_plane, n_seq)
     swaps = []
     for step in range(1, n_chip):
@@ -560,12 +565,12 @@
 
     def to_left(d):
         return remote(
-            blocks_all.at[d, k], blocks_all.at[d, k], left_send.at[d], line_recv.at[d], {"seq": s - 1}
+            blocks_all.at[d, k], blocks_all.at[d, k], left_send.at[d], line_recv.at[d], before
         )
 
     def to_right(d):
         return remote(
-            blocks_all.at[d, k], blocks_all.at[d, k], right_send.at[d], line_recv.at[d], {"seq": s + 1}
+            blocks_all.at[d, k], blocks_all.at[d, k], right_send.at[d], line_recv.at[d], after
         )
 
     def to_twin(d):
@@ -691,6 +696,7 @@
     s = lax.axis_index("seq")
     q = lax.axis_index("chip")
     k = lax.axis_index("core")
+    before, after = line_neighbours(s, n_seq)
     greet(n_plane, n_seq)
 
     def load(d):
@@ -702,11 +708,11 @@
         )
 
     def to_left(d):
-        return remote(held.at[d], line.at[d], line_send.at[d], line_recv.at[d], {"seq": s - 1})
+        return remote(held.at[d], line.at[d], line_send.at[d], line_recv.at[d], before)
 
     def to_right(d):
         return remote(
-            held.at[d], line.at[d + 1], line_send.at[d], line_recv.at[d + 1], {"seq": s + 1}
+            held.at[d], line.at[d + 1], line_send.at[d], line_recv.at[d + 1], after
         )
 
     def gather_terms(d, with_left, with_right):
@@ -1107,6 +1113,7 @@
     n = n_seq
     s = lax.axis_index("seq")
     k = lax.axis_index("core")
+    before, after = line_neighbours(s, n)
     twin = {"core": 1 - k}
     n_units, width = downs_v.shape
     piece_len = tokens.shape[1]
@@ -1114,12 +1121,12 @@
 
     def token_left(d, h, source):
         return remote(
-            source, held.at[d, h, 0], left_send.at[d, h], token_recv.at[d, h], {"seq": s - 1}
+            source, held.at[d, h, 0], left_send.at[d, h], token_recv.at[d, h], before
         )
 
     def token_right(d, h, source):
         return remote(
-            source, held.at[d, h, 0], right_send.at[d, h], token_recv.at[d, h], {"seq": s + 1}
+            source, held.at[d, h, 0], right_send.at[d, h], token_recv.at[d, h], after
         )
 
     def token_twin(d, h, source):

time: 748 us -> 748 us (level)
  no operation moved by 1% of the time
where the time goes in v10:
time: 748 us; the launch traced here: 740 us
  Pallas kernels  607 us (81%)
  other arithmetic  45 us (6%)
  local copies, waits for them, and re-layouts  41.8 us (6%)
  matrix products  27.8 us (4%)
  between operations  14.9 us (2%)
    pallas_call x2, Pallas kernels, run_units(): pl.pallas_call(partial(units_kernel, n_seq, backward), out_shape=outs, in...  263 us
    pallas_call x1, Pallas kernels, sum_last(): pl.pallas_call(partial(last_kernel, n_seq, n_plane), out_shape=[merged_sh...  98.7 us
    pallas_call x1, Pallas kernels, gather_first(): pl.pallas_call(partial(gather_kernel, n_seq, n_plane), out_shape=[jax.Sha...  97.2 us
    pallas_call x1, Pallas kernels, spread_plane(): pl.pallas_call(partial(spread_kernel, n_plane), out_shape=[jax.ShapeDtype...  68.5 us
    pallas_call x1, Pallas kernels, merge_plane(): pl.pallas_call(partial(merge_kernel, 2 * KV_HEADS), out_shape=[merged_sha...  54.1 us
    unnamed x102, local copies, waits for them, and re-layouts  21.7 us
    dot_general x2, matrix products, times_rows(): lax.dot_general(left, weight_piece, (((1,), (1,)), ((), ())), preferred_e...  16.9 us
  transfers between devices with their start and end apart: 5, of which 0 were waited for; matrix products, arithmetic and copies ran while one was open for 11% of the time, Pallas kernels for 47%

profile of v10, /device:TPU:0, one launch (start us, length us, event | category | flops | bytes accessed | tf_op | source)
XLA Modules:
  0.0 739.8 jit_solution(12265669761289890642)
XLA Ops:
  7.2 0.7 all-gather.2.cloned.1.call-update
  8.5 1.1 pad_maximum_fusion.2.blocks
  9.5 97.2 %shard_map.144 = (bf16[8,128,2304]{2,1,0:T(8,128)(2,1)}, bf16[4,2,4,80,1536]{4,3,2,1,0:T(8,128)(2,1)}) custom-call(bf16[2,128,2304]{2,1,0:T(8,128)(2,1)} %hidden.1, bf16[4,80,1536]{2,1,0:T(8,128)(2,1)} %pad_maximum_fusion.2.blocks), custom_call_target="tpu_custom_call" | custom-call | tf_op jit(solution)/shard_map/pallas_call | solution.py:645
  106.8 1.0 slice.190
  107.8 1.2 collective-permute-start
  109.0 0.8 collective-permute-start.1
  109.8 6.5 slice.216
  116.3 0.8 convert_bitcast_fusion
  117.4 6.9 copy.29
  124.4 1.0 fusion
  125.4 1.1 fusion.2.inputs
  126.6 1.1 slice-done.5
  127.7 5.1 fusion.7
  133.0 1.9 copy-done.28
  134.8 0.9 slice.224
  136.0 0.9 copy.37
  136.9 0.6 copy.36
  137.5 0.8 select_reduce_fusion
  138.3 1.9 multiply_cosine_fusion.1
  140.2 1.2 subtract_convert_fusion
  141.4 0.8 copy-done.9
  142.3 1.1 pad_maximum_fusion.1
  143.7 1.3 copy.38
  145.0 1.2 copy.39.values
  146.4 3.9 fusion.34
  150.5 3.7 shard_map.145.outs
  154.2 6.3 convolution_convert_fusion
  160.6 54.1 %shard_map.146 = (bf16[3,2,128,2304]{3,2,1,0:T(8,128)(2,1)}, bf16[2,96,2304]{2,1,0:T(8,128)(2,1)}) custom-call(bf16[8,128,2304]{2,1,0:T(8,128)(2,1)} %bitcast.126, bf16[192,2304]{1,0:T(8,128)(2,1)} %collective-permute-done.rows_x.refs_3_, bf16[192,2304]{1,0:T(8,128)(2,1)} %collective-permute-done.1.rows_y.refs_4_), custom_call_target="tpu_custom_call" | custom-call | tf_op jit(solution)/shard_map/pallas_call | solution.py:408
  214.7 2.8 convert_reduce_fusion.1
  217.7 1.9 copy-done.22
  219.6 0.6 multiply_reduce_fusion.5
  220.2 0.5 copy-done.30
  220.7 1.1 slice_bitcast_fusion
  221.9 1.3 multiply_convert_fusion.refs_0_
  223.2 127.0 %shard_map.147 = (f32[2,128,2304]{2,1,0:T(8,128)}, bf16[4,2,2,128,2304]{4,3,2,1,0:T(8,128)(2,1)}, bf16[4,96,2304]{2,1,0:T(8,128)(2,1)}, bf16[8,256,1152]{2,1,0:T...) custom-call(bf16[2,128,2304]{2,1,0:T(8,128)(2,1)} %multiply_convert_fusion.refs_0_, ...), custom_call_target="tpu_custom_call" | custom-call | tf_op jit(solution)/shard_map/pallas_call | solution.py:1667
  350.2 2.1 multiply_reduce_fusion.4
  352.5 2.3 fusion.12
  354.9 3.3 fusion.13
  358.2 135.9 %shard_map.148 = (f32[2,128,2304]{2,1,0:T(8,128)}, bf16[8,256,1152]{2,1,0:T(8,128)(2,1)}, bf16[8,256,1152]{2,1,0:T(8,128)(2,1)}, bf16[1152,1536]{1,0:T(8,128)(2,...) custom-call(bf16[2,128,2304]{2,1,0:T(8,128)(2,1)} %get-tuple-element.72.refs_0_, ...), custom_call_target="tpu_custom_call" | custom-call | tf_op jit(solution)/shard_map/pallas_call | solution.py:1667
  494.1 1.6 copy-done.18
  495.7 2.4 multiply_reduce_fusion
  498.4 3.1 multiply_reduce_fusion.1
  501.5 0.5 fusion.14.blocks
  502.0 0.9 copy-done.20
  502.9 68.5 %shard_map.149 = (bf16[8,128,2304]{2,1,0:T(8,128)(2,1)S(1)}, bf16[1152,4608]{1,0:T(8,128)(2,1)}) custom-call(bf16[2,128,2304]{2,1,0:T(8,128)(2,1)S(1)} %fusion.14.blocks, bf16[8,256,1152]{2,1,0:T(8,128)(2,1)} %get-tuple-element.41.low_gate, bf16[8,256,1152]{2,1,0:T(8,128)(2,1)} %get-tuple-element.42.low_up, ...), custom_call_target="tpu_custom_call" | custom-call | tf_op jit(solution)/shard_map/pallas_call | solution.py:496
  571.4 2.2 copy-done.8
  573.6 5.8 fusion.21.grads
  579.5 7.6 %shard_map.150.grads = bf16[1024,1024]{1,0:T(8,128)(2,1)S(1)} custom-call(bf16[1024,512]{1,0:T(8,128)(2,1)S(1)} %bitcast.109, bf16[1024,256]{1,0:T(8,128)(2,1)S(1)} %copy-done.7, bf16[1024,256]{1,0:T(8,128)(2,1)S(1)} %copy.39.values, s32[1024,1]{1,0:T(8,128)S(1)} %copy-done.5, s32[1,1024]{1,0:T(1,128)S(1)} %get-tuple-element.66.segment_row, ...), custom_call_target="tpu_custom_call" | custom-call | tf_op jit(solution)/shard_map/pallas_call | solution.py:950
  587.5 10.6 %fusion.4 = (f32[2304]{0:T(1024)S(1)}, bf16[1024,2304]{1,0:T(8,128)(2,1)}) fusion(bf16[8,128,2304]{2,1,0:T(8,128)(2,1)} %get-tuple-element.29, f32[1024]{0:T(1024)S(1)} %rsqrt_bitcast_fusion, bf16[1024,1024]{1,0:T(8,128)(2,1)S(1)} %shard_map.150.grads, bf16[2304,1536]{1,0:T(8,128)(2,1)} %bitcast.120), kind=kOutput, calls=%fused_computation.7 | convolution fusion | flops 4843632640 | bytes 16266240 | tf_op jit(solution)/shard_map/dot_general | solution.py:99
  598.3 1.3 pad.9.gains
  599.6 14.7 %shard_map.151.blocks = bf16[4,2,4,80,1536]{4,3,2,1,0:T(8,128)(2,1)} custom-call(bf16[1024,2304]{1,0:T(8,128)(2,1)} %copy-done.24, bf16[1024,1024]{1,0:T(8,128)(2,1)} %copy-done.3, bf16[1024,2304]{1,0:T(8,128)(2,1)} %bitcast.114, bf16[1024,512]{1,0:T(8,128)(2,1)} %copy-done.13, f32[32,8,1536]{2,1,0:T(8,128)} %pad.9.gains), custom_call_target="tpu_custom_call" | custom-call | tf_op jit(solution)/shard_map/pallas_call | solution.py:987
  614.3 3.6 copy-done
  617.9 98.7 %shard_map.152 = (bf16[3,2,128,2304]{3,2,1,0:T(8,128)(2,1)S(1)}, bf16[4,80,1536]{2,1,0:T(8,128)(2,1)S(1)}) custom-call(bf16[8,128,2304]{2,1,0:T(8,128)(2,1)S(1)} %bitcast.112, bf16[4,2,4,80,1536]{4,3,2,1,0:T(8,128)(2,1)S(1)} %copy-done), custom_call_target="tpu_custom_call" | custom-call | tf_op jit(solution)/shard_map/pallas_call | solution.py:823
  716.6 0.6 convert_reduce_fusion.3
  717.2 1.1 constant_dynamic-slice_fusion
  718.3 0.5 convert_reduce_fusion
  718.8 0.7 copy-done.23
  719.5 0.6 fusion.16
  720.6 0.9 pad_maximum_fusion.3
  721.5 1.0 copy-done.29
  723.2 2.1 fusion.15
  725.2 1.4 convert_element_type.136
  726.6 1.7 pad_maximum_fusion
  728.3 4.8 convert_element_type.134
  (135 shorter events, 4.4 us)
Async XLA Ops:
  7.2 1.1 copy-start.31
  7.2 1.1 copy-start.32
  7.2 1.2 copy-start.34
  7.2 216.0 %all-gather.2.cloned.1.call-start = ((), (), s32[]{:S(2)}) async-start(), calls=%async_computation.2 | async-start | bytes 13271040 | tf_op jit(solution)/shard_map/all_gather | solution.py:1932
  7.9 717.3 %reduce-scatter.5.cloned.1.call-start = ((), (), s32[]{:S(2)}) async-start(), calls=%async_computation.4 | async-start | bytes 4423680 | tf_op jit(solution)/shard_map/reduce_scatter | solution.py:2017
  8.5 98.3 %copy-start.27 = (bf16[288,2304]{1,0:T(8,128)(2,1)S(1)}, bf16[288,2304]{1,0:T(8,128)(2,1)}, u32[]{:S(2)}) copy-start(bf16[288,2304]{1,0:T(8,128)(2,1)} %refs_2_.1) | copy-start | bytes 3981316
  107.8 52.8 %collective-permute-start = (bf16[192,2304]{1,0:T(8,128)(2,1)}, bf16[192,2304]{1,0:T(8,128)(2,1)}, u32[]{:S(2)}, u32[]{:S(2)}) collective-permute-start(bf16[192,2304]{1,0:T(8,128)(2,1)} %slice.190), channel_id=1, source_target_pairs={{0,2},{2,0},{4,6},{6,4},{1,3},{3,1},{5,7},{7,5},{8,10},{10,8},{12,... | collective-permute-start | bytes 2654216 | tf_op jit(solution)/shard_map/ppermute | solution.py:1021
  109.0 51.6 %collective-permute-start.1 = (bf16[192,2304]{1,0:T(8,128)(2,1)}, bf16[192,2304]{1,0:T(8,128)(2,1)}, u32[]{:S(2)}, u32[]{:S(2)}) collective-permute-start(bf16[192,2304]{1,0:T(8,128)(2,1)} %slice.190), channel_id=1, source_target_pairs={{0,4},{2,6},{4,0},{6,2},{1,5},{3,7},{5,1},{7,3},{8,12},{10,14},{12... | collective-permute-start | bytes 2654216 | tf_op jit(solution)/shard_map/ppermute | solution.py:1021
  117.2 7.2 slice-start.2
  117.4 7.0 slice-start.3
  124.4 2.2 slice-start.4
  125.4 2.3 slice-start.5
  126.6 6.2 copy-start.24
  132.8 2.0 copy-start.28
  136.0 1.5 copy-start.35
  136.0 1.5 copy-start.36
  140.2 1.2 copy-start.11
  141.4 0.8 copy-start.9
  142.3 1.4 slice-start.6
  143.6 6.8 copy-start.1
  146.4 7.8 %copy-start.4 = (s32[1024,1]{1,0:T(8,128)}, s32[1024,1]{1,0:T(8,128)S(1)}, u32[]{:S(2)}) copy-start(s32[1024,1]{1,0:T(8,128)S(1)} %copy.34.segment_col) | copy-start | bytes 12292
  150.5 10.1 %copy-start.6 = (bf16[1024,256]{1,0:T(8,128)(2,1)}, bf16[1024,256]{1,0:T(8,128)(2,1)S(1)}, u32[]{:S(2)}) copy-start(bf16[1024,256]{1,0:T(8,128)(2,1)S(1)} %pad_maximum_fusion.4.keys) | copy-start | bytes 1572868
  154.2 6.3 copy-start.13
  217.4 2.8 copy-start.14
  217.4 2.1 copy-start.22
  219.6 1.2 copy-start.30
  220.2 1.7 copy-start.16
  350.2 2.4 copy-start.19
  352.2 2.6 copy-start.17
  352.2 2.6 copy-start.25
  494.1 1.7 copy-start.18
  494.1 234.2 %reduce-scatter.3.cloned.1.call-start = ((), (), s32[]{:S(2)}) async-start(), calls=%async_computation.3 | async-start | bytes 13271040 | tf_op jit(solution)/shard_map/reduce_scatter | solution.py:2031
  495.7 2.4 copy-start.15
  495.7 2.7 copy-start.26
  501.5 1.4 copy-start.20
  571.4 2.2 copy-start.8
  573.6 5.9 copy-start.2
  573.6 5.9 copy-start.5
  573.6 5.9 copy-start.7
  573.6 5.9 copy-start.10
  573.6 5.9 copy-start.12
  587.2 10.9 %copy-start.3 = (bf16[1024,1024]{1,0:T(8,128)(2,1)}, bf16[1024,1024]{1,0:T(8,128)(2,1)S(1)}, u32[]{:S(2)}) copy-start(bf16[1024,1024]{1,0:T(8,128)(2,1)S(1)} %shard_map.150.grads) | copy-start | bytes 6291460
  598.2 16.0 %slice-start = ((s8[4718592]{0:T(1024)(128)(4,1)}), s8[4194304]{0:T(1024)(128)(4,1)S(1)}, s32[]{:S(2)}) async-start(s8[4718592]{0:T(1024)(128)(4,1)} %bitcast.110), calls=%async_computation.5 | async-start | bytes 8388608
  599.6 14.7 %slice-start.1 = ((s8[4718592]{0:T(1024)(128)(4,1)}), s8[524288]{0:T(1024)(128)(4,1)S(1)}, s32[]{:S(2)}) async-start(s8[4718592]{0:T(1024)(128)(4,1)} %bitcast.110), calls=%async_computation.6 | async-start | bytes 1048576
  614.3 3.6 copy-start
  718.3 1.3 copy-start.23
  720.3 2.1 copy-start.29
  720.5 2.4 copy-start.33
  720.6 2.6 copy-start.21
Sparse Core Ops, SparseCore 0:
  9.9 162.2 all-gather.1
  494.2 75.2 reduce-scatter.4
  573.7 143.9 reduce-scatter.2
